TPU v7x, 256 devices: a whole 4x4x8 slice. The times are simulated.
256 devices in a mesh: dp: 4 (over x), fsdp: 64 (over z, y, core).
Axes of the slice: x: 4, y: 4, z: 8, core: 2. Of those that a mesh axis runs over, the one named last changes fastest.
Arguments:
- inputs: bfloat16 [512, 16384], P('dp', 'fsdp'), may hold values from -140 to 140
- norm_gain_vector: bfloat16 [16384], P('fsdp'), may hold values from 0.5 to 1.5
- weight: bfloat16 [16384, 16384], P(None, 'fsdp'), may hold values from -0.046875 to 0.046875
- down_adapters: bfloat16 [16384, 16, 32], P('fsdp'), may hold values from -0.046875 to 0.046875
- up_adapters: bfloat16 [16, 32, 16384], P(None, None, 'fsdp'), may hold values from -1 to 1
- tenant: int32 [512], P('dp'), may hold values from 0 to 15
- tenant_slot_index: int32 [16], replicated, may hold values from 0 to 31, as said below
- live_row_count: int32 [4], P('dp'), may hold values from 1 to 128, 320 in all
- cotangent: bfloat16 [512, 16384], P('dp', 'fsdp'), may hold values from -6 to 6
- down_row_factor: float32 [32, 16384], P('dp', 'fsdp'), may hold values from 300 to 30000
- down_column_factor: float32 [32, 32], P('dp'), may hold values from 300 to 30000
- up_row_factor: float32 [32, 32], P('dp'), may hold values from 0.5 to 50
- up_column_factor: float32 [32, 16384], P('dp', 'fsdp'), may hold values from 0.5 to 50
Outputs:
- projected: bfloat16 [512, 16384], P('dp', 'fsdp')
- normed_gradient_transposed: bfloat16 [16384, 512], P('fsdp', 'dp')
- update_a: float32 [32, 16384, 32], P('dp', 'fsdp')
- update_b: float32 [32, 32, 16384], P('dp', None, 'fsdp')
- row_a_new: float32 [32, 16384], P('dp', 'fsdp')
- col_a_new: float32 [32, 32], P('dp')
- row_b_new: float32 [32, 32], P('dp')
- col_b_new: float32 [32, 16384], P('dp', 'fsdp')
Inputs may be any that keep to these rules, and one draw needn't show every extreme that they name: Distinct slots; tenant t's optimizer state is in slot tenant_slot_index[t], owned by data group tenant_slot_index[t] // 8; every group owns at most 8 tenants and some group owns exactly 8. The first live_row_count[g] rows of data group g are live; some group has all 128 live; the counts sum to 320.
All inputs are finite; a program needn't handle non-finite values.
Results may differ from a plain program's by a relative error of at most 0.0095.
Values may be sent and summed in bfloat16 or wider, within the bound.
No kernel may reach another device: no remote copies, remote signals or barrier semaphores. Data moves between devices by JAX's collectives and lax.ppermute only.
A program may use at most 128 MiB of HBM per device.

v0:
```python
import functools

import jax
import jax.numpy as jnp
from jax import lax
from jax.experimental import pallas as pl
from jax.experimental.pallas import tpu as pltpu
from jax.sharding import Mesh, PartitionSpec as P

ADAPTER_SCALE = 0.5
BETA_TWO = 0.9
SQ_EPS = 1e-30
RMS_EPS = 1e-05
NX, NZ, NY, NC = 4, 8, 4, 2
F = ("z", "y", "core")
bf16, f32, i32 = jnp.bfloat16, jnp.float32, jnp.int32
NT = (((1,), (1,)), ((), ()))
NN = (((1,), (0,)), ((), ()))
TN = (((0,), (0,)), ((), ()))
ROWS, WIDTH, FULL, TENANTS, RANK, OWNED = 128, 256, 16384, 16, 32, 8
HBM = pl.BlockSpec(memory_space=pl.ANY)
VMEM = pl.BlockSpec(memory_space=pltpu.VMEM)
SMEM = pl.BlockSpec(memory_space=pltpu.SMEM)


def plane_moves(rule):
    pairs = []
    for z in range(NZ):
        for y in range(NY):
            for c in range(NC):
                to = rule(z, y, c)
                if to is not None:
                    z2, y2, c2 = to
                    pairs.append(
                        ((z * NY + y) * NC + c, ((z2 % NZ) * NY + y2 % NY) * NC + c2)
                    )
    return pairs


Z_BY_CORE = plane_moves(lambda z, y, c: (z + 1 - 2 * c, y, c))
Y_BY_CORE = plane_moves(lambda z, y, c: (z, y + 1 - 2 * c, c))


def turn(n, k):
    return [(i, (i + k) % n) for i in range(n)]


def swap(v):
    return lax.ppermute(v, "core", turn(NC, 1))


def like(shape, dtype):
    return jax.ShapeDtypeStruct(shape, dtype)


def params(n=48):
    return pltpu.CompilerParams(vmem_limit_bytes=n * 1024 * 1024)


def cost(flops, moved):
    return pl.CostEstimate(flops=flops, bytes_accessed=moved, transcendentals=0)


def dot(a, b, dims=NN):
    return lax.dot_general(a, b, dims, preferred_element_type=f32)


def column_to_rows(v):
    return jnp.broadcast_to(v, (v.shape[0], 128)).T


def row_to_columns(v):
    return jnp.broadcast_to(v, (128, v.shape[1])).T


def rows_body(live_ref, x_ref, gain_ref, cot_ref, gained_ref, grad_ref, turned_ref):
    gained_ref[...] = (x_ref[...].astype(f32) * gain_ref[...].astype(f32)).astype(bf16)
    at = lax.broadcasted_iota(i32, (ROWS, WIDTH), 0)
    grad = jnp.where(at < live_ref[0], cot_ref[...].astype(f32), 0.0)
    grad_ref[...] = grad.astype(bf16)
    turned_ref[...] = grad.T.astype(bf16)


def rows_kernel(live, x, gain, cot):
    return pl.pallas_call(
        rows_body,
        in_specs=[SMEM, VMEM, VMEM, VMEM],
        out_specs=[VMEM] * 3,
        out_shape=[like((ROWS, WIDTH), bf16)] * 2 + [like((WIDTH, ROWS), bf16)],
        compiler_params=params(),
    )(live, x, gain, cot)


def inner_body(x_ref, gained_ref, grad_ref, down_ref, up_ref, tenant_ref, out_ref):
    tenant = tenant_ref[...]
    for at, w_ref, v_ref in ((0, down_ref, gained_ref), (RANK, up_ref, grad_ref)):
        every = dot(w_ref[...], v_ref[...], NT)
        picked = jnp.zeros((RANK, ROWS), f32)
        for t in range(TENANTS):
            picked = picked + jnp.where(tenant == t, every[t * RANK : (t + 1) * RANK], 0.0)
        out_ref[at : at + RANK] = picked
    x = x_ref[...].astype(f32)
    out_ref[2 * RANK :] = column_to_rows(jnp.sum(x * x, axis=1, keepdims=True))[:8]


def inner_kernel(x, gained, grad, down, up, tenant):
    return pl.pallas_call(
        inner_body,
        in_specs=[VMEM] * 6,
        out_specs=VMEM,
        out_shape=like((2 * RANK + 8, ROWS), f32),
        compiler_params=params(),
        cost_estimate=cost(2**26, 2**20),
    )(x, gained, grad, down, up, tenant)


def part_body(counts, spots_ref, turned_ref, *refs):
    n = len(counts)
    refs = list(refs)
    w = [refs.pop(0) for _ in range(n)]
    adds = [[refs.pop(0) for _ in range(k)] for k in counts]
    outs = refs[len(refs) - n :]
    turned = turned_ref[...]
    for i in range(n):
        for at in range(w[i].shape[0]):
            total = dot(w[i][at, 0, 0], turned)
            for a in adds[i]:
                total = total + a[at].astype(f32)
            outs[i][at] = total.astype(bf16)


def part_kernel(w5, turned, spots, first, adds, tokens, tiles=4):
    n = len(adds)
    step = NZ // tiles
    w_specs = [
        pl.BlockSpec(
            (step, 1, 1, WIDTH, WIDTH),
            lambda i, s, k=k: (i, s[2 * (first + k)], s[2 * (first + k) + 1], 0, 0),
        )
        for k in range(n)
    ]
    tile = pl.BlockSpec((step, WIDTH, ROWS), lambda i, s: (i, 0, 0))
    flat = [a for some in adds for a in some]
    return pl.pallas_call(
        functools.partial(part_body, [len(a) for a in adds]),
        grid_spec=pltpu.PrefetchScalarGridSpec(
            num_scalar_prefetch=1,
            grid=(tiles,),
            in_specs=[pl.BlockSpec((WIDTH, ROWS), lambda i, s: (0, 0))]
            + w_specs
            + [tile] * len(flat)
            + [HBM] * len(tokens),
            out_specs=[tile] * n,
        ),
        out_shape=[like((NZ, WIDTH, ROWS), bf16)] * n,
        compiler_params=params(),
        cost_estimate=cost(n * 2**27, n * 2**21),
    )(spots, turned, *([w5] * n), *flat, *tokens)


def last_part_body(spots_ref, turned_ref, w_ref, a_ref, b_ref, c_ref, *refs):
    outs = refs[len(refs) - NZ :]
    turned = turned_ref[...]
    z = spots_ref[16]
    for k in range(NZ):
        at = (z + k) % NZ
        total = dot(w_ref[at, 0, 0], turned)
        for a in (a_ref, b_ref, c_ref):
            total = total + a[at].astype(f32)
        outs[k][...] = total.astype(bf16)


def last_part_kernel(w5, turned, spots, at, adds, tokens):
    whole = pl.BlockSpec((NZ, WIDTH, ROWS), lambda i, s: (0, 0, 0))
    flat = pl.BlockSpec((WIDTH, ROWS), lambda i, s: (0, 0))
    return pl.pallas_call(
        last_part_body,
        grid_spec=pltpu.PrefetchScalarGridSpec(
            num_scalar_prefetch=1,
            grid=(1,),
            in_specs=[
                flat,
                pl.BlockSpec(
                    (NZ, 1, 1, WIDTH, WIDTH), lambda i, s: (0, s[2 * at], s[2 * at + 1], 0, 0)
                ),
            ]
            + [whole] * 3
            + [HBM] * len(tokens),
            out_specs=[flat] * NZ,
        ),
        out_shape=[like((WIDTH, ROWS), bf16)] * NZ,
        compiler_params=params(),
        cost_estimate=cost(2**27, 2**21),
    )(spots, turned, w5, *adds, *tokens)


def block_body(spots_ref, *refs):
    own, other, grad_ref = refs[:NY], refs[NY : 2 * NY], refs[2 * NY]
    block_ref, both_ref = refs[2 * NY + 1 :]
    y, core = spots_ref[17], spots_ref[18]
    for j in range(NY):
        at = ((y + j) % NY) * NC
        block_ref[at + core] = own[j][...]
        block_ref[at + 1 - core] = other[j][...]
    both_ref[0] = own[0][...]
    both_ref[1] = grad_ref[...]


def block_kernel(spots, own, other, grad):
    return pl.pallas_call(
        block_body,
        in_specs=[SMEM] + [VMEM] * (2 * NY + 1),
        out_specs=[VMEM] * 2,
        out_shape=[like((NY * NC, ROWS, WIDTH), bf16), like((2, ROWS, WIDTH), bf16)],
        compiler_params=params(),
    )(spots, *own, *other, grad)


def frozen_body(n, has_acc, spots_ref, *refs):
    refs = list(refs)
    acc_ref = refs.pop(0) if has_acc else None
    xs, ws, out_ref = refs[:n], refs[n : 2 * n], refs[2 * n]
    total = None
    for x_ref, w_ref in zip(xs, ws):
        for g in range(x_ref.shape[0]):
            term = dot(x_ref[g], w_ref[0, g])
            total = term if total is None else total + term

    @pl.when(pl.program_id(0) == 0)
    def _():
        out_ref[...] = total + acc_ref[...] if has_acc else total

    @pl.when(pl.program_id(0) > 0)
    def _():
        out_ref[...] = out_ref[...] + total


def frozen_kernel(w4, spots, acc, blocks, ats, tiles=4):
    n = len(blocks)
    flat = pl.BlockSpec((ROWS, WIDTH), lambda i, s: (0, 0))
    step = blocks[0].shape[0] // tiles
    has_acc = acc is not None
    return pl.pallas_call(
        functools.partial(frozen_body, n, has_acc),
        grid_spec=pltpu.PrefetchScalarGridSpec(
            num_scalar_prefetch=1,
            grid=(tiles,),
            in_specs=[flat] * has_acc
            + [pl.BlockSpec((step, ROWS, WIDTH), lambda i, s: (i, 0, 0))] * n
            + [
                pl.BlockSpec((1, step, WIDTH, WIDTH), lambda i, s, a=a: (s[a], i, 0, 0))
                for a in ats
            ],
            out_specs=flat,
        ),
        out_shape=like((ROWS, WIDTH), f32),
        compiler_params=params(),
        cost_estimate=cost(n * 2**27, n * 2**20),
    )(spots, *([acc] * has_acc), *blocks, *([w4] * n))


def final_body(spots_ref, acc_ref, a_ref, b_ref, wa_ref, wb_ref, scale_ref, small_ref, up_ref, tenant_ref, out_ref):
    total = acc_ref[...]
    for x_ref, w_ref in ((a_ref, wa_ref), (b_ref, wb_ref)):
        for g in range(x_ref.shape[0]):
            total = total + dot(x_ref[g], w_ref[0, g])
    tenant = tenant_ref[...]
    inner = small_ref[:RANK].astype(f32)
    spread = jnp.concatenate([jnp.where(tenant == t, inner, 0.0) for t in range(TENANTS)])
    adapted = dot(spread.T.astype(bf16), up_ref[...])
    scale = row_to_columns(scale_ref[:1])[:, :1]
    out_ref[...] = (scale * total + ADAPTER_SCALE * adapted).astype(bf16)


def final_kernel(w_half, spots, acc, a, b, scale, small, up, tenant):
    def full(v):
        return pl.BlockSpec(v.shape, lambda i, s, n=v.ndim: (0,) * n)

    half = (1, NY * NC // 2, WIDTH, WIDTH)
    return pl.pallas_call(
        final_body,
        grid_spec=pltpu.PrefetchScalarGridSpec(
            num_scalar_prefetch=1,
            grid=(1,),
            in_specs=[full(acc), full(a), full(b)]
            + [pl.BlockSpec(half, lambda i, s, k=k: (s[k], 0, 0, 0)) for k in (26, 27)]
            + [full(scale), full(small), full(up), full(tenant)],
            out_specs=full(acc),
        ),
        out_shape=like((ROWS, WIDTH), bf16),
        compiler_params=params(),
        cost_estimate=cost(2**28, 2**21),
    )(spots, acc, a, b, w_half, w_half, scale, small, up, tenant)


def gradient_body(*refs):
    pieces, (down_ref, back_ref, tenant_ref, out_ref) = refs[:NZ], refs[NZ:]
    total = pieces[0][...].astype(f32)
    for p in pieces[1:]:
        total = total + p[...].astype(f32)
    tenant = tenant_ref[...]
    back = back_ref[...].astype(f32)
    spread = jnp.concatenate([jnp.where(tenant == t, back, 0.0) for t in range(TENANTS)])
    adapter = dot(down_ref[...].astype(f32).T.astype(bf16), spread.astype(bf16))
    out_ref[...] = (total + ADAPTER_SCALE * adapter).astype(bf16)


def gradient_kernel(pieces, down, back, tenant):
    return pl.pallas_call(
        gradient_body,
        in_specs=[VMEM] * (NZ + 3),
        out_specs=VMEM,
        out_shape=like((WIDTH, ROWS), bf16),
        compiler_params=params(),
        cost_estimate=cost(2**25, 2**20),
    )(*pieces, down, back, tenant)


def small_body(a_ref, b_ref, tenant_ref, small_ref, back_ref, scale_ref):
    total = a_ref[...] + b_ref[...]
    scale = lax.rsqrt(total[2 * RANK : 2 * RANK + 1] / FULL + RMS_EPS)
    back = total[RANK : 2 * RANK]
    small_ref[:RANK] = (total[:RANK] * scale).astype(bf16)
    small_ref[RANK : 2 * RANK] = (back * scale).astype(bf16)
    small_ref[2 * RANK :] = jnp.broadcast_to(tenant_ref[...].astype(f32), (16, ROWS)).astype(bf16)
    back_ref[...] = back.astype(bf16)
    scale_ref[...] = jnp.broadcast_to(scale, (8, ROWS))


def small_kernel(a, b, tenant):
    return pl.pallas_call(
        small_body,
        in_specs=[VMEM] * 3,
        out_specs=[VMEM] * 3,
        out_shape=[
            like((2 * RANK + 16, ROWS), bf16),
            like((RANK, ROWS), bf16),
            like((8, ROWS), f32),
        ],
        compiler_params=params(),
    )(a, b, tenant)


def lift(v, size):
    return jnp.broadcast_to(v[:, None, :], (OWNED, RANK, size)).reshape(OWNED * RANK, size)


def slots_body(slot_ref, spots_ref, *refs):
    smalls, boths = refs[:NX], refs[NX : 2 * NX]
    row_ref, col_ref, ga_ref, gb_ref, row_out, col_out, sum_ref = refs[2 * NX :]
    first = spots_ref[19] * OWNED
    a_rows, b_rows = [], []
    for small_ref in smalls:
        tenant = small_ref[2 * RANK : 2 * RANK + 16].astype(f32)[:1]
        slot = jnp.full((1, ROWS), -1, i32)
        for t in range(TENANTS):
            slot = jnp.where(tenant == t, slot_ref[t], slot)
        inner = small_ref[:RANK].astype(f32)
        back = small_ref[RANK : 2 * RANK].astype(f32)
        a_rows.append(
            jnp.concatenate([jnp.where(slot == first + s, back, 0.0) for s in range(OWNED)])
        )
        b_rows.append(
            jnp.concatenate([jnp.where(slot == first + s, inner, 0.0) for s in range(OWNED)])
        )
    for rows, at, out_ref in ((a_rows, 0, ga_ref), (b_rows, 1, gb_ref)):
        total = dot(rows[0].astype(bf16), boths[0][at])
        for k in range(1, NX):
            total = total + dot(rows[k].astype(bf16), boths[k][at])
        out_ref[...] = ADAPTER_SCALE * total
    sq_a = ga_ref[...] * ga_ref[...] + SQ_EPS
    sq_b = gb_ref[...] * gb_ref[...] + SQ_EPS
    row_new = BETA_TWO * row_ref[...] + (1.0 - BETA_TWO) * (
        jnp.sum(sq_a.reshape(OWNED, RANK, WIDTH), axis=1) / RANK
    )
    row_out[...] = row_new
    col_out[...] = BETA_TWO * col_ref[...] + (1.0 - BETA_TWO) * (
        jnp.sum(sq_b.reshape(OWNED, RANK, WIDTH), axis=1) / RANK
    )
    lane = lax.broadcasted_iota(i32, (OWNED * RANK, 128), 1)
    columns = [jnp.sum(v, axis=1, keepdims=True) for v in (sq_a, sq_b, lift(row_new, WIDTH))]
    mixed = jnp.where(lane == 0, columns[0], jnp.where(lane == 1, columns[1], columns[2]))
    sum_ref[...] = mixed.T[:8]


def slots_kernel(slot, spots, smalls, boths, row, col):
    n = OWNED * RANK
    return pl.pallas_call(
        slots_body,
        in_specs=[SMEM] * 2 + [VMEM] * (2 * NX + 2),
        out_specs=[VMEM] * 5,
        out_shape=[like((n, WIDTH), f32)] * 2
        + [like((OWNED, WIDTH), f32)] * 2
        + [like((8, n), f32)],
        compiler_params=params(),
        cost_estimate=cost(2**27, 2**21),
    )(slot, spots, *smalls, *boths, row, col)


def update_body(p_ref, q_ref, ga_ref, gb_ref, row_ref, col_ref, dcol_ref, urow_ref, ua_ref, ub_ref, ca_ref, rb_ref):
    total = p_ref[...] + q_ref[...]
    col_a = BETA_TWO * dcol_ref[...] + (1.0 - BETA_TWO) * (total[0:1] / FULL)
    row_b = BETA_TWO * urow_ref[...] + (1.0 - BETA_TWO) * (total[1:2] / FULL)
    ca_ref[...] = col_a
    rb_ref[...] = row_b
    col_a = row_to_columns(col_a)[:, :1]
    row_b = row_to_columns(row_b)
    mean_a = row_to_columns(total[2:3])[:, :1] / FULL
    mean_b = lift(jnp.sum(row_b.reshape(OWNED, RANK, 128), axis=1), 128)[:, :1] / RANK
    ua_ref[...] = ga_ref[...] * lax.rsqrt(lift(row_ref[...], WIDTH) * col_a / mean_a)
    ub_ref[...] = gb_ref[...] * lax.rsqrt(row_b[:, :1] * lift(col_ref[...], WIDTH) / mean_b)


def update_kernel(p, q, ga, gb, row, col, dcol, urow):
    n = OWNED * RANK
    return pl.pallas_call(
        update_body,
        in_specs=[VMEM] * 8,
        out_specs=[VMEM] * 4,
        out_shape=[like((n, WIDTH), f32)] * 2 + [like((1, n), f32)] * 2,
        compiler_params=params(),
        cost_estimate=cost(2**20, 2**20),
    )(p, q, ga, gb, row, col, dcol, urow)


def add_body(a_ref, b_ref, *refs):
    refs[-1][...] = a_ref[...] + b_ref[...]


def add_kernel(a, b, *tokens):
    return pl.pallas_call(
        add_body,
        in_specs=[VMEM] * 2 + [HBM] * len(tokens),
        out_specs=VMEM,
        out_shape=like(a.shape, a.dtype),
        compiler_params=params(),
    )(a, b, *tokens)


def all_sum(v, core, *tokens):
    v = v + swap(v)
    a = lax.ppermute(v, F, plane_moves(lambda z, y, c: (z, y ^ (1 + c), c)))
    b = lax.ppermute(v, F, plane_moves(lambda z, y, c: (z, y ^ 3, c) if c else None))
    q = jnp.where(core == 0, v + a, a + b)
    v = add_kernel(q, swap(q), *tokens)
    a, b, d = [
        lax.ppermute(v, F, plane_moves(lambda z, y, c: (z ^ (k + 3 * c), y, c)))
        for k in (1, 2, 3)
    ]
    e = lax.ppermute(v, F, plane_moves(lambda z, y, c: (z ^ 7, y, c) if c else None))
    q = jnp.where(core == 0, (v + a) + (b + d), (a + b) + (d + e))
    return q, swap(q)


def on_device(
    inputs,
    norm_gain_vector,
    weight,
    down_adapters,
    up_adapters,
    tenant,
    tenant_slot_index,
    live_row_count,
    cotangent,
    down_row_factor,
    down_column_factor,
    up_row_factor,
    up_column_factor,
):
    dp = lax.axis_index("dp")
    z, y, core = lax.axis_index("z"), lax.axis_index("y"), lax.axis_index("core")
    opposite = 1 - core
    sign = 1 - 2 * core
    y_two, y_keep, y_send = (y + 2) % NY, (y + 1 + 2 * core) % NY, (y + 3 + 2 * core) % NY
    z_steps = [(z + NZ - s * sign * way) % NZ for s in (1, 2, 3) for way in (1, -1)]
    z_far = (z + NZ // 2) % NZ
    spots = jnp.stack(
        [y_two, opposite, y_send, core, y_send, opposite, y, opposite]
        + [y_two, core, y_keep, opposite, y_keep, core, y, core]
        + [z, y, core, dp]
        + z_steps
        + [z_far * 2 + core, z_far * 2 + opposite]
    ).astype(i32)
    down = down_adapters.transpose(1, 2, 0).reshape(TENANTS * RANK, WIDTH)
    up = up_adapters.reshape(TENANTS * RANK, WIDTH)
    tenant = tenant.reshape(1, ROWS)
    w5 = weight.reshape(NZ, NY, NC, WIDTH, WIDTH)
    w4 = weight.reshape(NZ, NY * NC, WIDTH, WIDTH)
    w_half = weight.reshape(NZ * 2, NY * NC // 2, WIDTH, WIDTH)

    gained, grad, turned = rows_kernel(
        live_row_count, inputs, norm_gain_vector.reshape(1, WIDTH), cotangent
    )
    own = [gained] + [lax.ppermute(gained, "y", turn(NY, k)) for k in (3, 2, 1)]
    other = [swap(v) for v in own]
    packed = inner_kernel(inputs, gained, grad, down, up, tenant)

    s_two, s_far, s_near, s_own = part_kernel(w5, turned, spots, 0, [[], [], [], []], [])
    r_two, r_far, r_near, r_own = [swap(v) for v in (s_two, s_far, s_near, s_own)]

    block, both = block_kernel(spots, own, other, grad)
    one = lax.ppermute(block, F, Z_BY_CORE)
    one_o = swap(one)
    two = lax.ppermute(one, F, Z_BY_CORE)
    two_o = swap(two)
    three = lax.ppermute(two, F, Z_BY_CORE)
    three_o = swap(three)
    half = jnp.where(core == 0, three[: NY * NC // 2], three[NY * NC // 2 :])
    four = lax.ppermute(half, F, Z_BY_CORE)
    four_o = swap(four)

    t_two, t_far = part_kernel(w5, turned, spots, 4, [[r_two], [r_far]], [block])
    g_two = lax.ppermute(t_two, F, Y_BY_CORE)
    g_far = lax.ppermute(t_far, F, Y_BY_CORE)
    (t_near,) = part_kernel(w5, turned, spots, 6, [[r_near, g_two]], [one])
    g_near = lax.ppermute(t_near, F, Y_BY_CORE)
    reduced = last_part_kernel(w5, turned, spots, 7, [r_own, swap(g_far), g_near], [two])
    pieces = [reduced[0]] + [
        lax.ppermute(reduced[k], "z", turn(NZ, k)) for k in (4, 3, 5, 2, 6, 1, 7)
    ]

    boths = [both] + [lax.ppermute(both, "dp", turn(NX, k)) for k in (1, 3, 2)]
    p, q = all_sum(packed, core, block)
    small, back, scale = small_kernel(p, q, tenant)
    smalls = [small] + [lax.ppermute(small, "dp", turn(NX, k)) for k in (1, 3, 2)]

    frozen = frozen_kernel(w4, spots, None, [block], [16])
    frozen = frozen_kernel(w4, spots, frozen, [one, one_o], [20, 21])
    frozen = frozen_kernel(w4, spots, frozen, [two, two_o], [22, 23])
    frozen = frozen_kernel(w4, spots, frozen, [three, three_o], [24, 25])
    projected = final_kernel(w_half, spots, frozen, four, four_o, scale, small, up, tenant)

    normed_gradient_transposed = gradient_kernel(pieces, down, back, tenant)

    ga, gb, row_a_new, col_b_new, moments = slots_kernel(
        tenant_slot_index, spots, smalls, boths, down_row_factor, up_column_factor
    )
    p, q = all_sum(moments, core)
    n = OWNED * RANK
    update_a, update_b, col_a_new, row_b_new = update_kernel(
        p,
        q,
        ga,
        gb,
        row_a_new,
        col_b_new,
        down_column_factor.reshape(1, n),
        up_row_factor.reshape(1, n),
    )
    return (
        projected,
        normed_gradient_transposed,
        update_a.reshape(OWNED, RANK, WIDTH).swapaxes(1, 2),
        update_b.reshape(OWNED, RANK, WIDTH),
        row_a_new,
        col_a_new.reshape(OWNED, RANK),
        row_b_new.reshape(OWNED, RANK),
        col_b_new,
    )


def solution(mesh):
    split = Mesh(mesh.devices.reshape(NX, NZ, NY, NC), ("dp",) + F)
    return jax.shard_map(
        on_device,
        mesh=split,
        in_specs=(
            P("dp", F),
            P(F),
            P(None, F),
            P(F, None, None),
            P(None, None, F),
            P("dp"),
            P(),
            P("dp"),
            P("dp", F),
            P("dp", F),
            P("dp", None),
            P("dp", None),
            P("dp", F),
        ),
        out_specs=(
            P("dp", F),
            P(F, "dp"),
            P("dp", F, None),
            P("dp", None, F),
            P("dp", F),
            P("dp", None),
            P("dp", None),
            P("dp", F),
        ),
        check_vma=False,
    )
```

profile of v0, /device:TPU:2, one launch (start us, length us, event | category | flops | bytes accessed | tf_op | source)
XLA Modules:
  0.0 187.0 jit_solution(2529574980112956040)
XLA Ops:
  2.0 0.8 copy-done.8
  2.8 0.8 copy-done.16
  3.7 3.1 %collective-permute-start = (bf16[128,256]{1,0:T(8,128)(2,1)S(1)}, bf16[128,256]{1,0:T(8,128)(2,1)S(1)}, u32[]{:S(2)}, u32[]{:S(2)}) collective-permute-start(bf16[128,256]{1,0:T(8,128)(2,1)S(1)} %get-tuple-element.39.refs_0_.gained_ref), channel_id=1, source_target_pairs={{0,6},{2,0},{4,2},{6,4},{1,7},{3,1},{5,3},{7,5},{8,14},{10,8},{12,... | collective-permute-start | bytes 196616 | tf_op jit(solution)/shard_map/ppermute | solution.py:494
  7.5 1.0 collective-permute-start.2
  9.0 3.7 %collective-permute-done.1.refs_2_ = bf16[128,256]{1,0:T(8,128)(2,1)S(1)} collective-permute-done((bf16[128,256]{1,0:T(8,128)(2,1)S(1)}, bf16[128,256]{1,0:T(8,128)(2,1)S(1)}, u32[]{:S(2)}, u32[]{:S(2)}) %collective-permute-start.1) | collective-permute-done | bytes 65568 | tf_op jit(solution)/shard_map/ppermute | solution.py:494
  13.5 5.0 %shard_map.198 = (bf16[8,256,128]{2,1,0:T(8,128)(2,1)}, bf16[8,256,128]{2,1,0:T(8,128)(2,1)}, bf16[8,256,128]{2,1,0:T(8,128)(2,1)S(1)}, bf16[8,256,128]{2,1,0:T(8,128)(2,1)S(1)}) custom-call(s32[28]{0:T(128)S(1)} %stack.79.spots_ref, bf16[256,128]{1,0:T(8,128)(2,1)S(1)} %get-tuple-element.44.turned_ref, bf16[8,4,2,256,256]{4,3,2,1,0:T(8,128)(2,1)} %bitcast.36, ...), custom_call_target="tpu_custom_call" | custom-call | flops 536870912 | bytes 8388608 | tf_op jit(solution)/shard_map/pallas_call | solution.py:144
  20.5 2.0 %collective-permute-start.7 = (bf16[8,128,256]{2,1,0:T(8,128)(2,1)S(1)}, bf16[8,128,256]{2,1,0:T(8,128)(2,1)S(1)}, u32[]{:S(2)}, u32[]{:S(2)}) collective-permute-start(bf16[8,128,256]{2,1,0:T(8,128)(2,1)S(1)} %get-tuple-element.41.refs_0_.refs_4_), channel_id=1, source_target_pairs={{0,8},{1,57},{2,10},{3,59},{4,12},{5,61},{6,14},{7,63},{8,16},{9,1... | collective-permute-start | bytes 1572872 | tf_op jit(solution)/shard_map/ppermute | solution.py:502
  22.8 4.2 %collective-permute-start.15 = (f32[72,128]{1,0:T(8,128)S(1)}, f32[72,128]{1,0:T(8,128)S(1)}, u32[]{:S(2)}, u32[]{:S(2)}) collective-permute-start(f32[72,128]{1,0:T(8,128)S(1)} %shard_map.194), channel_id=1, source_target_pairs={{0,1},{1,0},{2,3},{3,2},{4,5},{5,4},{6,7},{7,6},{8,9},{9,8},{10,11... | collective-permute-start | bytes 110600 | tf_op jit(solution)/shard_map/ppermute | solution.py:49
  27.0 0.9 collective-permute-done.15
  28.7 3.3 %collective-permute-done.16 = f32[72,128]{1,0:T(8,128)S(1)} collective-permute-done((f32[72,128]{1,0:T(8,128)S(1)}, f32[72,128]{1,0:T(8,128)S(1)}, u32[]{:S(2)}, u32[]{:S(2)}) %collective-permute-start.16) | collective-permute-done | bytes 36896 | tf_op jit(solution)/shard_map/ppermute | solution.py:442
  31.9 3.4 %collective-permute-start.18 = (f32[72,128]{1,0:T(8,128)S(1)}, f32[72,128]{1,0:T(8,128)S(1)}, u32[]{:S(2)}, u32[]{:S(2)}) collective-permute-start(f32[72,128]{1,0:T(8,128)S(1)} %add_select_fusion.1.a_ref), channel_id=1, source_target_pairs={{0,1},{1,0},{2,3},{3,2},{4,5},{5,4},{6,7},{7,6},{8,9},{9,8},{10,11... | collective-permute-start | bytes 110600 | tf_op jit(solution)/shard_map/ppermute | solution.py:49
  35.4 0.9 collective-permute-done.18.b_ref
  36.4 2.5 %collective-permute-start.20 = (f32[72,128]{1,0:T(8,128)S(1)}, f32[72,128]{1,0:T(8,128)S(1)}, u32[]{:S(2)}, u32[]{:S(2)}) collective-permute-start(f32[72,128]{1,0:T(8,128)S(1)} %shard_map.195), channel_id=1, source_target_pairs={{0,16},{1,41},{2,18},{3,43},{4,20},{5,45},{6,22},{7,47},{8,24},{9,... | collective-permute-start | bytes 110600 | tf_op jit(solution)/shard_map/ppermute | solution.py:447
  38.8 1.9 %collective-permute-start.21 = (f32[72,128]{1,0:T(8,128)S(1)}, f32[72,128]{1,0:T(8,128)S(1)}, u32[]{:S(2)}, u32[]{:S(2)}) collective-permute-start(f32[72,128]{1,0:T(8,128)S(1)} %shard_map.195), channel_id=1, source_target_pairs={{0,24},{1,49},{2,26},{3,51},{4,28},{5,53},{6,30},{7,55},{8,16},{9,... | collective-permute-start | bytes 110600 | tf_op jit(solution)/shard_map/ppermute | solution.py:447
  41.5 3.6 %shard_map.199 = (bf16[8,256,128]{2,1,0:T(8,128)(2,1)S(1)}, bf16[8,256,128]{2,1,0:T(8,128)(2,1)S(1)}) custom-call(s32[28]{0:T(128)S(1)} %stack.79.spots_ref, bf16[256,128]{1,0:T(8,128)(2,1)S(1)} %get-tuple-element.44.turned_ref, bf16[8,4,2,256,256]{4,3,2,1,0:T(8,128)(2,1)} %bitcast.40, bf16[8,4,2,256,256]{4,3,2,1,0:T(8,128)(2,1)} %bitcast.41, ...), custom_call_target="tpu_custom_call" | custom-call | flops 268435456 | bytes 4194304 | tf_op jit(solution)/shard_map/pallas_call | solution.py:144
  45.1 6.2 %collective-permute-start.29 = (bf16[8,256,128]{2,1,0:T(8,128)(2,1)S(1)}, bf16[8,256,128]{2,1,0:T(8,128)(2,1)S(1)}, u32[]{:S(2)}, u32[]{:S(2)}) collective-permute-start(bf16[8,256,128]{2,1,0:T(8,128)(2,1)S(1)} %copy-done.26), channel_id=1, source_target_pairs={{0,1},{1,0},{2,3},{3,2},{4,5},{5,4},{6,7},{7,6},{8,9},{9,8},{10,11... | collective-permute-start | bytes 1572872 | tf_op jit(solution)/shard_map/ppermute | solution.py:49
  52.0 1.3 collective-permute-start.27
  53.3 1.6 collective-permute-start.39
  54.9 2.3 %collective-permute-done.39.refs_1_ = bf16[80,128]{1,0:T(8,128)(2,1)S(1)} collective-permute-done((bf16[80,128]{1,0:T(8,128)(2,1)S(1)}, bf16[80,128]{1,0:T(8,128)(2,1)S(1)}, u32[]{:S(2)}, u32[]{:S(2)}) %collective-permute-start.39) | collective-permute-done | bytes 20512 | tf_op jit(solution)/shard_map/ppermute | solution.py:525
  57.2 1.7 collective-permute-start.40
  59.0 2.1 %collective-permute-done.40.refs_2_ = bf16[80,128]{1,0:T(8,128)(2,1)S(1)} collective-permute-done((bf16[80,128]{1,0:T(8,128)(2,1)S(1)}, bf16[80,128]{1,0:T(8,128)(2,1)S(1)}, u32[]{:S(2)}, u32[]{:S(2)}) %collective-permute-start.40) | collective-permute-done | bytes 20512 | tf_op jit(solution)/shard_map/ppermute | solution.py:525
  61.0 3.3 %collective-permute-start.41 = (bf16[80,128]{1,0:T(8,128)(2,1)S(1)}, bf16[80,128]{1,0:T(8,128)(2,1)S(1)}, u32[]{:S(2)}, u32[]{:S(2)}) collective-permute-start(bf16[80,128]{1,0:T(8,128)(2,1)S(1)} %get-tuple-element.43.small_ref.refs_0_), channel_id=1, source_target_pairs={{0,128},{64,192},{128,0},{192,64},{1,129},{65,193},{129,1},{193,65... | collective-permute-start | bytes 61448 | tf_op jit(solution)/shard_map/ppermute | solution.py:525
  64.3 1.9 %collective-permute-done.41.refs_3_ = bf16[80,128]{1,0:T(8,128)(2,1)S(1)} collective-permute-done((bf16[80,128]{1,0:T(8,128)(2,1)S(1)}, bf16[80,128]{1,0:T(8,128)(2,1)S(1)}, u32[]{:S(2)}, u32[]{:S(2)}) %collective-permute-start.41) | collective-permute-done | bytes 20512 | tf_op jit(solution)/shard_map/ppermute | solution.py:525
  66.3 1.5 collective-permute-start.42
  67.8 3.5 %collective-permute-done.42.refs_5_ = bf16[2,128,256]{2,1,0:T(8,128)(2,1)S(1)} collective-permute-done((bf16[2,128,256]{2,1,0:T(8,128)(2,1)S(1)}, bf16[2,128,256]{2,1,0:T(8,128)(2,1)S(1)}, u32[]{:S(2)}, u32[]{:S(2)}) %collective-permute-start.42) | collective-permute-done | bytes 131104 | tf_op jit(solution)/shard_map/ppermute | solution.py:522
  71.3 3.0 %collective-permute-start.43 = (bf16[2,128,256]{2,1,0:T(8,128)(2,1)S(1)}, bf16[2,128,256]{2,1,0:T(8,128)(2,1)S(1)}, u32[]{:S(2)}, u32[]{:S(2)}) collective-permute-start(bf16[2,128,256]{2,1,0:T(8,128)(2,1)S(1)} %get-tuple-element.60.refs_4_), channel_id=1, source_target_pairs={{0,192},{64,0},{128,64},{192,128},{1,193},{65,1},{129,65},{193,129... | collective-permute-start | bytes 393224 | tf_op jit(solution)/shard_map/ppermute | solution.py:522
  74.2 1.0 collective-permute-start.11
  75.3 1.5 collective-permute-done.43.refs_6_
  76.7 4.0 %collective-permute-start.44 = (bf16[2,128,256]{2,1,0:T(8,128)(2,1)S(1)}, bf16[2,128,256]{2,1,0:T(8,128)(2,1)S(1)}, u32[]{:S(2)}, u32[]{:S(2)}) collective-permute-start(bf16[2,128,256]{2,1,0:T(8,128)(2,1)S(1)} %get-tuple-element.60.refs_4_), channel_id=1, source_target_pairs={{0,128},{64,192},{128,0},{192,64},{1,129},{65,193},{129,1},{193,65... | collective-permute-start | bytes 393224 | tf_op jit(solution)/shard_map/ppermute | solution.py:522
  80.8 2.9 %collective-permute-done.44.refs_7_ = bf16[2,128,256]{2,1,0:T(8,128)(2,1)S(1)} collective-permute-done((bf16[2,128,256]{2,1,0:T(8,128)(2,1)S(1)}, bf16[2,128,256]{2,1,0:T(8,128)(2,1)S(1)}, u32[]{:S(2)}, u32[]{:S(2)}) %collective-permute-start.44) | collective-permute-done | bytes 131104 | tf_op jit(solution)/shard_map/ppermute | solution.py:522
  83.8 1.6 shard_map.203
  86.6 3.2 %shard_map.200 = bf16[8,256,128]{2,1,0:T(8,128)(2,1)S(1)} custom-call(s32[28]{0:T(128)S(1)} %stack.79.spots_ref, bf16[256,128]{1,0:T(8,128)(2,1)S(1)} %get-tuple-element.44.turned_ref, bf16[8,4,2,256,256]{4,3,2,1,0:T(8,128)(2,1)} %bitcast.42, bf16[8,256,128]{2,1,0:T(8,128)(2,1)S(1)} %collective-permute-done.29.refs_1_, ...), custom_call_target="tpu_custom_call" | custom-call | flops 134217728 | bytes 2097152 | tf_op jit(solution)/shard_map/pallas_call | solution.py:144
  89.8 2.3 %collective-permute-start.31 = (bf16[8,256,128]{2,1,0:T(8,128)(2,1)S(1)}, bf16[8,256,128]{2,1,0:T(8,128)(2,1)S(1)}, u32[]{:S(2)}, u32[]{:S(2)}) collective-permute-start(bf16[8,256,128]{2,1,0:T(8,128)(2,1)S(1)} %shard_map.200), channel_id=1, source_target_pairs={{0,2},{1,7},{2,4},{3,1},{4,6},{5,3},{6,0},{7,5},{8,10},{9,15},{10,... | collective-permute-start | bytes 1572872 | tf_op jit(solution)/shard_map/ppermute | solution.py:516
  92.1 1.3 collective-permute-start.46
  93.4 5.6 %collective-permute-done.46 = f32[8,256]{1,0:T(8,128)S(1)} collective-permute-done((f32[8,256]{1,0:T(8,128)S(1)}, f32[8,256]{1,0:T(8,128)S(1)}, u32[]{:S(2)}, u32[]{:S(2)}) %collective-permute-start.46) | collective-permute-done | bytes 8224 | tf_op jit(solution)/shard_map/ppermute | solution.py:442
  99.6 3.4 %collective-permute-start.28 = (bf16[8,256,128]{2,1,0:T(8,128)(2,1)S(1)}, bf16[8,256,128]{2,1,0:T(8,128)(2,1)S(1)}, u32[]{:S(2)}, u32[]{:S(2)}) collective-permute-start(bf16[8,256,128]{2,1,0:T(8,128)(2,1)S(1)} %collective-permute-done.27), channel_id=1, source_target_pairs={{0,1},{1,0},{2,3},{3,2},{4,5},{5,4},{6,7},{7,6},{8,9},{9,8},{10,11... | collective-permute-start | bytes 1572872 | tf_op jit(solution)/shard_map/ppermute | solution.py:49
  103.1 0.9 collective-permute-start.48
  104.8 1.0 collective-permute-start.49
  105.9 2.6 %collective-permute-done.49 = f32[8,256]{1,0:T(8,128)S(1)} collective-permute-done((f32[8,256]{1,0:T(8,128)S(1)}, f32[8,256]{1,0:T(8,128)S(1)}, u32[]{:S(2)}, u32[]{:S(2)}) %collective-permute-start.49) | collective-permute-done | bytes 8224 | tf_op jit(solution)/shard_map/ppermute | solution.py:447
  108.5 4.5 %collective-permute-done.50 = f32[8,256]{1,0:T(8,128)S(1)} collective-permute-done((f32[8,256]{1,0:T(8,128)S(1)}, f32[8,256]{1,0:T(8,128)S(1)}, u32[]{:S(2)}, u32[]{:S(2)}) %collective-permute-start.50) | collective-permute-done | bytes 8224 | tf_op jit(solution)/shard_map/ppermute | solution.py:447
  113.0 1.2 collective-permute-start.51
  114.2 4.3 %collective-permute-done.51 = f32[8,256]{1,0:T(8,128)S(1)} collective-permute-done((f32[8,256]{1,0:T(8,128)S(1)}, f32[8,256]{1,0:T(8,128)S(1)}, u32[]{:S(2)}, u32[]{:S(2)}) %collective-permute-start.51) | collective-permute-done | bytes 8224 | tf_op jit(solution)/shard_map/ppermute | solution.py:447
  119.2 8.2 %collective-permute-start.8 = (bf16[8,128,256]{2,1,0:T(8,128)(2,1)S(1)}, bf16[8,128,256]{2,1,0:T(8,128)(2,1)S(1)}, u32[]{:S(2)}, u32[]{:S(2)}) collective-permute-start(bf16[8,128,256]{2,1,0:T(8,128)(2,1)S(1)} %collective-permute-done.7.refs_1_.refs_3_), channel_id=1, source_target_pairs={{0,1},{1,0},{2,3},{3,2},{4,5},{5,4},{6,7},{7,6},{8,9},{9,8},{10,11... | collective-permute-start | bytes 1572872 | tf_op jit(solution)/shard_map/ppermute | solution.py:49
  127.4 2.9 %collective-permute-start.13 = (bf16[4,128,256]{2,1,0:T(8,128)(2,1)S(1)}, bf16[4,128,256]{2,1,0:T(8,128)(2,1)}, u32[]{:S(2)}, u32[]{:S(2)}) collective-permute-start(bf16[4,128,256]{2,1,0:T(8,128)(2,1)S(1)} %slice_select_fusion), channel_id=1, source_target_pairs={{0,8},{1,57},{2,10},{3,59},{4,12},{5,61},{6,14},{7,63},{8,16},{9,1... | collective-permute-start | bytes 786440 | tf_op jit(solution)/shard_map/ppermute | solution.py:509
  130.9 2.8 %shard_map.201 = (bf16[256,128]{1,0:T(8,128)(2,1)S(1)}, bf16[256,128]{1,0:T(8,128)(2,1)}, bf16[256,128]{1,0:T(8,128)(2,1)S(1)}, bf16[256,128]{1,0:T(8,128)(2,1)S...) custom-call(s32[28]{0:T(128)S(1)} %stack.79.spots_ref, ...), custom_call_target="tpu_custom_call" | custom-call | flops 134217728 | bytes 2097152 | tf_op jit(solution)/shard_map/pallas_call | solution.py:176
  133.7 2.7 %collective-permute-start.32 = (bf16[256,128]{1,0:T(8,128)(2,1)S(1)}, bf16[256,128]{1,0:T(8,128)(2,1)S(1)}, u32[]{:S(2)}, u32[]{:S(2)}) collective-permute-start(bf16[256,128]{1,0:T(8,128)(2,1)S(1)} %get-tuple-element.52), channel_id=1, source_target_pairs={{0,32},{8,40},{16,48},{24,56},{32,0},{40,8},{48,16},{56,24},{1,33}... | collective-permute-start | bytes 196616 | tf_op jit(solution)/shard_map/ppermute | solution.py:519
  137.2 2.5 %collective-permute-start.33 = (bf16[256,128]{1,0:T(8,128)(2,1)S(1)}, bf16[256,128]{1,0:T(8,128)(2,1)S(1)}, u32[]{:S(2)}, u32[]{:S(2)}) collective-permute-start(bf16[256,128]{1,0:T(8,128)(2,1)S(1)} %get-tuple-element.53), channel_id=1, source_target_pairs={{0,24},{8,32},{16,40},{24,48},{32,56},{40,0},{48,8},{56,16},{1,25}... | collective-permute-start | bytes 196616 | tf_op jit(solution)/shard_map/ppermute | solution.py:519
  139.7 3.0 %collective-permute-done.32.refs_1_ = bf16[256,128]{1,0:T(8,128)(2,1)S(1)} collective-permute-done((bf16[256,128]{1,0:T(8,128)(2,1)S(1)}, bf16[256,128]{1,0:T(8,128)(2,1)S(1)}, u32[]{:S(2)}, u32[]{:S(2)}) %collective-permute-start.32) | collective-permute-done | bytes 65568 | tf_op jit(solution)/shard_map/ppermute | solution.py:519
  142.7 2.7 %collective-permute-start.34 = (bf16[256,128]{1,0:T(8,128)(2,1)S(1)}, bf16[256,128]{1,0:T(8,128)(2,1)S(1)}, u32[]{:S(2)}, u32[]{:S(2)}) collective-permute-start(bf16[256,128]{1,0:T(8,128)(2,1)S(1)} %get-tuple-element.54), channel_id=1, source_target_pairs={{0,40},{8,48},{16,56},{24,0},{32,8},{40,16},{48,24},{56,32},{1,41}... | collective-permute-start | bytes 196616 | tf_op jit(solution)/shard_map/ppermute | solution.py:519
  145.4 1.3 collective-permute-done.33.refs_2_
  147.1 2.3 %collective-permute-done.34.refs_3_ = bf16[256,128]{1,0:T(8,128)(2,1)S(1)} collective-permute-done((bf16[256,128]{1,0:T(8,128)(2,1)S(1)}, bf16[256,128]{1,0:T(8,128)(2,1)S(1)}, u32[]{:S(2)}, u32[]{:S(2)}) %collective-permute-start.34) | collective-permute-done | bytes 65568 | tf_op jit(solution)/shard_map/ppermute | solution.py:519
  150.1 4.4 %collective-permute-start.36 = (bf16[256,128]{1,0:T(8,128)(2,1)S(1)}, bf16[256,128]{1,0:T(8,128)(2,1)S(1)}, u32[]{:S(2)}, u32[]{:S(2)}) collective-permute-start(bf16[256,128]{1,0:T(8,128)(2,1)S(1)} %get-tuple-element.56), channel_id=1, source_target_pairs={{0,48},{8,56},{16,0},{24,8},{32,16},{40,24},{48,32},{56,40},{1,49}... | collective-permute-start | bytes 196616 | tf_op jit(solution)/shard_map/ppermute | solution.py:519
  155.2 1.0 collective-permute-start.37
  157.6 3.0 %collective-permute-start.38 = (bf16[256,128]{1,0:T(8,128)(2,1)}, bf16[256,128]{1,0:T(8,128)(2,1)}, u32[]{:S(2)}, u32[]{:S(2)}) collective-permute-start(bf16[256,128]{1,0:T(8,128)(2,1)} %get-tuple-element.58), channel_id=1, source_target_pairs={{0,56},{8,0},{16,8},{24,16},{32,24},{40,32},{48,40},{56,48},{1,57}... | collective-permute-start | bytes 196616 | tf_op jit(solution)/shard_map/ppermute | solution.py:519
  161.4 3.1 %shard_map.190.refs_0_ = f32[128,256]{1,0:T(8,128)S(1)} custom-call(s32[28]{0:T(128)S(1)} %stack.79.spots_ref, bf16[8,128,256]{2,1,0:T(8,128)(2,1)S(1)} %get-tuple-element.41.refs_0_.refs_4_, bf16[8,8,256,256]{3,2,1,0:T(8,128)(2,1)} %bitcast.44), custom_call_target="tpu_custom_call" | custom-call | flops 134217728 | bytes 1048576 | tf_op jit(solution)/shard_map/pallas_call | solution.py:243
  164.6 0.9 copy-done.5
  165.5 0.9 copy-done.7
  166.4 1.1 shard_map.205
  170.7 1.0 copy-done.3
  171.8 3.5 %shard_map.191.refs_0_ = f32[128,256]{1,0:T(8,128)S(1)} custom-call(s32[28]{0:T(128)S(1)} %stack.79.spots_ref, f32[128,256]{1,0:T(8,128)S(1)} %shard_map.190.refs_0_, bf16[8,128,256]{2,1,0:T(8,128)(2,1)S(1)} %collective-permute-done.7.refs_1_.refs_3_, bf16[8,128,256]{2,1,0:T(8,128)(2,1)S(1)} %copy-done.3, bf16[8,8,256,256]{3,2,1,0:T(8,128)(2,1)} %bitcast.45, ...), custom_call_target="tpu_custom_call" | custom-call | flops 268435456 | bytes 2097152 | tf_op jit(solution)/shard_map/pallas_call | solution.py:243
  175.3 1.8 shard_map.202
  177.1 3.4 %shard_map.192.refs_0_ = f32[128,256]{1,0:T(8,128)S(1)} custom-call(s32[28]{0:T(128)S(1)} %stack.79.spots_ref, f32[128,256]{1,0:T(8,128)S(1)} %shard_map.191.refs_0_, bf16[8,128,256]{2,1,0:T(8,128)(2,1)S(1)} %collective-permute-done.9.refs_1_.refs_0_, bf16[8,128,256]{2,1,0:T(8,128)(2,1)S(1)} %collective-permute-done.10.refs_2_, ...), custom_call_target="tpu_custom_call" | custom-call | flops 268435456 | bytes 2097152 | tf_op jit(solution)/shard_map/pallas_call | solution.py:243
  180.5 3.6 %shard_map.193.acc_ref = f32[128,256]{1,0:T(8,128)S(1)} custom-call(s32[28]{0:T(128)S(1)} %stack.79.spots_ref, f32[128,256]{1,0:T(8,128)S(1)} %shard_map.192.refs_0_, bf16[8,128,256]{2,1,0:T(8,128)(2,1)S(1)} %collective-permute-done.11.refs_1_, bf16[8,128,256]{2,1,0:T(8,128)(2,1)} %collective-permute-done.12.refs_2_, bf16[8,8,256,256]{3,2,1,0:T(8,128)(2,1)} %bitcast.49, ...), custom_call_target="tpu_custom_call" | custom-call | flops 268435456 | bytes 2097152 | tf_op jit(solution)/shard_map/pallas_call | solution.py:243
  184.1 2.9 %shard_map.197 = bf16[128,256]{1,0:T(8,128)(2,1)} custom-call(s32[28]{0:T(128)S(1)} %stack.79.spots_ref, f32[128,256]{1,0:T(8,128)S(1)} %shard_map.193.acc_ref, bf16[4,128,256]{2,1,0:T(8,128)(2,1)} %collective-permute-done.13.a_ref, bf16[4,128,256]{2,1,0:T(8,128)(2,1)} %collective-permute-done.14.b_ref, bf16[16,4,256,256]{3,2,1,0:T(8,128)(2,1)} %bitcast.51, ...), custom_call_target="tpu_custom_call" | custom-call | flops 268435456 | bytes 2097152 | tf_op jit(solution)/shard_map/pallas_call | solution.py:280
  (134 shorter events, 19.3 us)
Async XLA Ops:
  3.7 5.2 %collective-permute-start = (bf16[128,256]{1,0:T(8,128)(2,1)S(1)}, bf16[128,256]{1,0:T(8,128)(2,1)S(1)}, u32[]{:S(2)}, u32[]{:S(2)}) collective-permute-start(bf16[128,256]{1,0:T(8,128)(2,1)S(1)} %get-tuple-element.39.refs_0_.gained_ref), channel_id=1, source_target_pairs={{0,6},{2,0},{4,2},{6,4},{1,7},{3,1},{5,3},{7,5},{8,14},{10,8},{12,... | collective-permute-start | bytes 196616 | tf_op jit(solution)/shard_map/ppermute | solution.py:494
  6.8 5.8 %collective-permute-start.1 = (bf16[128,256]{1,0:T(8,128)(2,1)S(1)}, bf16[128,256]{1,0:T(8,128)(2,1)S(1)}, u32[]{:S(2)}, u32[]{:S(2)}) collective-permute-start(bf16[128,256]{1,0:T(8,128)(2,1)S(1)} %get-tuple-element.39.refs_0_.gained_ref), channel_id=1, source_target_pairs={{0,4},{2,6},{4,0},{6,2},{1,5},{3,7},{5,1},{7,3},{8,12},{10,14},{12... | collective-permute-start | bytes 196616 | tf_op jit(solution)/shard_map/ppermute | solution.py:494
  7.5 5.8 %collective-permute-start.2 = (bf16[128,256]{1,0:T(8,128)(2,1)S(1)}, bf16[128,256]{1,0:T(8,128)(2,1)S(1)}, u32[]{:S(2)}, u32[]{:S(2)}) collective-permute-start(bf16[128,256]{1,0:T(8,128)(2,1)S(1)} %get-tuple-element.39.refs_0_.gained_ref), channel_id=1, source_target_pairs={{0,2},{2,4},{4,6},{6,0},{1,3},{3,5},{5,7},{7,1},{8,10},{10,12},{12... | collective-permute-start | bytes 196616 | tf_op jit(solution)/shard_map/ppermute | solution.py:494
  8.4 11.4 %collective-permute-start.3 = (bf16[128,256]{1,0:T(8,128)(2,1)S(1)}, bf16[128,256]{1,0:T(8,128)(2,1)S(1)}, u32[]{:S(2)}, u32[]{:S(2)}) collective-permute-start(bf16[128,256]{1,0:T(8,128)(2,1)S(1)} %get-tuple-element.39.refs_0_.gained_ref), channel_id=1, source_target_pairs={{0,1},{1,0},{2,3},{3,2},{4,5},{5,4},{6,7},{7,6},{8,9},{9,8},{10,11... | collective-permute-start | bytes 196616 | tf_op jit(solution)/shard_map/ppermute | solution.py:49
  9.0 10.9 %collective-permute-start.4 = (bf16[128,256]{1,0:T(8,128)(2,1)S(1)}, bf16[128,256]{1,0:T(8,128)(2,1)S(1)}, u32[]{:S(2)}, u32[]{:S(2)}) collective-permute-start(bf16[128,256]{1,0:T(8,128)(2,1)S(1)} %collective-permute-done.refs_1_), channel_id=1, source_target_pairs={{0,1},{1,0},{2,3},{3,2},{4,5},{5,4},{6,7},{7,6},{8,9},{9,8},{10,11... | collective-permute-start | bytes 196616 | tf_op jit(solution)/shard_map/ppermute | solution.py:49
  12.6 7.3 %collective-permute-start.5 = (bf16[128,256]{1,0:T(8,128)(2,1)S(1)}, bf16[128,256]{1,0:T(8,128)(2,1)S(1)}, u32[]{:S(2)}, u32[]{:S(2)}) collective-permute-start(bf16[128,256]{1,0:T(8,128)(2,1)S(1)} %collective-permute-done.1.refs_2_), channel_id=1, source_target_pairs={{0,1},{1,0},{2,3},{3,2},{4,5},{5,4},{6,7},{7,6},{8,9},{9,8},{10,11... | collective-permute-start | bytes 196616 | tf_op jit(solution)/shard_map/ppermute | solution.py:49
  13.3 6.6 %collective-permute-start.6 = (bf16[128,256]{1,0:T(8,128)(2,1)S(1)}, bf16[128,256]{1,0:T(8,128)(2,1)S(1)}, u32[]{:S(2)}, u32[]{:S(2)}) collective-permute-start(bf16[128,256]{1,0:T(8,128)(2,1)S(1)} %collective-permute-done.2.refs_3_), channel_id=1, source_target_pairs={{0,1},{1,0},{2,3},{3,2},{4,5},{5,4},{6,7},{7,6},{8,9},{9,8},{10,11... | collective-permute-start | bytes 196616 | tf_op jit(solution)/shard_map/ppermute | solution.py:49
  13.4 9.1 %copy-start = (bf16[16,32,256]{2,1,0:T(8,128)(2,1)S(1)}, bf16[16,32,256]{2,1,0:T(8,128)(2,1)}, u32[]{:S(2)}) copy-start(bf16[16,32,256]{2,1,0:T(8,128)(2,1)} %param.17) | copy-start | bytes 786436
  13.4 9.1 %copy-start.1 = (bf16[256,16,32]{0,2,1:T(8,128)(2,1)S(1)}, bf16[256,16,32]{0,2,1:T(8,128)(2,1)}, u32[]{:S(2)}) copy-start(bf16[256,16,32]{0,2,1:T(8,128)(2,1)} %param.16) | copy-start | bytes 786436
  19.3 19.5 %collective-permute-start.25 = (bf16[8,256,128]{2,1,0:T(8,128)(2,1)}, bf16[8,256,128]{2,1,0:T(8,128)(2,1)S(1)}, u32[]{:S(2)}, u32[]{:S(2)}) collective-permute-start(bf16[8,256,128]{2,1,0:T(8,128)(2,1)} %get-tuple-element.46), channel_id=1, source_target_pairs={{0,1},{1,0},{2,3},{3,2},{4,5},{5,4},{6,7},{7,6},{8,9},{9,8},{10,11... | collective-permute-start | bytes 1572872 | tf_op jit(solution)/shard_map/ppermute | solution.py:49
  19.8 20.9 %collective-permute-start.26 = (bf16[8,256,128]{2,1,0:T(8,128)(2,1)}, bf16[8,256,128]{2,1,0:T(8,128)(2,1)S(1)}, u32[]{:S(2)}, u32[]{:S(2)}) collective-permute-start(bf16[8,256,128]{2,1,0:T(8,128)(2,1)} %get-tuple-element.47), channel_id=1, source_target_pairs={{0,1},{1,0},{2,3},{3,2},{4,5},{5,4},{6,7},{7,6},{8,9},{9,8},{10,11... | collective-permute-start | bytes 1572872 | tf_op jit(solution)/shard_map/ppermute | solution.py:49
  20.5 20.9 %collective-permute-start.7 = (bf16[8,128,256]{2,1,0:T(8,128)(2,1)S(1)}, bf16[8,128,256]{2,1,0:T(8,128)(2,1)S(1)}, u32[]{:S(2)}, u32[]{:S(2)}) collective-permute-start(bf16[8,128,256]{2,1,0:T(8,128)(2,1)S(1)} %get-tuple-element.41.refs_0_.refs_4_), channel_id=1, source_target_pairs={{0,8},{1,57},{2,10},{3,59},{4,12},{5,61},{6,14},{7,63},{8,16},{9,1... | collective-permute-start | bytes 1572872 | tf_op jit(solution)/shard_map/ppermute | solution.py:502
  22.8 5.0 %collective-permute-start.15 = (f32[72,128]{1,0:T(8,128)S(1)}, f32[72,128]{1,0:T(8,128)S(1)}, u32[]{:S(2)}, u32[]{:S(2)}) collective-permute-start(f32[72,128]{1,0:T(8,128)S(1)} %shard_map.194), channel_id=1, source_target_pairs={{0,1},{1,0},{2,3},{3,2},{4,5},{5,4},{6,7},{7,6},{8,9},{9,8},{10,11... | collective-permute-start | bytes 110600 | tf_op jit(solution)/shard_map/ppermute | solution.py:49
  27.9 4.0 %collective-permute-start.16 = (f32[72,128]{1,0:T(8,128)S(1)}, f32[72,128]{1,0:T(8,128)S(1)}, u32[]{:S(2)}, u32[]{:S(2)}) collective-permute-start(f32[72,128]{1,0:T(8,128)S(1)} %add.136), channel_id=1, source_target_pairs={{0,2},{1,5},{2,0},{3,7},{4,6},{5,1},{6,4},{7,3},{8,10},{9,13},{10,... | collective-permute-start | bytes 110600 | tf_op jit(solution)/shard_map/ppermute | solution.py:442
  28.0 3.9 %collective-permute-start.17 = (f32[72,128]{1,0:T(8,128)S(1)}, f32[72,128]{1,0:T(8,128)S(1)}, u32[]{:S(2)}, u32[]{:S(2)}) collective-permute-start(f32[72,128]{1,0:T(8,128)S(1)} %add.136), channel_id=1, source_target_pairs={{1,7},{3,5},{5,3},{7,1},{9,15},{11,13},{13,11},{15,9},{17,23},{19,... | collective-permute-start | bytes 110600 | tf_op jit(solution)/shard_map/ppermute | solution.py:443
  31.9 4.3 %collective-permute-start.18 = (f32[72,128]{1,0:T(8,128)S(1)}, f32[72,128]{1,0:T(8,128)S(1)}, u32[]{:S(2)}, u32[]{:S(2)}) collective-permute-start(f32[72,128]{1,0:T(8,128)S(1)} %add_select_fusion.1.a_ref), channel_id=1, source_target_pairs={{0,1},{1,0},{2,3},{3,2},{4,5},{5,4},{6,7},{7,6},{8,9},{9,8},{10,11... | collective-permute-start | bytes 110600 | tf_op jit(solution)/shard_map/ppermute | solution.py:49
  36.2 47.5 %copy-start.24 = (bf16[8,256,128]{2,1,0:T(8,128)(2,1)S(1)}, bf16[8,256,128]{2,1,0:T(8,128)(2,1)}, u32[]{:S(2)}) copy-start(bf16[8,256,128]{2,1,0:T(8,128)(2,1)} %copy-done.23) | copy-start | bytes 1572868
  36.2 47.5 %copy-start.18 = (f32[8,256]{1,0:T(8,128)S(1)}, f32[8,256]{1,0:T(8,128)}, u32[]{:S(2)}) copy-start(f32[8,256]{1,0:T(8,128)} %refs_8_.1) | copy-start | bytes 24580
  36.3 47.5 %copy-start.19 = (f32[8,256]{1,0:T(8,128)S(1)}, f32[8,256]{1,0:T(8,128)}, u32[]{:S(2)}) copy-start(f32[8,256]{1,0:T(8,128)} %refs_9_.1) | copy-start | bytes 24580
  36.3 47.5 %copy-start.22 = (s32[16]{0:T(128)S(1)}, s32[16]{0:T(128)}, u32[]{:S(2)}) copy-start(s32[16]{0:T(128)} %slot_ref.1) | copy-start | bytes 196
  36.3 8.8 %collective-permute-start.19 = (f32[72,128]{1,0:T(8,128)S(1)}, f32[72,128]{1,0:T(8,128)S(1)}, u32[]{:S(2)}, u32[]{:S(2)}) collective-permute-start(f32[72,128]{1,0:T(8,128)S(1)} %shard_map.195), channel_id=1, source_target_pairs={{0,8},{1,33},{2,10},{3,35},{4,12},{5,37},{6,14},{7,39},{8,0},{9,41... | collective-permute-start | bytes 110600 | tf_op jit(solution)/shard_map/ppermute | solution.py:447
  36.4 15.0 %collective-permute-start.20 = (f32[72,128]{1,0:T(8,128)S(1)}, f32[72,128]{1,0:T(8,128)S(1)}, u32[]{:S(2)}, u32[]{:S(2)}) collective-permute-start(f32[72,128]{1,0:T(8,128)S(1)} %shard_map.195), channel_id=1, source_target_pairs={{0,16},{1,41},{2,18},{3,43},{4,20},{5,45},{6,22},{7,47},{8,24},{9,... | collective-permute-start | bytes 110600 | tf_op jit(solution)/shard_map/ppermute | solution.py:447
  38.8 12.5 %collective-permute-start.21 = (f32[72,128]{1,0:T(8,128)S(1)}, f32[72,128]{1,0:T(8,128)S(1)}, u32[]{:S(2)}, u32[]{:S(2)}) collective-permute-start(f32[72,128]{1,0:T(8,128)S(1)} %shard_map.195), channel_id=1, source_target_pairs={{0,24},{1,49},{2,26},{3,51},{4,28},{5,53},{6,30},{7,55},{8,16},{9,... | collective-permute-start | bytes 110600 | tf_op jit(solution)/shard_map/ppermute | solution.py:447
  40.8 10.6 %collective-permute-start.22 = (f32[72,128]{1,0:T(8,128)S(1)}, f32[72,128]{1,0:T(8,128)S(1)}, u32[]{:S(2)}, u32[]{:S(2)}) collective-permute-start(f32[72,128]{1,0:T(8,128)S(1)} %shard_map.195), channel_id=1, source_target_pairs={{1,57},{3,59},{5,61},{7,63},{9,49},{11,51},{13,53},{15,55},{17,41}... | collective-permute-start | bytes 110600 | tf_op jit(solution)/shard_map/ppermute | solution.py:450
  41.4 32.8 %collective-permute-start.9 = (bf16[8,128,256]{2,1,0:T(8,128)(2,1)S(1)}, bf16[8,128,256]{2,1,0:T(8,128)(2,1)S(1)}, u32[]{:S(2)}, u32[]{:S(2)}) collective-permute-start(bf16[8,128,256]{2,1,0:T(8,128)(2,1)S(1)} %collective-permute-done.7.refs_1_.refs_3_), channel_id=1, source_target_pairs={{0,8},{1,57},{2,10},{3,59},{4,12},{5,61},{6,14},{7,63},{8,16},{9,1... | collective-permute-start | bytes 1572872 | tf_op jit(solution)/shard_map/ppermute | solution.py:504
  45.1 41.0 %collective-permute-start.29 = (bf16[8,256,128]{2,1,0:T(8,128)(2,1)S(1)}, bf16[8,256,128]{2,1,0:T(8,128)(2,1)S(1)}, u32[]{:S(2)}, u32[]{:S(2)}) collective-permute-start(bf16[8,256,128]{2,1,0:T(8,128)(2,1)S(1)} %copy-done.26), channel_id=1, source_target_pairs={{0,1},{1,0},{2,3},{3,2},{4,5},{5,4},{6,7},{7,6},{8,9},{9,8},{10,11... | collective-permute-start | bytes 1572872 | tf_op jit(solution)/shard_map/ppermute | solution.py:49
  51.4 35.2 %collective-permute-start.30 = (bf16[8,256,128]{2,1,0:T(8,128)(2,1)S(1)}, bf16[8,256,128]{2,1,0:T(8,128)(2,1)S(1)}, u32[]{:S(2)}, u32[]{:S(2)}) collective-permute-start(bf16[8,256,128]{2,1,0:T(8,128)(2,1)S(1)} %get-tuple-element.50), channel_id=1, source_target_pairs={{0,2},{1,7},{2,4},{3,1},{4,6},{5,3},{6,0},{7,5},{8,10},{9,15},{10,... | collective-permute-start | bytes 1572872 | tf_op jit(solution)/shard_map/ppermute | solution.py:513
  51.4 1.9 %collective-permute-start.23 = (f32[72,128]{1,0:T(8,128)S(1)}, f32[72,128]{1,0:T(8,128)S(1)}, u32[]{:S(2)}, u32[]{:S(2)}) collective-permute-start(f32[72,128]{1,0:T(8,128)S(1)} %add_select_fusion.a_ref), channel_id=1, source_target_pairs={{0,1},{1,0},{2,3},{3,2},{4,5},{5,4},{6,7},{7,6},{8,9},{9,8},{10,11... | collective-permute-start | bytes 110600 | tf_op jit(solution)/shard_map/ppermute | solution.py:49
  52.0 47.6 %collective-permute-start.27 = (bf16[8,256,128]{2,1,0:T(8,128)(2,1)S(1)}, bf16[8,256,128]{2,1,0:T(8,128)(2,1)S(1)}, u32[]{:S(2)}, u32[]{:S(2)}) collective-permute-start(bf16[8,256,128]{2,1,0:T(8,128)(2,1)S(1)} %get-tuple-element.48), channel_id=1, source_target_pairs={{0,2},{1,7},{2,4},{3,1},{4,6},{5,3},{6,0},{7,5},{8,10},{9,15},{10,... | collective-permute-start | bytes 1572872 | tf_op jit(solution)/shard_map/ppermute | solution.py:514
  53.3 3.9 %collective-permute-start.39 = (bf16[80,128]{1,0:T(8,128)(2,1)S(1)}, bf16[80,128]{1,0:T(8,128)(2,1)S(1)}, u32[]{:S(2)}, u32[]{:S(2)}) collective-permute-start(bf16[80,128]{1,0:T(8,128)(2,1)S(1)} %get-tuple-element.43.small_ref.refs_0_), channel_id=1, source_target_pairs={{0,64},{64,128},{128,192},{192,0},{1,65},{65,129},{129,193},{193,1... | collective-permute-start | bytes 61448 | tf_op jit(solution)/shard_map/ppermute | solution.py:525
  57.2 3.8 %collective-permute-start.40 = (bf16[80,128]{1,0:T(8,128)(2,1)S(1)}, bf16[80,128]{1,0:T(8,128)(2,1)S(1)}, u32[]{:S(2)}, u32[]{:S(2)}) collective-permute-start(bf16[80,128]{1,0:T(8,128)(2,1)S(1)} %get-tuple-element.43.small_ref.refs_0_), channel_id=1, source_target_pairs={{0,192},{64,0},{128,64},{192,128},{1,193},{65,1},{129,65},{193,129... | collective-permute-start | bytes 61448 | tf_op jit(solution)/shard_map/ppermute | solution.py:525
  61.0 5.3 %collective-permute-start.41 = (bf16[80,128]{1,0:T(8,128)(2,1)S(1)}, bf16[80,128]{1,0:T(8,128)(2,1)S(1)}, u32[]{:S(2)}, u32[]{:S(2)}) collective-permute-start(bf16[80,128]{1,0:T(8,128)(2,1)S(1)} %get-tuple-element.43.small_ref.refs_0_), channel_id=1, source_target_pairs={{0,128},{64,192},{128,0},{192,64},{1,129},{65,193},{129,1},{193,65... | collective-permute-start | bytes 61448 | tf_op jit(solution)/shard_map/ppermute | solution.py:525
  66.3 5.0 %collective-permute-start.42 = (bf16[2,128,256]{2,1,0:T(8,128)(2,1)S(1)}, bf16[2,128,256]{2,1,0:T(8,128)(2,1)S(1)}, u32[]{:S(2)}, u32[]{:S(2)}) collective-permute-start(bf16[2,128,256]{2,1,0:T(8,128)(2,1)S(1)} %get-tuple-element.60.refs_4_), channel_id=1, source_target_pairs={{0,64},{64,128},{128,192},{192,0},{1,65},{65,129},{129,193},{193,1... | collective-permute-start | bytes 393224 | tf_op jit(solution)/shard_map/ppermute | solution.py:522
  71.3 5.5 %collective-permute-start.43 = (bf16[2,128,256]{2,1,0:T(8,128)(2,1)S(1)}, bf16[2,128,256]{2,1,0:T(8,128)(2,1)S(1)}, u32[]{:S(2)}, u32[]{:S(2)}) collective-permute-start(bf16[2,128,256]{2,1,0:T(8,128)(2,1)S(1)} %get-tuple-element.60.refs_4_), channel_id=1, source_target_pairs={{0,192},{64,0},{128,64},{192,128},{1,193},{65,1},{129,65},{193,129... | collective-permute-start | bytes 393224 | tf_op jit(solution)/shard_map/ppermute | solution.py:522
  74.2 53.1 %collective-permute-start.11 = (bf16[8,128,256]{2,1,0:T(8,128)(2,1)S(1)}, bf16[8,128,256]{2,1,0:T(8,128)(2,1)S(1)}, u32[]{:S(2)}, u32[]{:S(2)}) collective-permute-start(bf16[8,128,256]{2,1,0:T(8,128)(2,1)S(1)} %collective-permute-done.9.refs_1_.refs_0_), channel_id=1, source_target_pairs={{0,8},{1,57},{2,10},{3,59},{4,12},{5,61},{6,14},{7,63},{8,16},{9,1... | collective-permute-start | bytes 1572872 | tf_op jit(solution)/shard_map/ppermute | solution.py:506
  76.7 7.0 %collective-permute-start.44 = (bf16[2,128,256]{2,1,0:T(8,128)(2,1)S(1)}, bf16[2,128,256]{2,1,0:T(8,128)(2,1)S(1)}, u32[]{:S(2)}, u32[]{:S(2)}) collective-permute-start(bf16[2,128,256]{2,1,0:T(8,128)(2,1)S(1)} %get-tuple-element.60.refs_4_), channel_id=1, source_target_pairs={{0,128},{64,192},{128,0},{192,64},{1,129},{65,193},{129,1},{193,65... | collective-permute-start | bytes 393224 | tf_op jit(solution)/shard_map/ppermute | solution.py:522
  83.7 43.6 %collective-permute-start.24 = (bf16[8,256,128]{2,1,0:T(8,128)(2,1)S(1)}, bf16[8,256,128]{2,1,0:T(8,128)(2,1)S(1)}, u32[]{:S(2)}, u32[]{:S(2)}) collective-permute-start(bf16[8,256,128]{2,1,0:T(8,128)(2,1)S(1)} %copy-done.24), channel_id=1, source_target_pairs={{0,1},{1,0},{2,3},{3,2},{4,5},{5,4},{6,7},{7,6},{8,9},{9,8},{10,11... | collective-permute-start | bytes 1572872 | tf_op jit(solution)/shard_map/ppermute | solution.py:49
  86.1 13.5 %copy-start.4 = (f32[256,256]{1,0:T(8,128)}, f32[256,256]{1,0:T(8,128)S(1)}, u32[]{:S(2)}) copy-start(f32[256,256]{1,0:T(8,128)S(1)} %get-tuple-element.62.ga_ref) | copy-start | bytes 786436
  86.1 74.5 %copy-start.27 = (f32[8,32]{1,0:T(8,128)S(1)}, f32[8,32]{1,0:T(8,128)}, u32[]{:S(2)}) copy-start(f32[8,32]{1,0:T(8,128)} %param.23) | copy-start | bytes 3076
  86.1 6.0 %collective-permute-start.45 = (f32[8,256]{1,0:T(8,128)S(1)}, f32[8,256]{1,0:T(8,128)S(1)}, u32[]{:S(2)}, u32[]{:S(2)}) collective-permute-start(f32[8,256]{1,0:T(8,128)S(1)} %get-tuple-element.61), channel_id=1, source_target_pairs={{0,1},{1,0},{2,3},{3,2},{4,5},{5,4},{6,7},{7,6},{8,9},{9,8},{10,11... | collective-permute-start | bytes 24584 | tf_op jit(solution)/shard_map/ppermute | solution.py:49
  89.8 40.5 %collective-permute-start.31 = (bf16[8,256,128]{2,1,0:T(8,128)(2,1)S(1)}, bf16[8,256,128]{2,1,0:T(8,128)(2,1)S(1)}, u32[]{:S(2)}, u32[]{:S(2)}) collective-permute-start(bf16[8,256,128]{2,1,0:T(8,128)(2,1)S(1)} %shard_map.200), channel_id=1, source_target_pairs={{0,2},{1,7},{2,4},{3,1},{4,6},{5,3},{6,0},{7,5},{8,10},{9,15},{10,... | collective-permute-start | bytes 1572872 | tf_op jit(solution)/shard_map/ppermute | solution.py:516
  92.1 6.9 %collective-permute-start.46 = (f32[8,256]{1,0:T(8,128)S(1)}, f32[8,256]{1,0:T(8,128)S(1)}, u32[]{:S(2)}, u32[]{:S(2)}) collective-permute-start(f32[8,256]{1,0:T(8,128)S(1)} %add.145), channel_id=1, source_target_pairs={{0,2},{1,5},{2,0},{3,7},{4,6},{5,1},{6,4},{7,3},{8,10},{9,13},{10,... | collective-permute-start | bytes 24584 | tf_op jit(solution)/shard_map/ppermute | solution.py:442
  99.0 4.1 %collective-permute-start.47 = (f32[8,256]{1,0:T(8,128)S(1)}, f32[8,256]{1,0:T(8,128)S(1)}, u32[]{:S(2)}, u32[]{:S(2)}) collective-permute-start(f32[8,256]{1,0:T(8,128)S(1)} %add.145), channel_id=1, source_target_pairs={{1,7},{3,5},{5,3},{7,1},{9,15},{11,13},{13,11},{15,9},{17,23},{19,... | collective-permute-start | bytes 24584 | tf_op jit(solution)/shard_map/ppermute | solution.py:443
  99.6 30.7 %collective-permute-start.28 = (bf16[8,256,128]{2,1,0:T(8,128)(2,1)S(1)}, bf16[8,256,128]{2,1,0:T(8,128)(2,1)S(1)}, u32[]{:S(2)}, u32[]{:S(2)}) collective-permute-start(bf16[8,256,128]{2,1,0:T(8,128)(2,1)S(1)} %collective-permute-done.27), channel_id=1, source_target_pairs={{0,1},{1,0},{2,3},{3,2},{4,5},{5,4},{6,7},{7,6},{8,9},{9,8},{10,11... | collective-permute-start | bytes 1572872 | tf_op jit(solution)/shard_map/ppermute | solution.py:49
  103.1 1.7 collective-permute-start.48
  104.8 3.7 %collective-permute-start.49 = (f32[8,256]{1,0:T(8,128)S(1)}, f32[8,256]{1,0:T(8,128)S(1)}, u32[]{:S(2)}, u32[]{:S(2)}) collective-permute-start(f32[8,256]{1,0:T(8,128)S(1)} %shard_map.204), channel_id=1, source_target_pairs={{0,8},{1,33},{2,10},{3,35},{4,12},{5,37},{6,14},{7,39},{8,0},{9,41... | collective-permute-start | bytes 24584 | tf_op jit(solution)/shard_map/ppermute | solution.py:447
  108.5 4.5 %collective-permute-start.50 = (f32[8,256]{1,0:T(8,128)S(1)}, f32[8,256]{1,0:T(8,128)S(1)}, u32[]{:S(2)}, u32[]{:S(2)}) collective-permute-start(f32[8,256]{1,0:T(8,128)S(1)} %shard_map.204), channel_id=1, source_target_pairs={{0,16},{1,41},{2,18},{3,43},{4,20},{5,45},{6,22},{7,47},{8,24},{9,... | collective-permute-start | bytes 24584 | tf_op jit(solution)/shard_map/ppermute | solution.py:447
  113.0 5.4 %collective-permute-start.51 = (f32[8,256]{1,0:T(8,128)S(1)}, f32[8,256]{1,0:T(8,128)S(1)}, u32[]{:S(2)}, u32[]{:S(2)}) collective-permute-start(f32[8,256]{1,0:T(8,128)S(1)} %shard_map.204), channel_id=1, source_target_pairs={{0,24},{1,49},{2,26},{3,51},{4,28},{5,53},{6,30},{7,55},{8,16},{9,... | collective-permute-start | bytes 24584 | tf_op jit(solution)/shard_map/ppermute | solution.py:447
  118.5 0.7 collective-permute-start.52
  119.2 17.3 %collective-permute-start.8 = (bf16[8,128,256]{2,1,0:T(8,128)(2,1)S(1)}, bf16[8,128,256]{2,1,0:T(8,128)(2,1)S(1)}, u32[]{:S(2)}, u32[]{:S(2)}) collective-permute-start(bf16[8,128,256]{2,1,0:T(8,128)(2,1)S(1)} %collective-permute-done.7.refs_1_.refs_3_), channel_id=1, source_target_pairs={{0,1},{1,0},{2,3},{3,2},{4,5},{5,4},{6,7},{7,6},{8,9},{9,8},{10,11... | collective-permute-start | bytes 1572872 | tf_op jit(solution)/shard_map/ppermute | solution.py:49
  127.3 49.8 %collective-permute-start.10 = (bf16[8,128,256]{2,1,0:T(8,128)(2,1)S(1)}, bf16[8,128,256]{2,1,0:T(8,128)(2,1)S(1)}, u32[]{:S(2)}, u32[]{:S(2)}) collective-permute-start(bf16[8,128,256]{2,1,0:T(8,128)(2,1)S(1)} %collective-permute-done.9.refs_1_.refs_0_), channel_id=1, source_target_pairs={{0,1},{1,0},{2,3},{3,2},{4,5},{5,4},{6,7},{7,6},{8,9},{9,8},{10,11... | collective-permute-start | bytes 1572872 | tf_op jit(solution)/shard_map/ppermute | solution.py:49
  127.4 9.0 %collective-permute-start.13 = (bf16[4,128,256]{2,1,0:T(8,128)(2,1)S(1)}, bf16[4,128,256]{2,1,0:T(8,128)(2,1)}, u32[]{:S(2)}, u32[]{:S(2)}) collective-permute-start(bf16[4,128,256]{2,1,0:T(8,128)(2,1)S(1)} %slice_select_fusion), channel_id=1, source_target_pairs={{0,8},{1,57},{2,10},{3,59},{4,12},{5,61},{6,14},{7,63},{8,16},{9,1... | collective-permute-start | bytes 786440 | tf_op jit(solution)/shard_map/ppermute | solution.py:509
  130.3 50.3 %collective-permute-start.12 = (bf16[8,128,256]{2,1,0:T(8,128)(2,1)S(1)}, bf16[8,128,256]{2,1,0:T(8,128)(2,1)}, u32[]{:S(2)}, u32[]{:S(2)}) collective-permute-start(bf16[8,128,256]{2,1,0:T(8,128)(2,1)S(1)} %collective-permute-done.11.refs_1_), channel_id=1, source_target_pairs={{0,1},{1,0},{2,3},{3,2},{4,5},{5,4},{6,7},{7,6},{8,9},{9,8},{10,11... | collective-permute-start | bytes 1572872 | tf_op jit(solution)/shard_map/ppermute | solution.py:49
  130.3 34.2 %copy-start.20 = (f32[8,256]{1,0:T(8,128)S(1)}, f32[8,256]{1,0:T(8,128)}, u32[]{:S(2)}) copy-start(f32[8,256]{1,0:T(8,128)} %get-tuple-element.35.row_ref) | copy-start | bytes 24580
  130.3 34.2 %copy-start.21 = (f32[8,256]{1,0:T(8,128)S(1)}, f32[8,256]{1,0:T(8,128)}, u32[]{:S(2)}) copy-start(f32[8,256]{1,0:T(8,128)} %get-tuple-element.38.col_ref) | copy-start | bytes 24580
  130.3 3.4 %collective-permute-start.53 = (f32[8,256]{1,0:T(8,128)S(1)}, f32[8,256]{1,0:T(8,128)S(1)}, u32[]{:S(2)}, u32[]{:S(2)}) collective-permute-start(f32[8,256]{1,0:T(8,128)S(1)} %add_select_fusion.2.p_ref), channel_id=1, source_target_pairs={{0,1},{1,0},{2,3},{3,2},{4,5},{5,4},{6,7},{7,6},{8,9},{9,8},{10,11... | collective-permute-start | bytes 24584 | tf_op jit(solution)/shard_map/ppermute | solution.py:49
  133.7 9.0 %collective-permute-start.32 = (bf16[256,128]{1,0:T(8,128)(2,1)S(1)}, bf16[256,128]{1,0:T(8,128)(2,1)S(1)}, u32[]{:S(2)}, u32[]{:S(2)}) collective-permute-start(bf16[256,128]{1,0:T(8,128)(2,1)S(1)} %get-tuple-element.52), channel_id=1, source_target_pairs={{0,32},{8,40},{16,48},{24,56},{32,0},{40,8},{48,16},{56,24},{1,33}... | collective-permute-start | bytes 196616 | tf_op jit(solution)/shard_map/ppermute | solution.py:519
  136.4 47.7 %collective-permute-start.14 = (bf16[4,128,256]{2,1,0:T(8,128)(2,1)}, bf16[4,128,256]{2,1,0:T(8,128)(2,1)}, u32[]{:S(2)}, u32[]{:S(2)}) collective-permute-start(bf16[4,128,256]{2,1,0:T(8,128)(2,1)} %collective-permute-done.13.a_ref), channel_id=1, source_target_pairs={{0,1},{1,0},{2,3},{3,2},{4,5},{5,4},{6,7},{7,6},{8,9},{9,8},{10,11... | collective-permute-start | bytes 786440 | tf_op jit(solution)/shard_map/ppermute | solution.py:49
  137.2 9.5 %collective-permute-start.33 = (bf16[256,128]{1,0:T(8,128)(2,1)S(1)}, bf16[256,128]{1,0:T(8,128)(2,1)S(1)}, u32[]{:S(2)}, u32[]{:S(2)}) collective-permute-start(bf16[256,128]{1,0:T(8,128)(2,1)S(1)} %get-tuple-element.53), channel_id=1, source_target_pairs={{0,24},{8,32},{16,40},{24,48},{32,56},{40,0},{48,8},{56,16},{1,25}... | collective-permute-start | bytes 196616 | tf_op jit(solution)/shard_map/ppermute | solution.py:519
  142.7 6.7 %collective-permute-start.34 = (bf16[256,128]{1,0:T(8,128)(2,1)S(1)}, bf16[256,128]{1,0:T(8,128)(2,1)S(1)}, u32[]{:S(2)}, u32[]{:S(2)}) collective-permute-start(bf16[256,128]{1,0:T(8,128)(2,1)S(1)} %get-tuple-element.54), channel_id=1, source_target_pairs={{0,40},{8,48},{16,56},{24,0},{32,8},{40,16},{48,24},{56,32},{1,41}... | collective-permute-start | bytes 196616 | tf_op jit(solution)/shard_map/ppermute | solution.py:519
  146.8 7.8 %collective-permute-start.35 = (bf16[256,128]{1,0:T(8,128)(2,1)S(1)}, bf16[256,128]{1,0:T(8,128)(2,1)S(1)}, u32[]{:S(2)}, u32[]{:S(2)}) collective-permute-start(bf16[256,128]{1,0:T(8,128)(2,1)S(1)} %get-tuple-element.55), channel_id=1, source_target_pairs={{0,16},{8,24},{16,32},{24,40},{32,48},{40,56},{48,0},{56,8},{1,17}... | collective-permute-start | bytes 196616 | tf_op jit(solution)/shard_map/ppermute | solution.py:519
  150.1 6.8 %collective-permute-start.36 = (bf16[256,128]{1,0:T(8,128)(2,1)S(1)}, bf16[256,128]{1,0:T(8,128)(2,1)S(1)}, u32[]{:S(2)}, u32[]{:S(2)}) collective-permute-start(bf16[256,128]{1,0:T(8,128)(2,1)S(1)} %get-tuple-element.56), channel_id=1, source_target_pairs={{0,48},{8,56},{16,0},{24,8},{32,16},{40,24},{48,32},{56,40},{1,49}... | collective-permute-start | bytes 196616 | tf_op jit(solution)/shard_map/ppermute | solution.py:519
  155.2 20.0 %collective-permute-start.37 = (bf16[256,128]{1,0:T(8,128)(2,1)}, bf16[256,128]{1,0:T(8,128)(2,1)}, u32[]{:S(2)}, u32[]{:S(2)}) collective-permute-start(bf16[256,128]{1,0:T(8,128)(2,1)} %get-tuple-element.57), channel_id=1, source_target_pairs={{0,8},{8,16},{16,24},{24,32},{32,40},{40,48},{48,56},{56,0},{1,9},... | collective-permute-start | bytes 196616 | tf_op jit(solution)/shard_map/ppermute | solution.py:519
  157.6 17.7 %collective-permute-start.38 = (bf16[256,128]{1,0:T(8,128)(2,1)}, bf16[256,128]{1,0:T(8,128)(2,1)}, u32[]{:S(2)}, u32[]{:S(2)}) collective-permute-start(bf16[256,128]{1,0:T(8,128)(2,1)} %get-tuple-element.58), channel_id=1, source_target_pairs={{0,56},{8,0},{16,8},{24,16},{32,24},{40,32},{48,40},{56,48},{1,57}... | collective-permute-start | bytes 196616 | tf_op jit(solution)/shard_map/ppermute | solution.py:519
  (18 other events, 55.0 us)
where the time goes:
time: 189 us; the launch traced here: 187 us
  starting transfers between devices  85.5 us (45%)
  waiting for transfers between devices  49.4 us (26%)
  Pallas kernels  36.6 us (19%)
  local copies, waits for them, and re-layouts  12.4 us (7%)
    ppermute x19, starting transfers between devices, swap(): return lax.ppermute(v, 'core', turn(NC, 1))  28.6 us
    ppermute x7, starting transfers between devices, on_device(): lax.ppermute(reduced[k], 'z', turn(NZ, k))  16.6 us
    pallas_call x4, Pallas kernels, frozen_kernel(): pl.pallas_call(functools.partial(frozen_body, n, has_acc), grid_spec=pltp...  13.6 us
    pallas_call x3, Pallas kernels, part_kernel(): pl.pallas_call(functools.partial(part_body, [len(a) for a in adds]), grid...  11.8 us
    ppermute x6, waiting for transfers between devices, all_sum(): lax.ppermute(v, F, plane_moves(lambda z, y, c: (z ^ k + 3 * c, y, c)))  11.4 us
    unnamed x56, local copies, waits for them, and re-layouts  8.92 us
    ppermute x2, waiting for transfers between devices, all_sum(): a = lax.ppermute(v, F, plane_moves(lambda z, y, c: (z, y ^ 1 + c, c)))  8.82 us
    ppermute x3, starting transfers between devices, on_device(): boths = [both] + [lax.ppermute(both, 'dp', turn(NX, k)) for k in (1, 3, 2)]  8.48 us
  transfers between devices with their start and end apart: 54, of which 21 were waited for; matrix products, arithmetic and copies ran while one was open for 2% of the time, Pallas kernels for 18%

commit v1 on v0

v1 whole, which is shorter than its diff:
```python
import functools

import jax
import jax.numpy as jnp
from jax import lax
from jax.experimental import pallas as pl
from jax.experimental.pallas import tpu as pltpu
from jax.sharding import Mesh, PartitionSpec as P

ADAPTER_SCALE = 0.5
BETA_TWO = 0.9
SQ_EPS = 1e-30
RMS_EPS = 1e-05
NX, NZ, NY, NC = 4, 8, 4, 2
F = ("z", "y", "core")
bf16, f32, i32 = jnp.bfloat16, jnp.float32, jnp.int32
NT = (((1,), (1,)), ((), ()))
NN = (((1,), (0,)), ((), ()))
TN = (((0,), (0,)), ((), ()))
ROWS, WIDTH, FULL, TENANTS, RANK, OWNED = 128, 256, 16384, 16, 32, 8
HBM = pl.BlockSpec(memory_space=pl.ANY)
VMEM = pl.BlockSpec(memory_space=pltpu.VMEM)
SMEM = pl.BlockSpec(memory_space=pltpu.SMEM)


def plane_moves(rule):
    pairs = []
    for z in range(NZ):
        for y in range(NY):
            for c in range(NC):
                to = rule(z, y, c)
                if to is not None:
                    z2, y2, c2 = to
                    pairs.append(
                        ((z * NY + y) * NC + c, ((z2 % NZ) * NY + y2 % NY) * NC + c2)
                    )
    return pairs


Z_BY_CORE = plane_moves(lambda z, y, c: (z + 1 - 2 * c, y, c))
Y_BY_CORE = plane_moves(lambda z, y, c: (z, y + 1 - 2 * c, c))


def turn(n, k):
    return [(i, (i + k) % n) for i in range(n)]


def swap(v):
    return lax.ppermute(v, "core", turn(NC, 1))


def like(shape, dtype):
    return jax.ShapeDtypeStruct(shape, dtype)


def tile_of(v):
    return pl.BlockSpec(v.shape, lambda *_, n=v.ndim: (0,) * n)


def whole(shape):
    return pl.BlockSpec(shape, lambda *_, n=len(shape): (0,) * n)


def params(n=48):
    return pltpu.CompilerParams(vmem_limit_bytes=n * 1024 * 1024)


def cost(flops, moved):
    return pl.CostEstimate(flops=flops, bytes_accessed=moved, transcendentals=0)


def dot(a, b, dims=NN):
    return lax.dot_general(a, b, dims, preferred_element_type=f32)


def column_to_rows(v):
    return jnp.broadcast_to(v, (v.shape[0], 128)).T


def row_to_columns(v):
    return jnp.broadcast_to(v, (128, v.shape[1])).T


def split_store(ref, at, v):
    n = v.shape[0]
    high = v.astype(bf16)
    ref[at : at + n] = high
    ref[at + n : at + 2 * n] = (v - high.astype(f32)).astype(bf16)


def split_load(ref, at, n):
    return ref[at : at + n].astype(f32) + ref[at + n : at + 2 * n].astype(f32)


PACKED = 2 * RANK + 16
MESSAGE = 2 * ROWS + 2 * PACKED


def rows_body(live_ref, x_ref, gain_ref, cot_ref, down_ref, up_ref, tenant_ref, message_ref, both_ref, turned_ref):
    x = x_ref[...].astype(f32)
    gained = (x * gain_ref[...].astype(f32)[None, :]).astype(bf16)
    at = lax.broadcasted_iota(i32, (ROWS, WIDTH), 0)
    grad = jnp.where(at < live_ref[0], cot_ref[...].astype(f32), 0.0)
    turned_ref[...] = grad.T.astype(bf16)
    grad = grad.astype(bf16)
    for k in range(NX):
        both_ref[k, 0] = gained
        both_ref[k, 1] = grad
    message_ref[:ROWS] = gained[:, :128]
    message_ref[ROWS : 2 * ROWS] = gained[:, 128:]
    tenant = tenant_ref[...]
    parts = []
    for w_ref, v in ((down_ref, gained), (up_ref, grad)):
        every = dot(w_ref[...], v, NT)
        picked = jnp.zeros((RANK, ROWS), f32)
        for t in range(TENANTS):
            picked = picked + jnp.where(tenant == t, every[t * RANK : (t + 1) * RANK], 0.0)
        parts.append(picked)
    parts.append(column_to_rows(jnp.sum(x * x, axis=1, keepdims=True))[:16])
    split_store(message_ref, 2 * ROWS, jnp.concatenate(parts))


def rows_kernel(live, x, gain, cot, down, up, tenant):
    return pl.pallas_call(
        rows_body,
        grid=(1,),
        in_specs=[SMEM] + [tile_of(v) for v in (x, gain, cot, down, up, tenant)],
        out_specs=[whole((MESSAGE, 128)), whole((NX, 2, ROWS, WIDTH)), whole((WIDTH, ROWS))],
        out_shape=[
            like((MESSAGE, 128), bf16),
            like((NX, 2, ROWS, WIDTH), bf16),
            like((WIDTH, ROWS), bf16),
        ],
        compiler_params=params(60),
        cost_estimate=cost(2**26, 2**20),
    )(live, x, gain, cot, down, up, tenant)


def part_body(counts, spots_ref, turned_ref, *refs):
    n = len(counts)
    refs = list(refs)
    w = [refs.pop(0) for _ in range(n)]
    adds = [[refs.pop(0) for _ in range(k)] for k in counts]
    outs = refs[len(refs) - n :]
    turned = turned_ref[...]
    for i in range(n):
        many = w[i].shape[0]
        total = dot(w[i][...].reshape(many * WIDTH, WIDTH), turned)
        for a in adds[i]:
            total = total + a[...].reshape(many * WIDTH, ROWS).astype(f32)
        outs[i][...] = total.astype(bf16).reshape(many, WIDTH, ROWS)


def part_kernel(w5, turned, spots, first, adds, tokens, tiles=2):
    n = len(adds)
    step = NZ // tiles
    w_specs = [
        pl.BlockSpec(
            (step, 1, 1, WIDTH, WIDTH),
            lambda i, s, k=k: (i, s[2 * (first + k)], s[2 * (first + k) + 1], 0, 0),
        )
        for k in range(n)
    ]
    tile = pl.BlockSpec((step, WIDTH, ROWS), lambda i, s: (i, 0, 0))
    flat = [a for some in adds for a in some]
    return pl.pallas_call(
        functools.partial(part_body, [len(a) for a in adds]),
        grid_spec=pltpu.PrefetchScalarGridSpec(
            num_scalar_prefetch=1,
            grid=(tiles,),
            in_specs=[pl.BlockSpec((WIDTH, ROWS), lambda i, s: (0, 0))]
            + w_specs
            + [tile] * len(flat)
            + [HBM] * len(tokens),
            out_specs=[tile] * n,
        ),
        out_shape=[like((NZ, WIDTH, ROWS), bf16)] * n,
        compiler_params=params(),
        cost_estimate=cost(n * 2**27, n * 2**21),
    )(spots, turned, *([w5] * n), *flat, *tokens)


MOMENTS = 2 * 8
PIECE = WIDTH + 2 * MOMENTS
ORDER = (0, 4, 3, 5, 2, 6, 1, 7)


def last_part_body(offsets, spots_ref, turned_ref, w_ref, a_ref, b_ref, c_ref, p_ref, q_ref, *refs):
    outs = refs[len(refs) - len(offsets) :]
    z = spots_ref[16]
    moments = p_ref[...] + q_ref[...]
    moments = jnp.concatenate([moments[:, :128], moments[:, 128:]])
    for k, out in zip(offsets, outs):
        at = (z + k) % NZ
        t = dot(w_ref[at, 0, 0], turned_ref[...])
        for a in (a_ref, b_ref, c_ref):
            t = t + a[at].astype(f32)
        out[:WIDTH] = t.astype(bf16)
        split_store(out, WIDTH, moments)


def last_part_kernel(w5, turned, spots, at, offsets, adds, moments, tokens):
    flat = pl.BlockSpec((WIDTH, ROWS), lambda i, s: (0, 0))
    wide = pl.BlockSpec((8, OWNED * RANK), lambda i, s: (0, 0))
    out = pl.BlockSpec((PIECE, ROWS), lambda i, s: (0, 0))
    return pl.pallas_call(
        functools.partial(last_part_body, offsets),
        grid_spec=pltpu.PrefetchScalarGridSpec(
            num_scalar_prefetch=1,
            grid=(1,),
            in_specs=[
                flat,
                pl.BlockSpec(
                    (NZ, 1, 1, WIDTH, WIDTH), lambda i, s: (0, s[2 * at], s[2 * at + 1], 0, 0)
                ),
            ]
            + [whole((NZ, WIDTH, ROWS))] * 3
            + [wide] * 2
            + [HBM] * len(tokens),
            out_specs=[out] * len(offsets),
        ),
        out_shape=[like((PIECE, ROWS), bf16)] * len(offsets),
        compiler_params=params(),
        cost_estimate=cost(2**27, 2**21),
    )(spots, turned, w5, *adds, *moments, *tokens)


BLOCK = NY * NC * 2 * ROWS
TAIL = 2 * ROWS


def block_body(spots_ref, *refs):
    own, other = refs[:NY], refs[NY : 2 * NY]
    block_ref, parts_ref = refs[-2:]
    y, core = spots_ref[17], spots_ref[18]
    for j in range(NY):
        at = ((y + j) % NY) * NC
        for spot, ref in ((at + core, own[j]), (at + 1 - core, other[j])):
            block_ref[pl.ds(pl.multiple_of(spot * 2 * ROWS, 2 * ROWS), 2 * ROWS)] = ref[
                : 2 * ROWS
            ]
            parts_ref[spot] = split_load(ref, 2 * ROWS, PACKED)
    total = parts_ref[0]
    for k in range(1, NY * NC):
        total = total + parts_ref[k]
    split_store(block_ref, BLOCK, total)
    block_ref[BLOCK + 2 * PACKED :] = jnp.zeros((TAIL - 2 * PACKED, 128), bf16)


def block_kernel(spots, own, other, *tokens):
    return pl.pallas_call(
        block_body,
        in_specs=[SMEM] + [VMEM] * (2 * NY) + [HBM] * len(tokens),
        out_specs=VMEM,
        out_shape=like((BLOCK + TAIL, 128), bf16),
        scratch_shapes=[pltpu.VMEM((NY * NC, PACKED, ROWS), f32)],
        compiler_params=params(),
    )(spots, *own, *other, *tokens)


def long_dot(x_ref, w_ref):
    many = x_ref.shape[0] // ROWS
    x = jnp.concatenate([x_ref[g * ROWS : (g + 1) * ROWS] for g in range(many)], axis=1)
    return dot(x, w_ref[...].reshape(many * 128, WIDTH))


def frozen_body(n, has_acc, spots_ref, *refs):
    refs = list(refs)
    acc_ref = refs.pop(0) if has_acc else None
    xs, ws, out_ref = refs[:n], refs[n : 2 * n], refs[-1]
    total = None
    for x_ref, w_ref in zip(xs, ws):
        term = long_dot(x_ref, w_ref)
        total = term if total is None else total + term

    @pl.when(pl.program_id(0) == 0)
    def _():
        out_ref[...] = total + acc_ref[...] if has_acc else total

    @pl.when(pl.program_id(0) > 0)
    def _():
        out_ref[...] = out_ref[...] + total


def frozen_kernel(w4, spots, acc, blocks, ats, tokens=(), tiles=2):
    n = len(blocks)
    flat = pl.BlockSpec((ROWS, WIDTH), lambda i, s: (0, 0))
    step = NY * NC // tiles
    has_acc = acc is not None
    return pl.pallas_call(
        functools.partial(frozen_body, n, has_acc),
        grid_spec=pltpu.PrefetchScalarGridSpec(
            num_scalar_prefetch=1,
            grid=(tiles,),
            in_specs=[flat] * has_acc
            + [pl.BlockSpec((step * 2 * ROWS, 128), lambda i, s: (i, 0))] * n
            + [
                pl.BlockSpec((1, step, WIDTH, WIDTH), lambda i, s, a=a: (s[a], i, 0, 0))
                for a in ats
            ]
            + [HBM] * len(tokens),
            out_specs=flat,
        ),
        out_shape=like((ROWS, WIDTH), f32),
        compiler_params=params(),
        cost_estimate=cost(n * 2**27, 9 * 2**20),
    )(spots, *([acc] * has_acc), *blocks, *([w4] * n), *tokens)


def final_body(spots_ref, acc_ref, x_ref, w_ref, scale_ref, small_ref, up_ref, tenant_ref, out_ref):
    total = acc_ref[...] + long_dot(x_ref, w_ref)
    tenant = tenant_ref[...]
    inner = small_ref[0, :RANK].astype(f32)
    spread = jnp.concatenate([jnp.where(tenant == t, inner, 0.0) for t in range(TENANTS)])
    adapted = dot(spread.T.astype(bf16), up_ref[...])
    scale = row_to_columns(scale_ref[:1])[:, :1]
    out_ref[...] = (scale * total + ADAPTER_SCALE * adapted).astype(bf16)


def final_kernel(w4, spots, acc, x, at, scale, small, up, tenant):
    def full(v):
        return pl.BlockSpec(v.shape, lambda i, s, n=v.ndim: (0,) * n)

    return pl.pallas_call(
        final_body,
        grid_spec=pltpu.PrefetchScalarGridSpec(
            num_scalar_prefetch=1,
            grid=(1,),
            in_specs=[
                full(acc),
                pl.BlockSpec((BLOCK, 128), lambda i, s: (0, 0)),
                pl.BlockSpec((1, NY * NC, WIDTH, WIDTH), lambda i, s: (s[at], 0, 0, 0)),
            ]
            + [full(v) for v in (scale, small, up, tenant)],
            out_specs=full(acc),
        ),
        out_shape=like((ROWS, WIDTH), bf16),
        compiler_params=params(),
        cost_estimate=cost(2**28, 9 * 2**20),
    )(spots, acc, x, w4, scale, small, up, tenant)


def gradient_body(*refs):
    pieces, (down_ref, back_ref, tenant_ref), out_ref = refs[:NZ], refs[NZ : NZ + 3], refs[-1]
    total = pieces[0][:WIDTH].astype(f32)
    for p in pieces[1:]:
        total = total + p[:WIDTH].astype(f32)
    tenant = tenant_ref[...]
    back = back_ref[...].astype(f32)
    spread = jnp.concatenate([jnp.where(tenant == t, back, 0.0) for t in range(TENANTS)])
    adapter = dot(down_ref[...].astype(f32).T.astype(bf16), spread.astype(bf16))
    out_ref[...] = (total + ADAPTER_SCALE * adapter).astype(bf16)


def gradient_kernel(pieces, down, back, tenant, *tokens):
    return pl.pallas_call(
        gradient_body,
        grid=(1,),
        in_specs=[VMEM] * NZ + [tile_of(v) for v in (down, back, tenant)] + [HBM] * len(tokens),
        out_specs=VMEM,
        out_shape=like((WIDTH, ROWS), bf16),
        compiler_params=params(),
        cost_estimate=cost(2**25, 2**20),
    )(*pieces, down, back, tenant, *tokens)


def small_body(spots_ref, *refs):
    parts, tenant_ref = refs[:NZ], refs[NZ]
    small_ref, back_ref, scale_ref, all_ref = refs[-4:]
    for at, ref in zip((16, 20, 21, 22, 23, 24, 25, 26), parts):
        all_ref[spots_ref[at]] = split_load(ref, 0, PACKED)
    total = all_ref[0]
    for k in range(1, NZ):
        total = total + all_ref[k]
    scale = lax.rsqrt(total[2 * RANK : 2 * RANK + 1] / FULL + RMS_EPS)
    back = total[RANK : 2 * RANK]
    for k in range(NX):
        small_ref[k, :RANK] = (total[:RANK] * scale).astype(bf16)
        small_ref[k, RANK : 2 * RANK] = (back * scale).astype(bf16)
        small_ref[k, 2 * RANK :] = jnp.broadcast_to(
            tenant_ref[...].astype(f32), (16, ROWS)
        ).astype(bf16)
    back_ref[...] = back.astype(bf16)
    scale_ref[...] = jnp.broadcast_to(scale, (8, ROWS))


def small_kernel(spots, blocks, tenant, *tokens):
    return pl.pallas_call(
        small_body,
        grid=(1,),
        in_specs=[SMEM]
        + [pl.BlockSpec((TAIL, 128), lambda i: (BLOCK // TAIL, 0))] * NZ
        + [tile_of(tenant)]
        + [HBM] * len(tokens),
        out_specs=[whole((NX, 2 * RANK + 16, ROWS)), whole((RANK, ROWS)), whole((8, ROWS))],
        out_shape=[
            like((NX, 2 * RANK + 16, ROWS), bf16),
            like((RANK, ROWS), bf16),
            like((8, ROWS), f32),
        ],
        scratch_shapes=[pltpu.VMEM((NZ, PACKED, ROWS), f32)],
        compiler_params=params(),
    )(spots, *blocks, tenant, *tokens)


def lift(v, size):
    return jnp.broadcast_to(v[:, None, :], (OWNED, RANK, size)).reshape(OWNED * RANK, size)


def slots_body(slot_ref, spots_ref, *refs):
    smalls, boths, row_ref, col_ref = refs[:4]
    ga_ref, gb_ref, row_out, col_out, sum_ref = refs[-5:]
    first = spots_ref[19] * OWNED
    a_rows, b_rows = [], []
    for k in range(NX):
        small_ref = smalls.at[k]
        tenant = small_ref[2 * RANK : 2 * RANK + 16].astype(f32)[:1]
        slot = jnp.full((1, ROWS), -1, i32)
        for t in range(TENANTS):
            slot = jnp.where(tenant == t, slot_ref[t], slot)
        inner = small_ref[:RANK].astype(f32)
        back = small_ref[RANK : 2 * RANK].astype(f32)
        a_rows.append(
            jnp.concatenate([jnp.where(slot == first + s, back, 0.0) for s in range(OWNED)])
        )
        b_rows.append(
            jnp.concatenate([jnp.where(slot == first + s, inner, 0.0) for s in range(OWNED)])
        )
    for rows, at, out_ref in ((a_rows, 0, ga_ref), (b_rows, 1, gb_ref)):
        total = dot(rows[0].astype(bf16), boths[0, at])
        for k in range(1, NX):
            total = total + dot(rows[k].astype(bf16), boths[k, at])
        out_ref[...] = ADAPTER_SCALE * total
    sq_a = ga_ref[...] * ga_ref[...] + SQ_EPS
    sq_b = gb_ref[...] * gb_ref[...] + SQ_EPS
    row_new = BETA_TWO * row_ref[...] + (1.0 - BETA_TWO) * (
        jnp.sum(sq_a.reshape(OWNED, RANK, WIDTH), axis=1) / RANK
    )
    row_out[...] = row_new
    col_out[...] = BETA_TWO * col_ref[...] + (1.0 - BETA_TWO) * (
        jnp.sum(sq_b.reshape(OWNED, RANK, WIDTH), axis=1) / RANK
    )
    lane = lax.broadcasted_iota(i32, (OWNED * RANK, 128), 1)
    columns = [jnp.sum(v, axis=1, keepdims=True) for v in (sq_a, sq_b, lift(row_new, WIDTH))]
    mixed = jnp.where(lane == 0, columns[0], jnp.where(lane == 1, columns[1], columns[2]))
    sum_ref[...] = mixed.T[:8]


def slots_kernel(slot, spots, smalls, boths, row, col, *tokens):
    n = OWNED * RANK
    return pl.pallas_call(
        slots_body,
        grid=(1,),
        in_specs=[SMEM] * 2
        + [tile_of(v) for v in (smalls, boths, row, col)]
        + [HBM] * len(tokens),
        out_specs=[whole((n, WIDTH))] * 2 + [whole((OWNED, WIDTH))] * 2 + [whole((8, n))],
        out_shape=[like((n, WIDTH), f32)] * 2
        + [like((OWNED, WIDTH), f32)] * 2
        + [like((8, n), f32)],
        compiler_params=params(60),
        cost_estimate=cost(2**27, 2**21),
    )(slot, spots, smalls, boths, row, col, *tokens)


def update_body(spots_ref, *refs):
    pieces = refs[:NZ]
    ga_ref, gb_ref, row_ref, col_ref, dcol_ref, urow_ref = refs[NZ : NZ + 6]
    ua_ref, ub_ref, ca_ref, rb_ref, parts_ref = refs[NZ + 6 :]
    z = spots_ref[16]
    for k, ref in zip(ORDER, pieces):
        parts_ref[(z + NZ - k) % NZ] = split_load(ref, WIDTH, MOMENTS)
    total = parts_ref[0]
    for k in range(1, NZ):
        total = total + parts_ref[k]
    total = jnp.concatenate([total[:8], total[8:]], axis=1)
    total = jnp.concatenate([total, jnp.zeros((120, 2 * ROWS), f32)]).T
    same = lax.broadcasted_iota(i32, (OWNED, RANK, RANK), 1) == lax.broadcasted_iota(
        i32, (OWNED, RANK, RANK), 2
    )

    def mixed(old_ref, sums, out_ref):
        old = jnp.where(same, old_ref[...][:, None, :], 0.0)
        old = jnp.sum(old, axis=2, keepdims=True).reshape(OWNED * RANK, 1)
        new = BETA_TWO * old + (1.0 - BETA_TWO) * (sums / FULL)
        back = jnp.broadcast_to(new, (OWNED * RANK, RANK)).reshape(OWNED, RANK, RANK)
        out_ref[...] = jnp.sum(jnp.where(same, back, 0.0), axis=1)
        return new

    col_a = mixed(dcol_ref, total[:, 0:1], ca_ref)
    row_b = mixed(urow_ref, total[:, 1:2], rb_ref)
    mean_a = total[:, 2:3] / FULL
    wide = jnp.broadcast_to(row_b, (OWNED * RANK, 128)).reshape(OWNED, RANK, 128)
    mean_b = lift(jnp.sum(wide, axis=1), 128)[:, :1] / RANK
    ua_ref[...] = ga_ref[...] * lax.rsqrt(lift(row_ref[...], WIDTH) * col_a / mean_a)
    ub_ref[...] = gb_ref[...] * lax.rsqrt(row_b * lift(col_ref[...], WIDTH) / mean_b)


def update_kernel(spots, pieces, ga, gb, row, col, dcol, urow):
    n = OWNED * RANK
    return pl.pallas_call(
        update_body,
        grid=(1,),
        in_specs=[SMEM] + [VMEM] * NZ + [tile_of(v) for v in (ga, gb, row, col, dcol, urow)],
        out_specs=[VMEM] * 4,
        out_shape=[like((n, WIDTH), f32)] * 2 + [like((OWNED, RANK), f32)] * 2,
        scratch_shapes=[pltpu.VMEM((NZ, MOMENTS, 128), f32)],
        compiler_params=params(),
        cost_estimate=cost(2**20, 2**20),
    )(spots, *pieces, ga, gb, row, col, dcol, urow)


def tied_body(*refs):
    pass


def tied(v, *tokens):
    return pl.pallas_call(
        tied_body,
        in_specs=[HBM] * (1 + len(tokens)),
        out_specs=HBM,
        out_shape=like(v.shape, v.dtype),
        input_output_aliases={0: 0},
        compiler_params=params(),
    )(v, *tokens)


def sum_y(v, core):
    v = v + swap(v)
    a = lax.ppermute(v, F, plane_moves(lambda z, y, c: (z, y ^ (1 + c), c)))
    b = lax.ppermute(v, F, plane_moves(lambda z, y, c: (z, y ^ 3, c) if c else None))
    q = jnp.where(core == 0, v + a, a + b)
    return q, swap(q)


def on_device(
    inputs,
    norm_gain_vector,
    weight,
    down_adapters,
    up_adapters,
    tenant,
    tenant_slot_index,
    live_row_count,
    cotangent,
    down_row_factor,
    down_column_factor,
    up_row_factor,
    up_column_factor,
):
    dp = lax.axis_index("dp")
    z, y, core = lax.axis_index("z"), lax.axis_index("y"), lax.axis_index("core")
    opposite = 1 - core
    sign = 1 - 2 * core
    y_two, y_keep, y_send = (y + 2) % NY, (y + 1 + 2 * core) % NY, (y + 3 + 2 * core) % NY
    z_steps = [(z + NZ - s * sign * way) % NZ for s in (1, 2, 3) for way in (1, -1)]
    z_far = (z + NZ // 2) % NZ
    spots = jnp.stack(
        [y_two, opposite, y_send, core, y_send, opposite, y, opposite]
        + [y_two, core, y_keep, opposite, y_keep, core, y, core]
        + [z, y, core, dp]
        + z_steps
        + [z_far]
    ).astype(i32)
    down = down_adapters.transpose(1, 2, 0).reshape(TENANTS * RANK, WIDTH)
    up = up_adapters.reshape(TENANTS * RANK, WIDTH)
    tenant = tenant.reshape(1, ROWS)
    w5 = weight.reshape(NZ, NY, NC, WIDTH, WIDTH)
    w4 = weight.reshape(NZ, NY * NC, WIDTH, WIDTH)

    message, both, turned = rows_kernel(
        live_row_count, inputs, norm_gain_vector, cotangent, down, up, tenant
    )
    s_two, s_far = part_kernel(w5, turned, spots, 0, [[], []], [])
    own = [message] + [lax.ppermute(message, "y", turn(NY, k)) for k in (3, 2, 1)]
    own[1] = tied(own[1], s_two)
    other = [swap(v) for v in own]
    boths = lax.all_to_all(both, "dp", 0, 0, tiled=True)

    block = block_kernel(spots, own, other)
    s_near, s_own = part_kernel(w5, turned, spots, 2, [[], []], [block])
    r_two, r_far, r_near, r_own = [swap(v) for v in (s_two, s_far, s_near, s_own)]
    t_two, t_far = part_kernel(w5, turned, spots, 4, [[r_two], [r_far]], [block])
    g_two = lax.ppermute(t_two, F, Y_BY_CORE)
    g_far = lax.ppermute(t_far, F, Y_BY_CORE)
    frozen_zero = frozen_kernel(w4, spots, None, [block], [16])

    one = tied(lax.ppermute(block, F, Z_BY_CORE), t_far, s_near)
    one_o = swap(one)
    two = lax.ppermute(one, F, Z_BY_CORE)
    (t_near,) = part_kernel(w5, turned, spots, 6, [[r_near, g_two]], [])
    g_near = lax.ppermute(t_near, F, Y_BY_CORE)
    two = tied(two, t_near, frozen_zero, boths)
    two_o = swap(two)
    frozen_one = frozen_kernel(w4, spots, frozen_zero, [one, one_o], [20, 21])
    three = lax.ppermute(two, F, Z_BY_CORE)
    three = tied(three, frozen_one)
    three_o = swap(three)
    frozen_two = frozen_kernel(w4, spots, frozen_one, [two, two_o], [22, 23])
    four = lax.ppermute(three, F, Z_BY_CORE)
    four = tied(four, frozen_two)
    frozen_three = frozen_kernel(w4, spots, frozen_two, [three, three_o], [24, 25])

    small, back, scale = small_kernel(
        spots, [block, one, one_o, two, two_o, three, three_o, four], tenant
    )
    smalls = lax.all_to_all(small, "dp", 0, 0, tiled=True)
    projected = final_kernel(w4, spots, frozen_three, four, 26, scale, small, up, tenant)
    ga, gb, row_a_new, col_b_new, moments = slots_kernel(
        tenant_slot_index,
        spots,
        smalls,
        boths,
        down_row_factor,
        up_column_factor,
        projected,
    )
    moments = sum_y(moments, core)

    adds = [r_own, swap(g_far), g_near]
    first = last_part_kernel(w5, turned, spots, 7, ORDER[1:4], adds, moments, [])
    second = last_part_kernel(
        w5, turned, spots, 7, ORDER[4:] + ORDER[:1], adds, moments, [first[0]]
    )
    pieces = [second[-1]]
    for k, piece in zip(ORDER[1:], first + second[:-1]):
        pieces.append(lax.ppermute(piece, "z", turn(NZ, k)))
    normed_gradient_transposed = gradient_kernel(pieces, down, back, tenant)
    update_a, update_b, col_a_new, row_b_new = update_kernel(
        spots,
        pieces,
        ga,
        gb,
        row_a_new,
        col_b_new,
        down_column_factor,
        up_row_factor,
    )
    return (
        projected,
        normed_gradient_transposed,
        update_a.reshape(OWNED, RANK, WIDTH).swapaxes(1, 2),
        update_b.reshape(OWNED, RANK, WIDTH),
        row_a_new,
        col_a_new,
        row_b_new,
        col_b_new,
    )


def solution(mesh):
    split = Mesh(mesh.devices.reshape(NX, NZ, NY, NC), ("dp",) + F)
    return jax.shard_map(
        on_device,
        mesh=split,
        in_specs=(
            P("dp", F),
            P(F),
            P(None, F),
            P(F, None, None),
            P(None, None, F),
            P("dp"),
            P(),
            P("dp"),
            P("dp", F),
            P("dp", F),
            P("dp", None),
            P("dp", None),
            P("dp", F),
        ),
        out_specs=(
            P("dp", F),
            P(F, "dp"),
            P("dp", F, None),
            P("dp", None, F),
            P("dp", F),
            P("dp", None),
            P("dp", None),
            P("dp", F),
        ),
        check_vma=False,
    )
```

time: 189 us -> 125 us (0.66)
  starting transfers between devices: 85.5 us -> 47.3 us
  waiting for transfers between devices: 49.4 us -> 29.6 us
  local copies, waits for them, and re-layouts: 12.4 us -> 6.65 us
    ppermute x30 -> x14, waiting for transfers between devices: 46.8 us -> 16.5 us  [the longest x1 7.27 us: on_device(): four = lax.ppermute(three, F, Z_BY_CORE)]
    ppermute x30 -> x14, starting transfers between devices: 52.1 us -> 24.7 us  [the longest x7 15.7 us: on_device(): pieces.append(lax.ppermute(piece, 'z', turn(NZ, k)))]
    ppermute x19 -> x14, starting transfers between devices: 28.6 us -> 12.3 us  [swap(): return lax.ppermute(v, 'core', turn(NC, 1))]
    all_to_all x0 -> x2, starting transfers between devices: none -> 9.56 us  [the longest x1 4.84 us: on_device(): boths = lax.all_to_all(both, 'dp', 0, 0, tiled=True)]
    ppermute x1, waiting for transfers between devices: 0.01 us -> 6.12 us  [on_device(): three = lax.ppermute(two, F, Z_BY_CORE)]
    pallas_call x10 -> x13, Pallas kernels: 8.36 us -> 13.2 us  [the longest x2 4.69 us: last_part_kernel(): pl.pallas_call(functools.partial(last_part_body, offsets), grid_spec=pltp...]
    pallas_call x4, Pallas kernels: 13.6 us -> 9.44 us  [frozen_kernel(): pl.pallas_call(functools.partial(frozen_body, n, has_acc), grid_spec=pltp...]
    ppermute x1, waiting for transfers between devices: 0.01 us -> 3.05 us  [on_device(): g_two = lax.ppermute(t_two, F, Y_BY_CORE)]
  transfers between devices with their start and end apart: 54 -> 35, of which waited for: 21 -> 13; matrix products, arithmetic and copies ran while one was open for 2% -> 1% of each run, Pallas kernels for 18% -> 24%
where the time goes in v1:
time: 125 us; the launch traced here: 124 us
  starting transfers between devices  47.3 us (38%)
  Pallas kernels  37.9 us (30%)
  waiting for transfers between devices  29.6 us (24%)
  local copies, waits for them, and re-layouts  6.65 us (5%)
  between operations  1.63 us (1%)
    ppermute x7, starting transfers between devices, on_device(): pieces.append(lax.ppermute(piece, 'z', turn(NZ, k)))  15.7 us
    pallas_call x4, Pallas kernels, part_kernel(): pl.pallas_call(functools.partial(part_body, [len(a) for a in adds]), grid...  12.6 us
    ppermute x14, starting transfers between devices, swap(): return lax.ppermute(v, 'core', turn(NC, 1))  12.3 us
    pallas_call x4, Pallas kernels, frozen_kernel(): pl.pallas_call(functools.partial(frozen_body, n, has_acc), grid_spec=pltp...  9.44 us
    ppermute x1, waiting for transfers between devices, on_device(): four = lax.ppermute(three, F, Z_BY_CORE)  7.27 us
    unnamed x60, local copies, waits for them, and re-layouts  6.55 us
    ppermute x1, waiting for transfers between devices, on_device(): three = lax.ppermute(two, F, Z_BY_CORE)  6.12 us
    ppermute x3, starting transfers between devices, on_device(): lax.ppermute(message, 'y', turn(NY, k))  5.82 us
  transfers between devices with their start and end apart: 35, of which 13 were waited for; matrix products, arithmetic and copies ran while one was open for 1% of the time, Pallas kernels for 24%

profile of v1, /device:TPU:2, one launch (start us, length us, event | category | flops | bytes accessed | tf_op | source)
XLA Modules:
  0.0 123.9 jit_solution(1145785036682670273)
XLA Ops:
  1.3 2.1 %shard_map.188 = (bf16[416,128]{1,0:T(8,128)(2,1)}, bf16[4,2,128,256]{3,2,1,0:T(8,128)(2,1)}, bf16[256,128]{1,0:T(8,128)(2,1)}) custom-call(s32[1]{0:T(128)S(6)} %copy.31.live_ref, bf16[128,256]{1,0:T(8,128)(2,1)} %x_ref.1, bf16[256]{0:T(256)(128)(2,1)} %gain_ref.1, bf16[128,256]{1,0:T(8,128)(2,1)} %cot_ref.1, bf16[512,256]{1,0:T(8,128)(2,1)} %bitcast.28, ...), custom_call_target="tpu_custom_call" | custom-call | flops 67108864 | bytes 1048576 | tf_op jit(solution)/shard_map/pallas_call | solution.py:124
  3.4 1.6 %collective-permute-start.2 = (bf16[416,128]{1,0:T(8,128)(2,1)}, bf16[416,128]{1,0:T(8,128)(2,1)S(1)}, u32[]{:S(2)}, u32[]{:S(2)}) collective-permute-start(bf16[416,128]{1,0:T(8,128)(2,1)} %get-tuple-element.37.refs_0_), channel_id=1, source_target_pairs={{0,2},{2,4},{4,6},{6,0},{1,3},{3,5},{5,7},{7,1},{8,10},{10,12},{12... | collective-permute-start | bytes 319496 | tf_op jit(solution)/shard_map/ppermute | solution.py:575
  5.0 2.9 %collective-permute-start.1 = (bf16[416,128]{1,0:T(8,128)(2,1)}, bf16[416,128]{1,0:T(8,128)(2,1)S(1)}, u32[]{:S(2)}, u32[]{:S(2)}) collective-permute-start(bf16[416,128]{1,0:T(8,128)(2,1)} %get-tuple-element.37.refs_0_), channel_id=1, source_target_pairs={{0,4},{2,6},{4,0},{6,2},{1,5},{3,7},{5,1},{7,3},{8,12},{10,14},{12... | collective-permute-start | bytes 319496 | tf_op jit(solution)/shard_map/ppermute | solution.py:575
  7.9 1.3 %collective-permute-start = (bf16[416,128]{1,0:T(8,128)(2,1)}, bf16[416,128]{1,0:T(8,128)(2,1)S(1)}, u32[]{:S(2)}, u32[]{:S(2)}) collective-permute-start(bf16[416,128]{1,0:T(8,128)(2,1)} %get-tuple-element.37.refs_0_), channel_id=1, source_target_pairs={{0,6},{2,0},{4,2},{6,4},{1,7},{3,1},{5,3},{7,5},{8,14},{10,8},{12,... | collective-permute-start | bytes 319496 | tf_op jit(solution)/shard_map/ppermute | solution.py:575
  9.2 0.1 stack.75.spots_ref
  9.3 0.8 copy-done.1
  10.2 2.7 %shard_map.189 = (bf16[8,256,128]{2,1,0:T(8,128)(2,1)S(1)}, bf16[8,256,128]{2,1,0:T(8,128)(2,1)S(1)}) custom-call(s32[27]{0:T(128)S(1)} %stack.75.spots_ref, bf16[256,128]{1,0:T(8,128)(2,1)S(1)} %copy-done.1, bf16[8,4,2,256,256]{4,3,2,1,0:T(8,128)(2,1)} %bitcast.34, bf16[8,4,2,256,256]{4,3,2,1,0:T(8,128)(2,1)} %bitcast.35), custom_call_target="tpu_custom_call" | custom-call | flops 268435456 | bytes 4194304 | tf_op jit(solution)/shard_map/pallas_call | solution.py:166
  12.9 0.6 collective-permute-start.6
  13.4 0.1 collective-permute-start.5
  13.6 0.4 collective-permute-start.4
  14.0 0.4 collective-permute-done.6.refs_7_
  14.4 0.4 collective-permute-done.5.refs_6_
  14.8 0.2 collective-permute-done.4.refs_5_
  14.9 0.6 shard_map.191.refs_0_.refs_4_.refs_2_
  15.6 2.0 %collective-permute-start.7 = (bf16[2304,128]{1,0:T(8,128)(2,1)S(1)}, bf16[2304,128]{1,0:T(8,128)(2,1)S(1)}, u32[]{:S(2)}, u32[]{:S(2)}) collective-permute-start(bf16[2304,128]{1,0:T(8,128)(2,1)S(1)} %shard_map.191.refs_0_.refs_4_.refs_2_), channel_id=1, source_target_pairs={{0,8},{1,57},{2,10},{3,59},{4,12},{5,61},{6,14},{7,63},{8,16},{9,1... | collective-permute-start | bytes 1769480 | tf_op jit(solution)/shard_map/ppermute | solution.py:588
  17.6 4.0 %collective-permute-start.9 = (bf16[8,256,128]{2,1,0:T(8,128)(2,1)S(1)}, bf16[8,256,128]{2,1,0:T(8,128)(2,1)S(1)}, u32[]{:S(2)}, u32[]{:S(2)}) collective-permute-start(bf16[8,256,128]{2,1,0:T(8,128)(2,1)S(1)} %get-tuple-element.40), channel_id=1, source_target_pairs={{0,1},{1,0},{2,3},{3,2},{4,5},{5,4},{6,7},{7,6},{8,9},{9,8},{10,11... | collective-permute-start | bytes 1572872 | tf_op jit(solution)/shard_map/ppermute | solution.py:49
  21.6 3.5 %shard_map.194 = (bf16[8,256,128]{2,1,0:T(8,128)(2,1)}, bf16[8,256,128]{2,1,0:T(8,128)(2,1)}) custom-call(s32[27]{0:T(128)S(1)} %stack.75.spots_ref, bf16[256,128]{1,0:T(8,128)(2,1)S(1)} %copy-done.2, bf16[8,4,2,256,256]{4,3,2,1,0:T(8,128)(2,1)} %bitcast.36, bf16[8,4,2,256,256]{4,3,2,1,0:T(8,128)(2,1)} %bitcast.37, ...), custom_call_target="tpu_custom_call" | custom-call | flops 268435456 | bytes 4194304 | tf_op jit(solution)/shard_map/pallas_call | solution.py:166
  25.1 3.4 %shard_map.193 = (bf16[8,256,128]{2,1,0:T(8,128)(2,1)}, bf16[8,256,128]{2,1,0:T(8,128)(2,1)S(1)}) custom-call(s32[27]{0:T(128)S(1)} %stack.75.spots_ref, bf16[256,128]{1,0:T(8,128)(2,1)S(1)} %copy-done.2, bf16[8,4,2,256,256]{4,3,2,1,0:T(8,128)(2,1)} %bitcast.38, bf16[8,4,2,256,256]{4,3,2,1,0:T(8,128)(2,1)} %bitcast.39, ...), custom_call_target="tpu_custom_call" | custom-call | flops 268435456 | bytes 4194304 | tf_op jit(solution)/shard_map/pallas_call | solution.py:166
  28.5 0.9 collective-permute-done.7.refs_0_
  29.4 2.2 %collective-permute-start.12 = (bf16[8,256,128]{2,1,0:T(8,128)(2,1)}, bf16[8,256,128]{2,1,0:T(8,128)(2,1)}, u32[]{:S(2)}, u32[]{:S(2)}) collective-permute-start(bf16[8,256,128]{2,1,0:T(8,128)(2,1)} %get-tuple-element.42.refs_2_), channel_id=1, source_target_pairs={{0,1},{1,0},{2,3},{3,2},{4,5},{5,4},{6,7},{7,6},{8,9},{9,8},{10,11... | collective-permute-start | bytes 1572872 | tf_op jit(solution)/shard_map/ppermute | solution.py:49
  31.5 0.7 collective-permute-start.13
  32.2 4.8 %all-to-all-start = ((bf16[4,2,128,256]{3,2,1,0:T(8,128)(2,1)}), bf16[4,2,128,256]{3,2,1,0:T(8,128)(2,1)S(1)}, u32[]{:S(2)}, u32[]{:S(2)}) async-start(bf16[4,2,128,256]{3,2,1,0:T(8,128)(2,1)} %get-tuple-element.44), calls=%async_computation | async-start | bytes 1048576 | tf_op jit(solution)/shard_map/all_to_all | solution.py:578
  37.0 2.1 %shard_map.192.refs_0_.refs_2_ = f32[128,256]{1,0:T(8,128)S(1)} custom-call(s32[27]{0:T(128)S(1)} %stack.75.spots_ref, bf16[2304,128]{1,0:T(8,128)(2,1)S(1)} %shard_map.191.refs_0_.refs_4_.refs_2_, bf16[8,8,256,256]{3,2,1,0:T(8,128)(2,1)} %bitcast.40), custom_call_target="tpu_custom_call" | custom-call | flops 134217728 | bytes 9437184 | tf_op jit(solution)/shard_map/pallas_call | solution.py:290
  39.2 3.1 %collective-permute-done.13.refs_2_ = bf16[8,256,128]{2,1,0:T(8,128)(2,1)} collective-permute-done((bf16[8,256,128]{2,1,0:T(8,128)(2,1)}, bf16[8,256,128]{2,1,0:T(8,128)(2,1)}, u32[]{:S(2)}, u32[]{:S(2)}) %collective-permute-start.13) | collective-permute-done | bytes 524320 | tf_op jit(solution)/shard_map/ppermute | solution.py:584
  42.2 3.1 %shard_map.197.refs_1_ = bf16[8,256,128]{2,1,0:T(8,128)(2,1)} custom-call(s32[27]{0:T(128)S(1)} %stack.75.spots_ref, bf16[256,128]{1,0:T(8,128)(2,1)S(1)} %copy-done.2, bf16[8,4,2,256,256]{4,3,2,1,0:T(8,128)(2,1)} %bitcast.41, bf16[8,256,128]{2,1,0:T(8,128)(2,1)} %collective-permute-done.12.refs_1_, bf16[8,256,128]{2,1,0:T(8,128)(2,1)} %collective-permute-done.13.refs_2_), custom_call_target="tpu_custom_call" | custom-call | flops 134217728 | bytes 2097152 | tf_op jit(solution)/shard_map/pallas_call | solution.py:166
  45.3 0.5 all-to-all-done.refs_3_.refs_1_
  45.9 1.6 %collective-permute-start.14 = (bf16[2304,128]{1,0:T(8,128)(2,1)S(1)}, bf16[2304,128]{1,0:T(8,128)(2,1)S(1)}, u32[]{:S(2)}, u32[]{:S(2)}) collective-permute-start(bf16[2304,128]{1,0:T(8,128)(2,1)S(1)} %shard_map.198.refs_1_.refs_3_), channel_id=1, source_target_pairs={{0,1},{1,0},{2,3},{3,2},{4,5},{5,4},{6,7},{7,6},{8,9},{9,8},{10,11... | collective-permute-start | bytes 1769480 | tf_op jit(solution)/shard_map/ppermute | solution.py:49
  47.5 0.9 copy-done.8
  48.4 2.4 %shard_map.196.refs_0_.refs_1_ = f32[128,256]{1,0:T(8,128)S(1)} custom-call(s32[27]{0:T(128)S(1)} %stack.75.spots_ref, f32[128,256]{1,0:T(8,128)S(1)} %copy-done.8, bf16[2304,128]{1,0:T(8,128)(2,1)S(1)} %shard_map.195.refs_1_, bf16[2304,128]{1,0:T(8,128)(2,1)S(1)} %collective-permute-done.10.refs_2_, bf16[8,8,256,256]{3,2,1,0:T(8,128)(2,1)} %bitcast.42, ...), custom_call_target="tpu_custom_call" | custom-call | flops 268435456 | bytes 9437184 | tf_op jit(solution)/shard_map/pallas_call | solution.py:290
  50.9 6.1 %collective-permute-done.15.refs_0_ = bf16[2304,128]{1,0:T(8,128)(2,1)S(1)} collective-permute-done((bf16[2304,128]{1,0:T(8,128)(2,1)S(1)}, bf16[2304,128]{1,0:T(8,128)(2,1)S(1)}, u32[]{:S(2)}, u32[]{:S(2)}) %collective-permute-start.15) | collective-permute-done | bytes 589856 | tf_op jit(solution)/shard_map/ppermute | solution.py:596
  57.0 0.8 collective-permute-start.16
  57.8 0.4 collective-permute-done.19
  58.2 0.2 collective-permute-start.20
  58.3 2.4 %shard_map.199.refs_0_.refs_1_ = f32[128,256]{1,0:T(8,128)S(1)} custom-call(s32[27]{0:T(128)S(1)} %stack.75.spots_ref, f32[128,256]{1,0:T(8,128)S(1)} %shard_map.196.refs_0_.refs_1_, bf16[2304,128]{1,0:T(8,128)(2,1)S(1)} %shard_map.198.refs_1_.refs_3_, bf16[2304,128]{1,0:T(8,128)(2,1)S(1)} %collective-permute-done.14.refs_2_.refs_4_, ...), custom_call_target="tpu_custom_call" | custom-call | flops 268435456 | bytes 9437184 | tf_op jit(solution)/shard_map/pallas_call | solution.py:290
  60.8 7.3 %collective-permute-done.17.refs_0_ = bf16[2304,128]{1,0:T(8,128)(2,1)S(1)} collective-permute-done((bf16[2304,128]{1,0:T(8,128)(2,1)S(1)}, bf16[2304,128]{1,0:T(8,128)(2,1)S(1)}, u32[]{:S(2)}, u32[]{:S(2)}) %collective-permute-start.17) | collective-permute-done | bytes 589856 | tf_op jit(solution)/shard_map/ppermute | solution.py:600
  68.1 0.6 shard_map.203
  68.7 0.2 copy-done.5
  69.0 0.6 copy-done.14
  69.6 0.6 copy-done.27
  70.2 4.7 %all-to-all-start.1 = ((bf16[4,80,128]{2,1,0:T(8,128)(2,1)}), bf16[4,80,128]{2,1,0:T(8,128)(2,1)S(1)}, u32[]{:S(2)}, u32[]{:S(2)}) async-start(bf16[4,80,128]{2,1,0:T(8,128)(2,1)} %copy-done.14), calls=%async_computation.1 | async-start | bytes 163840 | tf_op jit(solution)/shard_map/all_to_all | solution.py:607
  74.9 1.1 copy-done.6
  76.0 0.9 copy-done.10
  76.9 2.4 %shard_map.201.acc_ref = f32[128,256]{1,0:T(8,128)S(1)} custom-call(s32[27]{0:T(128)S(1)} %stack.75.spots_ref, f32[128,256]{1,0:T(8,128)S(1)} %copy-done.10, bf16[2304,128]{1,0:T(8,128)(2,1)S(1)} %shard_map.200.refs_1_.refs_5_, bf16[2304,128]{1,0:T(8,128)(2,1)S(1)} %copy-done.6, bf16[8,8,256,256]{3,2,1,0:T(8,128)(2,1)} %bitcast.46, ...), custom_call_target="tpu_custom_call" | custom-call | flops 268435456 | bytes 9437184 | tf_op jit(solution)/shard_map/pallas_call | solution.py:290
  79.4 2.7 %shard_map.204.refs_4_ = bf16[128,256]{1,0:T(8,128)(2,1)} custom-call(s32[27]{0:T(128)S(1)} %stack.75.spots_ref, f32[128,256]{1,0:T(8,128)S(1)} %shard_map.201.acc_ref, bf16[2304,128]{1,0:T(8,128)(2,1)S(1)} %shard_map.202.refs_7_.x_ref, bf16[8,8,256,256]{3,2,1,0:T(8,128)(2,1)} %bitcast.48, f32[8,128]{1,0:T(8,128)S(1)} %copy-done.28, ...), custom_call_target="tpu_custom_call" | custom-call | flops 268435456 | bytes 9437184 | tf_op jit(solution)/shard_map/pallas_call | solution.py:324
  82.1 0.6 copy-done.29
  82.8 2.3 %shard_map.205 = (f32[256,256]{1,0:T(8,128)}, f32[256,256]{1,0:T(8,128)}, f32[8,256]{1,0:T(8,128)}, f32[8,256]{1,0:T(8,128)}, f32[8,256]{1,0:T(8,128)}) custom-call(s32[16]{0:T(128)} %slot_ref.1, s32[27]{0:T(128)} %copy-done.18, bf16[4,80,128]{2,1,0:T(8,128)(2,1)} %copy-done.29, bf16[4,2,128,256]{3,2,1,0:T(8,128)(2,1)} %copy-done, f32[8,256]{1,0:T(8,128)} %refs_2_.1, ...), custom_call_target="tpu_custom_call" | custom-call | flops 134217728 | bytes 2097152 | tf_op jit(solution)/shard_map/pallas_call | solution.py:451
  85.1 1.4 %collective-permute-done.22 = f32[8,256]{1,0:T(8,128)S(1)} collective-permute-done((f32[8,256]{1,0:T(8,128)}, f32[8,256]{1,0:T(8,128)S(1)}, u32[]{:S(2)}, u32[]{:S(2)}) %collective-permute-start.22) | collective-permute-done | bytes 8224 | tf_op jit(solution)/shard_map/ppermute | solution.py:49
  86.4 0.7 add.83
  87.1 0.6 collective-permute-start.24
  87.8 0.6 collective-permute-start.23
  88.4 3.1 %collective-permute-done.23 = f32[8,256]{1,0:T(8,128)S(1)} collective-permute-done((f32[8,256]{1,0:T(8,128)S(1)}, f32[8,256]{1,0:T(8,128)S(1)}, u32[]{:S(2)}, u32[]{:S(2)}) %collective-permute-start.23) | collective-permute-done | bytes 8224 | tf_op jit(solution)/shard_map/ppermute | solution.py:530
  91.6 2.4 %collective-permute-start.25 = (f32[8,256]{1,0:T(8,128)S(1)}, f32[8,256]{1,0:T(8,128)S(1)}, u32[]{:S(2)}, u32[]{:S(2)}) collective-permute-start(f32[8,256]{1,0:T(8,128)S(1)} %add_select_fusion.p_ref), channel_id=1, source_target_pairs={{0,1},{1,0},{2,3},{3,2},{4,5},{5,4},{6,7},{7,6},{8,9},{9,8},{10,11... | collective-permute-start | bytes 24584 | tf_op jit(solution)/shard_map/ppermute | solution.py:49
  94.0 0.8 collective-permute-done.25.q_ref
  94.8 0.7 copy-done.19
  95.5 2.3 %shard_map.206 = (bf16[288,128]{1,0:T(8,128)(2,1)S(1)}, bf16[288,128]{1,0:T(8,128)(2,1)S(1)}, bf16[288,128]{1,0:T(8,128)(2,1)S(1)}) custom-call(s32[27]{0:T(128)S(1)} %copy-done.19, bf16[256,128]{1,0:T(8,128)(2,1)S(1)} %copy-done.2, bf16[8,4,2,256,256]{4,3,2,1,0:T(8,128)(2,1)} %bitcast.49, bf16[8,256,128]{2,1,0:T(8,128)(2,1)S(1)} %collective-permute-done.18.a_ref, ...), custom_call_target="tpu_custom_call" | custom-call | flops 134217728 | bytes 2097152 | tf_op jit(solution)/shard_map/pallas_call | solution.py:206
  97.8 1.3 %collective-permute-start.27 = (bf16[288,128]{1,0:T(8,128)(2,1)S(1)}, bf16[288,128]{1,0:T(8,128)(2,1)S(1)}, u32[]{:S(2)}, u32[]{:S(2)}) collective-permute-start(bf16[288,128]{1,0:T(8,128)(2,1)S(1)} %get-tuple-element.51), channel_id=1, source_target_pairs={{0,24},{8,32},{16,40},{24,48},{32,56},{40,0},{48,8},{56,16},{1,25}... | collective-permute-start | bytes 221192 | tf_op jit(solution)/shard_map/ppermute | solution.py:627
  99.2 3.8 %collective-permute-start.28 = (bf16[288,128]{1,0:T(8,128)(2,1)S(1)}, bf16[288,128]{1,0:T(8,128)(2,1)S(1)}, u32[]{:S(2)}, u32[]{:S(2)}) collective-permute-start(bf16[288,128]{1,0:T(8,128)(2,1)S(1)} %get-tuple-element.52), channel_id=1, source_target_pairs={{0,40},{8,48},{16,56},{24,0},{32,8},{40,16},{48,24},{56,32},{1,41}... | collective-permute-start | bytes 221192 | tf_op jit(solution)/shard_map/ppermute | solution.py:627
  102.9 2.4 %shard_map.207 = (bf16[288,128]{1,0:T(8,128)(2,1)S(1)}, bf16[288,128]{1,0:T(8,128)(2,1)S(1)}, bf16[288,128]{1,0:T(8,128)(2,1)S(1)}, bf16[288,128]{1,0:T(8,128)(2,1)S(1)}, bf16[288,128]{1,0:T(8,128)(2,1)S(1)}) custom-call(s32[27]{0:T(128)S(1)} %copy-done.20, bf16[256,128]{1,0:T(8,128)(2,1)S(1)} %copy-done.2, bf16[8,4,2,256,256]{4,3,2,1,0:T(8,128)(2,1)} %bitcast.50, ...), custom_call_target="tpu_custom_call" | custom-call | flops 134217728 | bytes 2097152 | tf_op jit(solution)/shard_map/pallas_call | solution.py:206
  105.4 4.1 %collective-permute-start.30 = (bf16[288,128]{1,0:T(8,128)(2,1)S(1)}, bf16[288,128]{1,0:T(8,128)(2,1)S(1)}, u32[]{:S(2)}, u32[]{:S(2)}) collective-permute-start(bf16[288,128]{1,0:T(8,128)(2,1)S(1)} %get-tuple-element.54), channel_id=1, source_target_pairs={{0,48},{8,56},{16,0},{24,8},{32,16},{40,24},{48,32},{56,40},{1,49}... | collective-permute-start | bytes 221192 | tf_op jit(solution)/shard_map/ppermute | solution.py:627
  109.5 3.2 %collective-permute-start.32 = (bf16[288,128]{1,0:T(8,128)(2,1)S(1)}, bf16[288,128]{1,0:T(8,128)(2,1)S(1)}, u32[]{:S(2)}, u32[]{:S(2)}) collective-permute-start(bf16[288,128]{1,0:T(8,128)(2,1)S(1)} %get-tuple-element.56), channel_id=1, source_target_pairs={{0,56},{8,0},{16,8},{24,16},{32,24},{40,32},{48,40},{56,48},{1,57}... | collective-permute-start | bytes 221192 | tf_op jit(solution)/shard_map/ppermute | solution.py:627
  112.8 3.1 %collective-permute-start.26 = (bf16[288,128]{1,0:T(8,128)(2,1)S(1)}, bf16[288,128]{1,0:T(8,128)(2,1)S(1)}, u32[]{:S(2)}, u32[]{:S(2)}) collective-permute-start(bf16[288,128]{1,0:T(8,128)(2,1)S(1)} %get-tuple-element.49.refs_0_), channel_id=1, source_target_pairs={{0,32},{8,40},{16,48},{24,56},{32,0},{40,8},{48,16},{56,24},{1,33}... | collective-permute-start | bytes 221192 | tf_op jit(solution)/shard_map/ppermute | solution.py:627
  115.9 5.1 %collective-permute-done.26.refs_1_ = bf16[288,128]{1,0:T(8,128)(2,1)S(1)} collective-permute-done((bf16[288,128]{1,0:T(8,128)(2,1)S(1)}, bf16[288,128]{1,0:T(8,128)(2,1)S(1)}, u32[]{:S(2)}, u32[]{:S(2)}) %collective-permute-start.26) | collective-permute-done | bytes 73760 | tf_op jit(solution)/shard_map/ppermute | solution.py:627
  121.0 0.9 shard_map.208
  122.0 1.9 %shard_map.209 = (f32[256,256]{1,0:T(8,128)}, f32[256,256]{1,0:T(8,128)}, f32[8,32]{1,0:T(8,128)}, f32[8,32]{1,0:T(8,128)}) custom-call(s32[27]{0:T(128)S(1)} %copy-done.20, bf16[288,128]{1,0:T(8,128)(2,1)S(1)} %get-tuple-element.50.refs_0_, bf16[288,128]{1,0:T(8,128)(2,1)S(1)} %collective-permute-done.26.refs_1_, ...), custom_call_target="tpu_custom_call" | custom-call | flops 1048576 | bytes 1048576 | tf_op jit(solution)/shard_map/pallas_call | solution.py:501
  (91 shorter events, 0.4 us)
Async XLA Ops:
  3.4 9.5 %collective-permute-start.2 = (bf16[416,128]{1,0:T(8,128)(2,1)}, bf16[416,128]{1,0:T(8,128)(2,1)S(1)}, u32[]{:S(2)}, u32[]{:S(2)}) collective-permute-start(bf16[416,128]{1,0:T(8,128)(2,1)} %get-tuple-element.37.refs_0_), channel_id=1, source_target_pairs={{0,2},{2,4},{4,6},{6,0},{1,3},{3,5},{5,7},{7,1},{8,10},{10,12},{12... | collective-permute-start | bytes 319496 | tf_op jit(solution)/shard_map/ppermute | solution.py:575
  5.0 8.5 %collective-permute-start.1 = (bf16[416,128]{1,0:T(8,128)(2,1)}, bf16[416,128]{1,0:T(8,128)(2,1)S(1)}, u32[]{:S(2)}, u32[]{:S(2)}) collective-permute-start(bf16[416,128]{1,0:T(8,128)(2,1)} %get-tuple-element.37.refs_0_), channel_id=1, source_target_pairs={{0,4},{2,6},{4,0},{6,2},{1,5},{3,7},{5,1},{7,3},{8,12},{10,14},{12... | collective-permute-start | bytes 319496 | tf_op jit(solution)/shard_map/ppermute | solution.py:575
  7.9 5.7 %collective-permute-start = (bf16[416,128]{1,0:T(8,128)(2,1)}, bf16[416,128]{1,0:T(8,128)(2,1)S(1)}, u32[]{:S(2)}, u32[]{:S(2)}) collective-permute-start(bf16[416,128]{1,0:T(8,128)(2,1)} %get-tuple-element.37.refs_0_), channel_id=1, source_target_pairs={{0,6},{2,0},{4,2},{6,4},{1,7},{3,1},{5,3},{7,5},{8,14},{10,8},{12,... | collective-permute-start | bytes 319496 | tf_op jit(solution)/shard_map/ppermute | solution.py:575
  9.2 4.8 %collective-permute-start.3 = (bf16[416,128]{1,0:T(8,128)(2,1)}, bf16[416,128]{1,0:T(8,128)(2,1)S(1)}, u32[]{:S(2)}, u32[]{:S(2)}) collective-permute-start(bf16[416,128]{1,0:T(8,128)(2,1)} %get-tuple-element.37.refs_0_), channel_id=1, source_target_pairs={{0,1},{1,0},{2,3},{3,2},{4,5},{5,4},{6,7},{7,6},{8,9},{9,8},{10,11... | collective-permute-start | bytes 319496 | tf_op jit(solution)/shard_map/ppermute | solution.py:49
  9.3 70.0 %copy-start.18 = (s32[27]{0:T(128)}, s32[27]{0:T(128)S(1)}, u32[]{:S(2)}) copy-start(s32[27]{0:T(128)S(1)} %stack.75.spots_ref) | copy-start | bytes 328
  9.3 0.8 copy-start.1
  10.2 4.7 %copy-start.21 = (bf16[416,128]{1,0:T(8,128)(2,1)S(1)}, bf16[416,128]{1,0:T(8,128)(2,1)}, u32[]{:S(2)}) copy-start(bf16[416,128]{1,0:T(8,128)(2,1)} %get-tuple-element.37.refs_0_) | copy-start | bytes 319492
  10.2 11.4 %copy-start.2 = (bf16[256,128]{1,0:T(8,128)(2,1)S(1)}, bf16[256,128]{1,0:T(8,128)(2,1)}, u32[]{:S(2)}) copy-start(bf16[256,128]{1,0:T(8,128)(2,1)} %get-tuple-element.38.turned_ref) | copy-start | bytes 196612
  12.9 1.5 %collective-permute-start.6 = (bf16[416,128]{1,0:T(8,128)(2,1)S(1)}, bf16[416,128]{1,0:T(8,128)(2,1)S(1)}, u32[]{:S(2)}, u32[]{:S(2)}) collective-permute-start(bf16[416,128]{1,0:T(8,128)(2,1)S(1)} %collective-permute-done.2.refs_3_), channel_id=1, source_target_pairs={{0,1},{1,0},{2,3},{3,2},{4,5},{5,4},{6,7},{7,6},{8,9},{9,8},{10,11... | collective-permute-start | bytes 319496 | tf_op jit(solution)/shard_map/ppermute | solution.py:49
  13.4 1.3 %collective-permute-start.5 = (bf16[416,128]{1,0:T(8,128)(2,1)S(1)}, bf16[416,128]{1,0:T(8,128)(2,1)S(1)}, u32[]{:S(2)}, u32[]{:S(2)}) collective-permute-start(bf16[416,128]{1,0:T(8,128)(2,1)S(1)} %collective-permute-done.1.refs_2_), channel_id=1, source_target_pairs={{0,1},{1,0},{2,3},{3,2},{4,5},{5,4},{6,7},{7,6},{8,9},{9,8},{10,11... | collective-permute-start | bytes 319496 | tf_op jit(solution)/shard_map/ppermute | solution.py:49
  13.6 1.4 %collective-permute-start.4 = (bf16[416,128]{1,0:T(8,128)(2,1)S(1)}, bf16[416,128]{1,0:T(8,128)(2,1)S(1)}, u32[]{:S(2)}, u32[]{:S(2)}) collective-permute-start(bf16[416,128]{1,0:T(8,128)(2,1)S(1)} %shard_map.190.refs_1_), channel_id=1, source_target_pairs={{0,1},{1,0},{2,3},{3,2},{4,5},{5,4},{6,7},{7,6},{8,9},{9,8},{10,11... | collective-permute-start | bytes 319496 | tf_op jit(solution)/shard_map/ppermute | solution.py:49
  15.6 13.8 %collective-permute-start.7 = (bf16[2304,128]{1,0:T(8,128)(2,1)S(1)}, bf16[2304,128]{1,0:T(8,128)(2,1)S(1)}, u32[]{:S(2)}, u32[]{:S(2)}) collective-permute-start(bf16[2304,128]{1,0:T(8,128)(2,1)S(1)} %shard_map.191.refs_0_.refs_4_.refs_2_), channel_id=1, source_target_pairs={{0,8},{1,57},{2,10},{3,59},{4,12},{5,61},{6,14},{7,63},{8,16},{9,1... | collective-permute-start | bytes 1769480 | tf_op jit(solution)/shard_map/ppermute | solution.py:588
  17.6 7.5 %collective-permute-start.9 = (bf16[8,256,128]{2,1,0:T(8,128)(2,1)S(1)}, bf16[8,256,128]{2,1,0:T(8,128)(2,1)S(1)}, u32[]{:S(2)}, u32[]{:S(2)}) collective-permute-start(bf16[8,256,128]{2,1,0:T(8,128)(2,1)S(1)} %get-tuple-element.40), channel_id=1, source_target_pairs={{0,1},{1,0},{2,3},{3,2},{4,5},{5,4},{6,7},{7,6},{8,9},{9,8},{10,11... | collective-permute-start | bytes 1572872 | tf_op jit(solution)/shard_map/ppermute | solution.py:49
  21.6 3.5 %collective-permute-start.8 = (bf16[8,256,128]{2,1,0:T(8,128)(2,1)S(1)}, bf16[8,256,128]{2,1,0:T(8,128)(2,1)S(1)}, u32[]{:S(2)}, u32[]{:S(2)}) collective-permute-start(bf16[8,256,128]{2,1,0:T(8,128)(2,1)S(1)} %get-tuple-element.39.refs_1_), channel_id=1, source_target_pairs={{0,1},{1,0},{2,3},{3,2},{4,5},{5,4},{6,7},{7,6},{8,9},{9,8},{10,11... | collective-permute-start | bytes 1572872 | tf_op jit(solution)/shard_map/ppermute | solution.py:49
  28.5 0.9 copy-start.13
  29.4 16.4 %collective-permute-start.11 = (bf16[2304,128]{1,0:T(8,128)(2,1)S(1)}, bf16[2304,128]{1,0:T(8,128)(2,1)S(1)}, u32[]{:S(2)}, u32[]{:S(2)}) collective-permute-start(bf16[2304,128]{1,0:T(8,128)(2,1)S(1)} %shard_map.195.refs_1_), channel_id=1, source_target_pairs={{0,8},{1,57},{2,10},{3,59},{4,12},{5,61},{6,14},{7,63},{8,16},{9,1... | collective-permute-start | bytes 1769480 | tf_op jit(solution)/shard_map/ppermute | solution.py:590
  29.4 9.8 %collective-permute-start.12 = (bf16[8,256,128]{2,1,0:T(8,128)(2,1)}, bf16[8,256,128]{2,1,0:T(8,128)(2,1)}, u32[]{:S(2)}, u32[]{:S(2)}) collective-permute-start(bf16[8,256,128]{2,1,0:T(8,128)(2,1)} %get-tuple-element.42.refs_2_), channel_id=1, source_target_pairs={{0,1},{1,0},{2,3},{3,2},{4,5},{5,4},{6,7},{7,6},{8,9},{9,8},{10,11... | collective-permute-start | bytes 1572872 | tf_op jit(solution)/shard_map/ppermute | solution.py:49
  31.5 10.7 %collective-permute-start.13 = (bf16[8,256,128]{2,1,0:T(8,128)(2,1)}, bf16[8,256,128]{2,1,0:T(8,128)(2,1)}, u32[]{:S(2)}, u32[]{:S(2)}) collective-permute-start(bf16[8,256,128]{2,1,0:T(8,128)(2,1)} %get-tuple-element.43), channel_id=1, source_target_pairs={{0,2},{1,7},{2,4},{3,1},{4,6},{5,3},{6,0},{7,5},{8,10},{9,15},{10,... | collective-permute-start | bytes 1572872 | tf_op jit(solution)/shard_map/ppermute | solution.py:584
  32.2 13.6 %all-to-all-start = ((bf16[4,2,128,256]{3,2,1,0:T(8,128)(2,1)}), bf16[4,2,128,256]{3,2,1,0:T(8,128)(2,1)S(1)}, u32[]{:S(2)}, u32[]{:S(2)}) async-start(bf16[4,2,128,256]{3,2,1,0:T(8,128)(2,1)} %get-tuple-element.44), calls=%async_computation | async-start | bytes 1048576 | tf_op jit(solution)/shard_map/all_to_all | solution.py:578
  37.0 10.4 %collective-permute-start.10 = (bf16[2304,128]{1,0:T(8,128)(2,1)S(1)}, bf16[2304,128]{1,0:T(8,128)(2,1)S(1)}, u32[]{:S(2)}, u32[]{:S(2)}) collective-permute-start(bf16[2304,128]{1,0:T(8,128)(2,1)S(1)} %shard_map.195.refs_1_), channel_id=1, source_target_pairs={{0,1},{1,0},{2,3},{3,2},{4,5},{5,4},{6,7},{7,6},{8,9},{9,8},{10,11... | collective-permute-start | bytes 1769480 | tf_op jit(solution)/shard_map/ppermute | solution.py:49
  39.2 6.6 %copy-start.7 = (f32[128,256]{1,0:T(8,128)}, f32[128,256]{1,0:T(8,128)S(1)}, u32[]{:S(2)}) copy-start(f32[128,256]{1,0:T(8,128)S(1)} %shard_map.192.refs_0_.refs_2_) | copy-start | bytes 393220
  45.8 5.1 %copy-start = (bf16[4,2,128,256]{3,2,1,0:T(8,128)(2,1)}, bf16[4,2,128,256]{3,2,1,0:T(8,128)(2,1)S(1)}, u32[]{:S(2)}) copy-start(bf16[4,2,128,256]{3,2,1,0:T(8,128)(2,1)S(1)} %all-to-all-done.refs_3_.refs_1_) | copy-start | bytes 1572868
  45.8 11.2 %collective-permute-start.15 = (bf16[2304,128]{1,0:T(8,128)(2,1)S(1)}, bf16[2304,128]{1,0:T(8,128)(2,1)S(1)}, u32[]{:S(2)}, u32[]{:S(2)}) collective-permute-start(bf16[2304,128]{1,0:T(8,128)(2,1)S(1)} %shard_map.198.refs_1_.refs_3_), channel_id=1, source_target_pairs={{0,8},{1,57},{2,10},{3,59},{4,12},{5,61},{6,14},{7,63},{8,16},{9,1... | collective-permute-start | bytes 1769480 | tf_op jit(solution)/shard_map/ppermute | solution.py:596
  45.9 12.4 %collective-permute-start.14 = (bf16[2304,128]{1,0:T(8,128)(2,1)S(1)}, bf16[2304,128]{1,0:T(8,128)(2,1)S(1)}, u32[]{:S(2)}, u32[]{:S(2)}) collective-permute-start(bf16[2304,128]{1,0:T(8,128)(2,1)S(1)} %shard_map.198.refs_1_.refs_3_), channel_id=1, source_target_pairs={{0,1},{1,0},{2,3},{3,2},{4,5},{5,4},{6,7},{7,6},{8,9},{9,8},{10,11... | collective-permute-start | bytes 1769480 | tf_op jit(solution)/shard_map/ppermute | solution.py:49
  47.5 10.7 %collective-permute-start.19 = (bf16[8,256,128]{2,1,0:T(8,128)(2,1)}, bf16[8,256,128]{2,1,0:T(8,128)(2,1)}, u32[]{:S(2)}, u32[]{:S(2)}) collective-permute-start(bf16[8,256,128]{2,1,0:T(8,128)(2,1)} %copy-done.13), channel_id=1, source_target_pairs={{0,2},{1,7},{2,4},{3,1},{4,6},{5,3},{6,0},{7,5},{8,10},{9,15},{10,... | collective-permute-start | bytes 1572872 | tf_op jit(solution)/shard_map/ppermute | solution.py:585
  47.5 0.9 copy-start.8
  48.4 2.5 %copy-start.3 = (bf16[2304,128]{1,0:T(8,128)(2,1)}, bf16[2304,128]{1,0:T(8,128)(2,1)S(1)}, u32[]{:S(2)}) copy-start(bf16[2304,128]{1,0:T(8,128)(2,1)S(1)} %collective-permute-done.10.refs_2_) | copy-start | bytes 1769476
  57.0 11.1 %collective-permute-start.17 = (bf16[2304,128]{1,0:T(8,128)(2,1)S(1)}, bf16[2304,128]{1,0:T(8,128)(2,1)S(1)}, u32[]{:S(2)}, u32[]{:S(2)}) collective-permute-start(bf16[2304,128]{1,0:T(8,128)(2,1)S(1)} %shard_map.200.refs_1_.refs_5_), channel_id=1, source_target_pairs={{0,8},{1,57},{2,10},{3,59},{4,12},{5,61},{6,14},{7,63},{8,16},{9,1... | collective-permute-start | bytes 1769480 | tf_op jit(solution)/shard_map/ppermute | solution.py:600
  57.0 11.1 %collective-permute-start.16 = (bf16[2304,128]{1,0:T(8,128)(2,1)S(1)}, bf16[2304,128]{1,0:T(8,128)(2,1)S(1)}, u32[]{:S(2)}, u32[]{:S(2)}) collective-permute-start(bf16[2304,128]{1,0:T(8,128)(2,1)S(1)} %shard_map.200.refs_1_.refs_5_), channel_id=1, source_target_pairs={{0,1},{1,0},{2,3},{3,2},{4,5},{5,4},{6,7},{7,6},{8,9},{9,8},{10,11... | collective-permute-start | bytes 1769480 | tf_op jit(solution)/shard_map/ppermute | solution.py:49
  57.8 10.3 %copy-start.4 = (bf16[2304,128]{1,0:T(8,128)(2,1)S(1)}, bf16[2304,128]{1,0:T(8,128)(2,1)}, u32[]{:S(2)}) copy-start(bf16[2304,128]{1,0:T(8,128)(2,1)} %copy-done.3) | copy-start | bytes 1769476
  57.8 10.3 %copy-start.24 = (s32[128]{0:T(128)S(1)}, s32[128]{0:T(128)}, u32[]{:S(2)}) copy-start(s32[128]{0:T(128)} %param.18) | copy-start | bytes 1540
  57.8 36.2 %collective-permute-start.18 = (bf16[8,256,128]{2,1,0:T(8,128)(2,1)}, bf16[8,256,128]{2,1,0:T(8,128)(2,1)S(1)}, u32[]{:S(2)}, u32[]{:S(2)}) collective-permute-start(bf16[8,256,128]{2,1,0:T(8,128)(2,1)} %get-tuple-element.47), channel_id=1, source_target_pairs={{0,1},{1,0},{2,3},{3,2},{4,5},{5,4},{6,7},{7,6},{8,9},{9,8},{10,11... | collective-permute-start | bytes 1572872 | tf_op jit(solution)/shard_map/ppermute | solution.py:49
  58.2 35.8 %collective-permute-start.20 = (bf16[8,256,128]{2,1,0:T(8,128)(2,1)}, bf16[8,256,128]{2,1,0:T(8,128)(2,1)}, u32[]{:S(2)}, u32[]{:S(2)}) collective-permute-start(bf16[8,256,128]{2,1,0:T(8,128)(2,1)} %collective-permute-done.19), channel_id=1, source_target_pairs={{0,1},{1,0},{2,3},{3,2},{4,5},{5,4},{6,7},{7,6},{8,9},{9,8},{10,11... | collective-permute-start | bytes 1572872 | tf_op jit(solution)/shard_map/ppermute | solution.py:49
  58.3 35.7 %collective-permute-start.21 = (bf16[8,256,128]{2,1,0:T(8,128)(2,1)}, bf16[8,256,128]{2,1,0:T(8,128)(2,1)}, u32[]{:S(2)}, u32[]{:S(2)}) collective-permute-start(bf16[8,256,128]{2,1,0:T(8,128)(2,1)} %shard_map.197.refs_1_), channel_id=1, source_target_pairs={{0,2},{1,7},{2,4},{3,1},{4,6},{5,3},{6,0},{7,5},{8,10},{9,15},{10,... | collective-permute-start | bytes 1572872 | tf_op jit(solution)/shard_map/ppermute | solution.py:592
  60.8 7.3 %copy-start.9 = (f32[128,256]{1,0:T(8,128)}, f32[128,256]{1,0:T(8,128)S(1)}, u32[]{:S(2)}) copy-start(f32[128,256]{1,0:T(8,128)S(1)} %shard_map.199.refs_0_.refs_1_) | copy-start | bytes 393220
  68.1 0.9 copy-start.5
  69.0 0.6 copy-start.14
  70.2 11.9 %all-to-all-start.1 = ((bf16[4,80,128]{2,1,0:T(8,128)(2,1)}), bf16[4,80,128]{2,1,0:T(8,128)(2,1)S(1)}, u32[]{:S(2)}, u32[]{:S(2)}) async-start(bf16[4,80,128]{2,1,0:T(8,128)(2,1)} %copy-done.14), calls=%async_computation.1 | async-start | bytes 163840 | tf_op jit(solution)/shard_map/all_to_all | solution.py:607
  74.9 1.1 copy-start.6
  76.0 0.9 copy-start.10
  76.9 2.5 %copy-start.11 = (bf16[16,32,256]{2,1,0:T(8,128)(2,1)S(1)}, bf16[16,32,256]{2,1,0:T(8,128)(2,1)}, u32[]{:S(2)}) copy-start(bf16[16,32,256]{2,1,0:T(8,128)(2,1)} %param.17) | copy-start | bytes 786436
  76.9 2.5 %copy-start.15 = (bf16[4,80,128]{2,1,0:T(8,128)(2,1)S(1)}, bf16[4,80,128]{2,1,0:T(8,128)(2,1)}, u32[]{:S(2)}) copy-start(bf16[4,80,128]{2,1,0:T(8,128)(2,1)} %copy-done.14) | copy-start | bytes 245764
  76.9 2.5 %copy-start.28 = (f32[8,128]{1,0:T(8,128)S(1)}, f32[8,128]{1,0:T(8,128)}, u32[]{:S(2)}) copy-start(f32[8,128]{1,0:T(8,128)} %copy-done.27) | copy-start | bytes 12292
  82.1 20.8 %copy-start.20 = (s32[27]{0:T(128)S(1)}, s32[27]{0:T(128)}, u32[]{:S(2)}) copy-start(s32[27]{0:T(128)} %copy-done.18) | copy-start | bytes 328
  82.1 0.6 copy-start.29
  85.1 1.4 %collective-permute-start.22 = (f32[8,256]{1,0:T(8,128)}, f32[8,256]{1,0:T(8,128)S(1)}, u32[]{:S(2)}, u32[]{:S(2)}) collective-permute-start(f32[8,256]{1,0:T(8,128)} %get-tuple-element.48), channel_id=1, source_target_pairs={{0,1},{1,0},{2,3},{3,2},{4,5},{5,4},{6,7},{7,6},{8,9},{9,8},{10,11... | collective-permute-start | bytes 24584 | tf_op jit(solution)/shard_map/ppermute | solution.py:49
  87.1 1.2 %collective-permute-start.24 = (f32[8,256]{1,0:T(8,128)S(1)}, f32[8,256]{1,0:T(8,128)S(1)}, u32[]{:S(2)}, u32[]{:S(2)}) collective-permute-start(f32[8,256]{1,0:T(8,128)S(1)} %add.83), channel_id=1, source_target_pairs={{1,7},{3,5},{5,3},{7,1},{9,15},{11,13},{13,11},{15,9},{17,23},{19,... | collective-permute-start | bytes 24584 | tf_op jit(solution)/shard_map/ppermute | solution.py:531
  87.8 3.7 %collective-permute-start.23 = (f32[8,256]{1,0:T(8,128)S(1)}, f32[8,256]{1,0:T(8,128)S(1)}, u32[]{:S(2)}, u32[]{:S(2)}) collective-permute-start(f32[8,256]{1,0:T(8,128)S(1)} %add.83), channel_id=1, source_target_pairs={{0,2},{1,5},{2,0},{3,7},{4,6},{5,1},{6,4},{7,3},{8,10},{9,13},{10,... | collective-permute-start | bytes 24584 | tf_op jit(solution)/shard_map/ppermute | solution.py:530
  91.5 30.4 %copy-start.22 = (f32[8,256]{1,0:T(8,128)S(1)}, f32[8,256]{1,0:T(8,128)}, u32[]{:S(2)}) copy-start(f32[8,256]{1,0:T(8,128)} %get-tuple-element.33.refs_10_) | copy-start | bytes 24580
  91.5 30.4 %copy-start.23 = (f32[8,256]{1,0:T(8,128)S(1)}, f32[8,256]{1,0:T(8,128)}, u32[]{:S(2)}) copy-start(f32[8,256]{1,0:T(8,128)} %get-tuple-element.36.refs_11_) | copy-start | bytes 24580
  91.5 30.4 %copy-start.25 = (f32[8,32]{1,0:T(8,128)S(1)}, f32[8,32]{1,0:T(8,128)}, u32[]{:S(2)}) copy-start(f32[8,32]{1,0:T(8,128)} %refs_12_.1) | copy-start | bytes 3076
  91.5 30.4 %copy-start.26 = (f32[8,32]{1,0:T(8,128)S(1)}, f32[8,32]{1,0:T(8,128)}, u32[]{:S(2)}) copy-start(f32[8,32]{1,0:T(8,128)} %refs_13_.1) | copy-start | bytes 3076
  91.6 29.5 %copy-start.12 = (bf16[256,16,32]{0,2,1:T(8,128)(2,1)S(1)}, bf16[256,16,32]{0,2,1:T(8,128)(2,1)}, u32[]{:S(2)}) copy-start(bf16[256,16,32]{0,2,1:T(8,128)(2,1)} %param.16) | copy-start | bytes 786436
  91.6 30.4 %copy-start.16 = (f32[256,256]{1,0:T(8,128)S(1)}, f32[256,256]{1,0:T(8,128)}, u32[]{:S(2)}) copy-start(f32[256,256]{1,0:T(8,128)} %get-tuple-element.58.refs_8_) | copy-start | bytes 786436
  91.6 30.4 %copy-start.17 = (f32[256,256]{1,0:T(8,128)S(1)}, f32[256,256]{1,0:T(8,128)}, u32[]{:S(2)}) copy-start(f32[256,256]{1,0:T(8,128)} %get-tuple-element.59.refs_9_) | copy-start | bytes 786436
  91.6 3.2 %collective-permute-start.25 = (f32[8,256]{1,0:T(8,128)S(1)}, f32[8,256]{1,0:T(8,128)S(1)}, u32[]{:S(2)}, u32[]{:S(2)}) collective-permute-start(f32[8,256]{1,0:T(8,128)S(1)} %add_select_fusion.p_ref), channel_id=1, source_target_pairs={{0,1},{1,0},{2,3},{3,2},{4,5},{5,4},{6,7},{7,6},{8,9},{9,8},{10,11... | collective-permute-start | bytes 24584 | tf_op jit(solution)/shard_map/ppermute | solution.py:49
  94.8 0.7 copy-start.19
  97.8 11.7 %collective-permute-start.27 = (bf16[288,128]{1,0:T(8,128)(2,1)S(1)}, bf16[288,128]{1,0:T(8,128)(2,1)S(1)}, u32[]{:S(2)}, u32[]{:S(2)}) collective-permute-start(bf16[288,128]{1,0:T(8,128)(2,1)S(1)} %get-tuple-element.51), channel_id=1, source_target_pairs={{0,24},{8,32},{16,40},{24,48},{32,56},{40,0},{48,8},{56,16},{1,25}... | collective-permute-start | bytes 221192 | tf_op jit(solution)/shard_map/ppermute | solution.py:627
  99.2 13.6 %collective-permute-start.28 = (bf16[288,128]{1,0:T(8,128)(2,1)S(1)}, bf16[288,128]{1,0:T(8,128)(2,1)S(1)}, u32[]{:S(2)}, u32[]{:S(2)}) collective-permute-start(bf16[288,128]{1,0:T(8,128)(2,1)S(1)} %get-tuple-element.52), channel_id=1, source_target_pairs={{0,40},{8,48},{16,56},{24,0},{32,8},{40,16},{48,24},{56,32},{1,41}... | collective-permute-start | bytes 221192 | tf_op jit(solution)/shard_map/ppermute | solution.py:627
  105.3 10.6 %collective-permute-start.29 = (bf16[288,128]{1,0:T(8,128)(2,1)S(1)}, bf16[288,128]{1,0:T(8,128)(2,1)S(1)}, u32[]{:S(2)}, u32[]{:S(2)}) collective-permute-start(bf16[288,128]{1,0:T(8,128)(2,1)S(1)} %get-tuple-element.53), channel_id=1, source_target_pairs={{0,16},{8,24},{16,32},{24,40},{32,48},{40,56},{48,0},{56,8},{1,17}... | collective-permute-start | bytes 221192 | tf_op jit(solution)/shard_map/ppermute | solution.py:627
  105.4 10.5 %collective-permute-start.30 = (bf16[288,128]{1,0:T(8,128)(2,1)S(1)}, bf16[288,128]{1,0:T(8,128)(2,1)S(1)}, u32[]{:S(2)}, u32[]{:S(2)}) collective-permute-start(bf16[288,128]{1,0:T(8,128)(2,1)S(1)} %get-tuple-element.54), channel_id=1, source_target_pairs={{0,48},{8,56},{16,0},{24,8},{32,16},{40,24},{48,32},{56,40},{1,49}... | collective-permute-start | bytes 221192 | tf_op jit(solution)/shard_map/ppermute | solution.py:627
  109.5 6.4 %collective-permute-start.31 = (bf16[288,128]{1,0:T(8,128)(2,1)S(1)}, bf16[288,128]{1,0:T(8,128)(2,1)S(1)}, u32[]{:S(2)}, u32[]{:S(2)}) collective-permute-start(bf16[288,128]{1,0:T(8,128)(2,1)S(1)} %get-tuple-element.55), channel_id=1, source_target_pairs={{0,8},{8,16},{16,24},{24,32},{32,40},{40,48},{48,56},{56,0},{1,9},... | collective-permute-start | bytes 221192 | tf_op jit(solution)/shard_map/ppermute | solution.py:627
  109.5 6.4 %collective-permute-start.32 = (bf16[288,128]{1,0:T(8,128)(2,1)S(1)}, bf16[288,128]{1,0:T(8,128)(2,1)S(1)}, u32[]{:S(2)}, u32[]{:S(2)}) collective-permute-start(bf16[288,128]{1,0:T(8,128)(2,1)S(1)} %get-tuple-element.56), channel_id=1, source_target_pairs={{0,56},{8,0},{16,8},{24,16},{32,24},{40,32},{48,40},{56,48},{1,57}... | collective-permute-start | bytes 221192 | tf_op jit(solution)/shard_map/ppermute | solution.py:627
  112.8 8.3 %collective-permute-start.26 = (bf16[288,128]{1,0:T(8,128)(2,1)S(1)}, bf16[288,128]{1,0:T(8,128)(2,1)S(1)}, u32[]{:S(2)}, u32[]{:S(2)}) collective-permute-start(bf16[288,128]{1,0:T(8,128)(2,1)S(1)} %get-tuple-element.49.refs_0_), channel_id=1, source_target_pairs={{0,32},{8,40},{16,48},{24,56},{32,0},{40,8},{48,16},{56,24},{1,33}... | collective-permute-start | bytes 221192 | tf_op jit(solution)/shard_map/ppermute | solution.py:627
  (1 other events, 0.6 us)

commit v2 on v1

--- a/solution.py
+++ b/solution.py
@@ -590,16 +590,16 @@
     two = lax.ppermute(one, F, Z_BY_CORE)
     (t_near,) = part_kernel(w5, turned, spots, 6, [[r_near, g_two]], [])
     g_near = lax.ppermute(t_near, F, Y_BY_CORE)
-    two = tied(two, t_near, frozen_zero, boths)
+    two = tied(two, g_two, frozen_zero)
     two_o = swap(two)
     frozen_one = frozen_kernel(w4, spots, frozen_zero, [one, one_o], [20, 21])
     three = lax.ppermute(two, F, Z_BY_CORE)
-    three = tied(three, frozen_one)
+    three = tied(three, t_near, frozen_one)
     three_o = swap(three)
     frozen_two = frozen_kernel(w4, spots, frozen_one, [two, two_o], [22, 23])
     four = lax.ppermute(three, F, Z_BY_CORE)
-    four = tied(four, frozen_two)
     frozen_three = frozen_kernel(w4, spots, frozen_two, [three, three_o], [24, 25])
+    four = tied(four, frozen_three, boths)
 
     small, back, scale = small_kernel(
         spots, [block, one, one_o, two, two_o, three, three_o, four], tenant
@@ -618,12 +618,9 @@
     moments = sum_y(moments, core)
 
     adds = [r_own, swap(g_far), g_near]
-    first = last_part_kernel(w5, turned, spots, 7, ORDER[1:4], adds, moments, [])
-    second = last_part_kernel(
-        w5, turned, spots, 7, ORDER[4:] + ORDER[:1], adds, moments, [first[0]]
-    )
-    pieces = [second[-1]]
-    for k, piece in zip(ORDER[1:], first + second[:-1]):
+    reduced = last_part_kernel(w5, turned, spots, 7, ORDER, adds, moments, [])
+    pieces = [reduced[0]]
+    for k, piece in zip(ORDER[1:], reduced[1:]):
         pieces.append(lax.ppermute(piece, "z", turn(NZ, k)))
     normed_gradient_transposed = gradient_kernel(pieces, down, back, tenant)
     update_a, update_b, col_a_new, row_b_new = update_kernel(

time: 125 us -> 122 us (0.976)
  waiting for transfers between devices: 29.6 us -> 22.6 us
  local copies, waits for them, and re-layouts: 6.65 us -> 10.6 us
  Pallas kernels: 37.9 us -> 34.9 us
  starting transfers between devices: 47.3 us -> 50.3 us
    ppermute x1, waiting for transfers between devices: 7.27 us -> 0.01 us  [on_device(): four = lax.ppermute(three, F, Z_BY_CORE)]
    unnamed x60 -> x58, local copies, waits for them, and re-layouts: 6.55 us -> 10.5 us
    ppermute x1, waiting for transfers between devices: 6.12 us -> 2.79 us  [on_device(): three = lax.ppermute(two, F, Z_BY_CORE)]
    ppermute x7, waiting for transfers between devices: 5.13 us -> 2.78 us  [on_device(): pieces.append(lax.ppermute(piece, 'z', turn(NZ, k)))]
    pallas_call x2 -> x1, Pallas kernels: 4.69 us -> 2.64 us  [last_part_kernel(): pl.pallas_call(functools.partial(last_part_body, offsets), grid_spec=pltp...]
    ppermute x14, waiting for transfers between devices: 3.17 us -> 5.03 us  [swap(): return lax.ppermute(v, 'core', turn(NC, 1))]
    ppermute x1, waiting for transfers between devices: 3.05 us -> 4.88 us  [on_device(): g_two = lax.ppermute(t_two, F, Y_BY_CORE)]
    pallas_call x4, Pallas kernels: 12.6 us -> 10.9 us  [part_kernel(): pl.pallas_call(functools.partial(part_body, [len(a) for a in adds]), grid...]
  transfers between devices with their start and end apart: 35 -> 35, of which waited for: 13 -> 16; matrix products, arithmetic and copies ran while one was open for 1% -> 1% of each run, Pallas kernels for 24% -> 22%
where the time goes in v2:
time: 122 us; the launch traced here: 121 us
  starting transfers between devices  50.3 us (41%)
  Pallas kernels  34.9 us (29%)
  waiting for transfers between devices  22.6 us (19%)
  local copies, waits for them, and re-layouts  10.6 us (9%)
  between operations  1.61 us (1%)
    ppermute x7, starting transfers between devices, on_device(): pieces.append(lax.ppermute(piece, 'z', turn(NZ, k)))  17.1 us
    ppermute x14, starting transfers between devices, swap(): return lax.ppermute(v, 'core', turn(NC, 1))  13.5 us
    pallas_call x4, Pallas kernels, part_kernel(): pl.pallas_call(functools.partial(part_body, [len(a) for a in adds]), grid...  10.9 us
    unnamed x58, local copies, waits for them, and re-layouts  10.5 us
    pallas_call x4, Pallas kernels, frozen_kernel(): pl.pallas_call(functools.partial(frozen_body, n, has_acc), grid_spec=pltp...  9.76 us
    ppermute x3, starting transfers between devices, on_device(): lax.ppermute(message, 'y', turn(NY, k))  5.82 us
    ppermute x14, waiting for transfers between devices, swap(): return lax.ppermute(v, 'core', turn(NC, 1))  5.03 us
    ppermute x1, waiting for transfers between devices, on_device(): g_two = lax.ppermute(t_two, F, Y_BY_CORE)  4.88 us
  transfers between devices with their start and end apart: 35, of which 16 were waited for; matrix products, arithmetic and copies ran while one was open for 1% of the time, Pallas kernels for 22%

profile of v2, /device:TPU:2, one launch (start us, length us, event | category | flops | bytes accessed | tf_op | source)
XLA Modules:
  0.0 120.7 jit_solution(17664652597094955930)
XLA Ops:
  1.3 2.1 %shard_map.188 = (bf16[416,128]{1,0:T(8,128)(2,1)}, bf16[4,2,128,256]{3,2,1,0:T(8,128)(2,1)}, bf16[256,128]{1,0:T(8,128)(2,1)}) custom-call(s32[1]{0:T(128)S(6)} %copy.31.live_ref, bf16[128,256]{1,0:T(8,128)(2,1)} %x_ref.1, bf16[256]{0:T(256)(128)(2,1)} %gain_ref.1, bf16[128,256]{1,0:T(8,128)(2,1)} %cot_ref.1, bf16[512,256]{1,0:T(8,128)(2,1)} %bitcast.28, ...), custom_call_target="tpu_custom_call" | custom-call | flops 67108864 | bytes 1048576 | tf_op jit(solution)/shard_map/pallas_call | solution.py:124
  3.4 1.6 %collective-permute-start.2 = (bf16[416,128]{1,0:T(8,128)(2,1)}, bf16[416,128]{1,0:T(8,128)(2,1)S(1)}, u32[]{:S(2)}, u32[]{:S(2)}) collective-permute-start(bf16[416,128]{1,0:T(8,128)(2,1)} %get-tuple-element.37.refs_0_), channel_id=1, source_target_pairs={{0,2},{2,4},{4,6},{6,0},{1,3},{3,5},{5,7},{7,1},{8,10},{10,12},{12... | collective-permute-start | bytes 319496 | tf_op jit(solution)/shard_map/ppermute | solution.py:575
  5.0 2.9 %collective-permute-start.1 = (bf16[416,128]{1,0:T(8,128)(2,1)}, bf16[416,128]{1,0:T(8,128)(2,1)S(1)}, u32[]{:S(2)}, u32[]{:S(2)}) collective-permute-start(bf16[416,128]{1,0:T(8,128)(2,1)} %get-tuple-element.37.refs_0_), channel_id=1, source_target_pairs={{0,4},{2,6},{4,0},{6,2},{1,5},{3,7},{5,1},{7,3},{8,12},{10,14},{12... | collective-permute-start | bytes 319496 | tf_op jit(solution)/shard_map/ppermute | solution.py:575
  7.9 1.3 %collective-permute-start = (bf16[416,128]{1,0:T(8,128)(2,1)}, bf16[416,128]{1,0:T(8,128)(2,1)S(1)}, u32[]{:S(2)}, u32[]{:S(2)}) collective-permute-start(bf16[416,128]{1,0:T(8,128)(2,1)} %get-tuple-element.37.refs_0_), channel_id=1, source_target_pairs={{0,6},{2,0},{4,2},{6,4},{1,7},{3,1},{5,3},{7,5},{8,14},{10,8},{12,... | collective-permute-start | bytes 319496 | tf_op jit(solution)/shard_map/ppermute | solution.py:575
  9.3 0.8 copy-done.4
  10.2 2.7 %shard_map.189 = (bf16[8,256,128]{2,1,0:T(8,128)(2,1)S(1)}, bf16[8,256,128]{2,1,0:T(8,128)(2,1)S(1)}) custom-call(s32[27]{0:T(128)S(1)} %stack.75.spots_ref, bf16[256,128]{1,0:T(8,128)(2,1)S(1)} %copy-done.4, bf16[8,4,2,256,256]{4,3,2,1,0:T(8,128)(2,1)} %bitcast.34, bf16[8,4,2,256,256]{4,3,2,1,0:T(8,128)(2,1)} %bitcast.35), custom_call_target="tpu_custom_call" | custom-call | flops 268435456 | bytes 4194304 | tf_op jit(solution)/shard_map/pallas_call | solution.py:166
  12.9 0.6 collective-permute-start.6
  13.6 0.4 collective-permute-start.4
  14.0 0.4 collective-permute-done.6.refs_7_
  14.9 0.6 shard_map.191.refs_0_.refs_4_.refs_2_
  15.6 2.0 %collective-permute-start.7 = (bf16[2304,128]{1,0:T(8,128)(2,1)S(1)}, bf16[2304,128]{1,0:T(8,128)(2,1)S(1)}, u32[]{:S(2)}, u32[]{:S(2)}) collective-permute-start(bf16[2304,128]{1,0:T(8,128)(2,1)S(1)} %shard_map.191.refs_0_.refs_4_.refs_2_), channel_id=1, source_target_pairs={{0,8},{1,57},{2,10},{3,59},{4,12},{5,61},{6,14},{7,63},{8,16},{9,1... | collective-permute-start | bytes 1769480 | tf_op jit(solution)/shard_map/ppermute | solution.py:588
  17.6 4.0 %collective-permute-start.9 = (bf16[8,256,128]{2,1,0:T(8,128)(2,1)S(1)}, bf16[8,256,128]{2,1,0:T(8,128)(2,1)S(1)}, u32[]{:S(2)}, u32[]{:S(2)}) collective-permute-start(bf16[8,256,128]{2,1,0:T(8,128)(2,1)S(1)} %get-tuple-element.40), channel_id=1, source_target_pairs={{0,1},{1,0},{2,3},{3,2},{4,5},{5,4},{6,7},{7,6},{8,9},{9,8},{10,11... | collective-permute-start | bytes 1572872 | tf_op jit(solution)/shard_map/ppermute | solution.py:49
  21.6 2.7 %shard_map.194 = (bf16[8,256,128]{2,1,0:T(8,128)(2,1)S(1)}, bf16[8,256,128]{2,1,0:T(8,128)(2,1)S(1)}) custom-call(s32[27]{0:T(128)S(1)} %stack.75.spots_ref, bf16[256,128]{1,0:T(8,128)(2,1)S(1)} %copy-done.4, bf16[8,4,2,256,256]{4,3,2,1,0:T(8,128)(2,1)} %bitcast.36, bf16[8,4,2,256,256]{4,3,2,1,0:T(8,128)(2,1)} %bitcast.37, ...), custom_call_target="tpu_custom_call" | custom-call | flops 268435456 | bytes 4194304 | tf_op jit(solution)/shard_map/pallas_call | solution.py:166
  24.3 3.4 %shard_map.193 = (bf16[8,256,128]{2,1,0:T(8,128)(2,1)S(1)}, bf16[8,256,128]{2,1,0:T(8,128)(2,1)}) custom-call(s32[27]{0:T(128)S(1)} %stack.75.spots_ref, bf16[256,128]{1,0:T(8,128)(2,1)S(1)} %copy-done.5, bf16[8,4,2,256,256]{4,3,2,1,0:T(8,128)(2,1)} %bitcast.38, bf16[8,4,2,256,256]{4,3,2,1,0:T(8,128)(2,1)} %bitcast.39, ...), custom_call_target="tpu_custom_call" | custom-call | flops 268435456 | bytes 4194304 | tf_op jit(solution)/shard_map/pallas_call | solution.py:166
  27.7 1.7 %collective-permute-done.7.refs_0_ = bf16[2304,128]{1,0:T(8,128)(2,1)S(1)} collective-permute-done((bf16[2304,128]{1,0:T(8,128)(2,1)S(1)}, bf16[2304,128]{1,0:T(8,128)(2,1)S(1)}, u32[]{:S(2)}, u32[]{:S(2)}) %collective-permute-start.7) | collective-permute-done | bytes 589856 | tf_op jit(solution)/shard_map/ppermute | solution.py:588
  29.4 0.7 collective-permute-start.12
  30.0 2.7 %collective-permute-start.10 = (bf16[2304,128]{1,0:T(8,128)(2,1)S(1)}, bf16[2304,128]{1,0:T(8,128)(2,1)S(1)}, u32[]{:S(2)}, u32[]{:S(2)}) collective-permute-start(bf16[2304,128]{1,0:T(8,128)(2,1)S(1)} %shard_map.195.refs_1_), channel_id=1, source_target_pairs={{0,1},{1,0},{2,3},{3,2},{4,5},{5,4},{6,7},{7,6},{8,9},{9,8},{10,11... | collective-permute-start | bytes 1769480 | tf_op jit(solution)/shard_map/ppermute | solution.py:49
  32.8 2.1 %shard_map.192.refs_0_.refs_2_ = f32[128,256]{1,0:T(8,128)S(1)} custom-call(s32[27]{0:T(128)S(1)} %stack.75.spots_ref, bf16[2304,128]{1,0:T(8,128)(2,1)S(1)} %shard_map.191.refs_0_.refs_4_.refs_2_, bf16[8,8,256,256]{3,2,1,0:T(8,128)(2,1)} %bitcast.40), custom_call_target="tpu_custom_call" | custom-call | flops 134217728 | bytes 9437184 | tf_op jit(solution)/shard_map/pallas_call | solution.py:290
  34.9 4.9 %collective-permute-done.12.refs_1_.refs_2_ = bf16[8,256,128]{2,1,0:T(8,128)(2,1)S(1)} collective-permute-done((bf16[8,256,128]{2,1,0:T(8,128)(2,1)S(1)}, bf16[8,256,128]{2,1,0:T(8,128)(2,1)S(1)}, u32[]{:S(2)}, u32[]{:S(2)}) %collective-permute-start.12) | collective-permute-done | bytes 524320 | tf_op jit(solution)/shard_map/ppermute | solution.py:584
  39.8 0.7 collective-permute-done.11.refs_0_
  40.5 1.3 %collective-permute-start.15 = (bf16[8,256,128]{2,1,0:T(8,128)(2,1)S(1)}, bf16[8,256,128]{2,1,0:T(8,128)(2,1)S(1)}, u32[]{:S(2)}, u32[]{:S(2)}) collective-permute-start(bf16[8,256,128]{2,1,0:T(8,128)(2,1)S(1)} %get-tuple-element.42.refs_2_), channel_id=1, source_target_pairs={{0,1},{1,0},{2,3},{3,2},{4,5},{5,4},{6,7},{7,6},{8,9},{9,8},{10,11... | collective-permute-start | bytes 1572872 | tf_op jit(solution)/shard_map/ppermute | solution.py:49
  41.8 0.4 collective-permute-start.19
  42.2 1.9 %collective-permute-done.15.refs_1_ = bf16[8,256,128]{2,1,0:T(8,128)(2,1)S(1)} collective-permute-done((bf16[8,256,128]{2,1,0:T(8,128)(2,1)S(1)}, bf16[8,256,128]{2,1,0:T(8,128)(2,1)S(1)}, u32[]{:S(2)}, u32[]{:S(2)}) %collective-permute-start.15) | collective-permute-done | bytes 524320 | tf_op jit(solution)/shard_map/ppermute | solution.py:49
  44.0 2.2 %shard_map.199.refs_1_ = bf16[8,256,128]{2,1,0:T(8,128)(2,1)S(1)} custom-call(s32[27]{0:T(128)S(1)} %stack.75.spots_ref, bf16[256,128]{1,0:T(8,128)(2,1)S(1)} %copy-done.5, bf16[8,4,2,256,256]{4,3,2,1,0:T(8,128)(2,1)} %bitcast.41, bf16[8,256,128]{2,1,0:T(8,128)(2,1)S(1)} %collective-permute-done.15.refs_1_, ...), custom_call_target="tpu_custom_call" | custom-call | flops 134217728 | bytes 2097152 | tf_op jit(solution)/shard_map/pallas_call | solution.py:166
  46.3 2.5 %shard_map.196.refs_0_.refs_2_ = f32[128,256]{1,0:T(8,128)S(1)} custom-call(s32[27]{0:T(128)S(1)} %stack.75.spots_ref, f32[128,256]{1,0:T(8,128)S(1)} %shard_map.192.refs_0_.refs_2_, bf16[2304,128]{1,0:T(8,128)(2,1)S(1)} %shard_map.195.refs_1_, bf16[2304,128]{1,0:T(8,128)(2,1)S(1)} %collective-permute-done.10.refs_2_, bf16[8,8,256,256]{3,2,1,0:T(8,128)(2,1)} %bitcast.42, ...), custom_call_target="tpu_custom_call" | custom-call | flops 268435456 | bytes 9437184 | tf_op jit(solution)/shard_map/pallas_call | solution.py:290
  48.8 2.8 %collective-permute-done.14.refs_0_ = bf16[2304,128]{1,0:T(8,128)(2,1)S(1)} collective-permute-done((bf16[2304,128]{1,0:T(8,128)(2,1)S(1)}, bf16[2304,128]{1,0:T(8,128)(2,1)S(1)}, u32[]{:S(2)}, u32[]{:S(2)}) %collective-permute-start.14) | collective-permute-done | bytes 589856 | tf_op jit(solution)/shard_map/ppermute | solution.py:596
  51.7 4.8 %all-to-all-start = ((bf16[4,2,128,256]{3,2,1,0:T(8,128)(2,1)}), bf16[4,2,128,256]{3,2,1,0:T(8,128)(2,1)S(1)}, u32[]{:S(2)}, u32[]{:S(2)}) async-start(bf16[4,2,128,256]{3,2,1,0:T(8,128)(2,1)} %get-tuple-element.44), calls=%async_computation | async-start | bytes 1048576 | tf_op jit(solution)/shard_map/all_to_all | solution.py:578
  56.5 0.9 collective-permute-start.18
  57.7 0.9 copy-done.7
  58.6 2.6 %shard_map.198.refs_0_ = f32[128,256]{1,0:T(8,128)S(1)} custom-call(s32[27]{0:T(128)S(1)} %stack.75.spots_ref, f32[128,256]{1,0:T(8,128)S(1)} %copy-done.7, bf16[2304,128]{1,0:T(8,128)(2,1)S(1)} %shard_map.197.refs_1_.refs_3_, bf16[2304,128]{1,0:T(8,128)(2,1)} %collective-permute-done.13.refs_2_.refs_4_, bf16[8,8,256,256]{3,2,1,0:T(8,128)(2,1)} %bitcast.44, ...), custom_call_target="tpu_custom_call" | custom-call | flops 268435456 | bytes 9437184 | tf_op jit(solution)/shard_map/pallas_call | solution.py:290
  61.2 2.6 %shard_map.201.refs_1_.acc_ref = f32[128,256]{1,0:T(8,128)S(1)} custom-call(s32[27]{0:T(128)S(1)} %stack.75.spots_ref, f32[128,256]{1,0:T(8,128)S(1)} %shard_map.198.refs_0_, bf16[2304,128]{1,0:T(8,128)(2,1)S(1)} %shard_map.200.refs_1_.refs_5_, bf16[2304,128]{1,0:T(8,128)(2,1)} %collective-permute-done.16.refs_2_.refs_6_, bf16[8,8,256,256]{3,2,1,0:T(8,128)(2,1)} %bitcast.46, ...), custom_call_target="tpu_custom_call" | custom-call | flops 268435456 | bytes 9437184 | tf_op jit(solution)/shard_map/pallas_call | solution.py:290
  63.9 0.6 copy-done.8
  64.5 1.2 %all-to-all-done.refs_2_.refs_1_ = bf16[4,2,128,256]{3,2,1,0:T(8,128)(2,1)S(1)} async-done(((bf16[4,2,128,256]{3,2,1,0:T(8,128)(2,1)}), bf16[4,2,128,256]{3,2,1,0:T(8,128)(2,1)S(1)}, u32[]{:S(2)}, u32[]{:S(2)}) %all-to-all-start) | async-done | bytes 524320 | tf_op jit(solution)/shard_map/all_to_all | solution.py:578
  65.7 1.0 copy-done.9
  66.8 1.1 copy-done.2
  67.8 0.9 shard_map.203
  68.8 0.6 copy-done.13
  69.4 0.6 copy-done.25
  70.0 4.7 %all-to-all-start.1 = ((bf16[4,80,128]{2,1,0:T(8,128)(2,1)}), bf16[4,80,128]{2,1,0:T(8,128)(2,1)S(1)}, u32[]{:S(2)}, u32[]{:S(2)}) async-start(bf16[4,80,128]{2,1,0:T(8,128)(2,1)} %copy-done.13), calls=%async_computation.1 | async-start | bytes 163840 | tf_op jit(solution)/shard_map/all_to_all | solution.py:607
  74.7 0.9 copy-done.10
  75.6 0.9 copy-done.11
  76.6 0.9 copy-done.14
  77.5 0.7 copy-done.26
  78.2 2.7 %shard_map.204.refs_4_ = bf16[128,256]{1,0:T(8,128)(2,1)} custom-call(s32[27]{0:T(128)S(1)} %stack.75.spots_ref, f32[128,256]{1,0:T(8,128)S(1)} %copy-done.10, bf16[2304,128]{1,0:T(8,128)(2,1)S(1)} %shard_map.202.refs_7_.x_ref, bf16[8,8,256,256]{3,2,1,0:T(8,128)(2,1)} %bitcast.48, f32[8,128]{1,0:T(8,128)S(1)} %copy-done.26, ...), custom_call_target="tpu_custom_call" | custom-call | flops 268435456 | bytes 9437184 | tf_op jit(solution)/shard_map/pallas_call | solution.py:324
  80.9 0.6 copy-done.28
  81.6 2.3 %shard_map.205 = (f32[256,256]{1,0:T(8,128)}, f32[256,256]{1,0:T(8,128)}, f32[8,256]{1,0:T(8,128)}, f32[8,256]{1,0:T(8,128)}, f32[8,256]{1,0:T(8,128)}) custom-call(s32[16]{0:T(128)} %slot_ref.1, s32[27]{0:T(128)} %copy-done.17, bf16[4,80,128]{2,1,0:T(8,128)(2,1)} %copy-done.28, bf16[4,2,128,256]{3,2,1,0:T(8,128)(2,1)} %copy-done, f32[8,256]{1,0:T(8,128)} %refs_2_.1, ...), custom_call_target="tpu_custom_call" | custom-call | flops 134217728 | bytes 2097152 | tf_op jit(solution)/shard_map/pallas_call | solution.py:451
  84.0 1.4 %collective-permute-done.22 = f32[8,256]{1,0:T(8,128)S(1)} collective-permute-done((f32[8,256]{1,0:T(8,128)}, f32[8,256]{1,0:T(8,128)S(1)}, u32[]{:S(2)}, u32[]{:S(2)}) %collective-permute-start.22) | collective-permute-done | bytes 8224 | tf_op jit(solution)/shard_map/ppermute | solution.py:49
  85.3 0.7 add.83
  86.0 0.6 collective-permute-start.24
  87.0 3.5 %collective-permute-done.23 = f32[8,256]{1,0:T(8,128)S(1)} collective-permute-done((f32[8,256]{1,0:T(8,128)S(1)}, f32[8,256]{1,0:T(8,128)S(1)}, u32[]{:S(2)}, u32[]{:S(2)}) %collective-permute-start.23) | collective-permute-done | bytes 8224 | tf_op jit(solution)/shard_map/ppermute | solution.py:530
  90.4 3.4 %collective-permute-start.25 = (f32[8,256]{1,0:T(8,128)S(1)}, f32[8,256]{1,0:T(8,128)S(1)}, u32[]{:S(2)}, u32[]{:S(2)}) collective-permute-start(f32[8,256]{1,0:T(8,128)S(1)} %add_select_fusion.p_ref), channel_id=1, source_target_pairs={{0,1},{1,0},{2,3},{3,2},{4,5},{5,4},{6,7},{7,6},{8,9},{9,8},{10,11... | collective-permute-start | bytes 24584 | tf_op jit(solution)/shard_map/ppermute | solution.py:49
  93.8 0.8 collective-permute-done.25.q_ref
  94.6 0.7 copy-done.18
  95.3 2.6 %shard_map.206 = (bf16[288,128]{1,0:T(8,128)(2,1)S(1)}, bf16[288,128]{1,0:T(8,128)(2,1)S(1)}, bf16[288,128]{1,0:T(8,128)(2,1)S(1)}, bf16[288,128]{1,0:T(8,128)(2...) custom-call(s32[27]{0:T(128)S(1)} %copy-done.18, ...), custom_call_target="tpu_custom_call" | custom-call | flops 134217728 | bytes 2097152 | tf_op jit(solution)/shard_map/pallas_call | solution.py:206
  97.9 4.7 %collective-permute-start.26 = (bf16[288,128]{1,0:T(8,128)(2,1)S(1)}, bf16[288,128]{1,0:T(8,128)(2,1)S(1)}, u32[]{:S(2)}, u32[]{:S(2)}) collective-permute-start(bf16[288,128]{1,0:T(8,128)(2,1)S(1)} %get-tuple-element.50), channel_id=1, source_target_pairs={{0,32},{8,40},{16,48},{24,56},{32,0},{40,8},{48,16},{56,24},{1,33}... | collective-permute-start | bytes 221192 | tf_op jit(solution)/shard_map/ppermute | solution.py:624
  102.6 1.4 %collective-permute-start.27 = (bf16[288,128]{1,0:T(8,128)(2,1)S(1)}, bf16[288,128]{1,0:T(8,128)(2,1)S(1)}, u32[]{:S(2)}, u32[]{:S(2)}) collective-permute-start(bf16[288,128]{1,0:T(8,128)(2,1)S(1)} %get-tuple-element.51), channel_id=1, source_target_pairs={{0,24},{8,32},{16,40},{24,48},{32,56},{40,0},{48,8},{56,16},{1,25}... | collective-permute-start | bytes 221192 | tf_op jit(solution)/shard_map/ppermute | solution.py:624
  104.1 3.6 %collective-permute-start.28 = (bf16[288,128]{1,0:T(8,128)(2,1)S(1)}, bf16[288,128]{1,0:T(8,128)(2,1)S(1)}, u32[]{:S(2)}, u32[]{:S(2)}) collective-permute-start(bf16[288,128]{1,0:T(8,128)(2,1)S(1)} %get-tuple-element.52), channel_id=1, source_target_pairs={{0,40},{8,48},{16,56},{24,0},{32,8},{40,16},{48,24},{56,32},{1,41}... | collective-permute-start | bytes 221192 | tf_op jit(solution)/shard_map/ppermute | solution.py:624
  107.7 4.0 %collective-permute-start.30 = (bf16[288,128]{1,0:T(8,128)(2,1)S(1)}, bf16[288,128]{1,0:T(8,128)(2,1)S(1)}, u32[]{:S(2)}, u32[]{:S(2)}) collective-permute-start(bf16[288,128]{1,0:T(8,128)(2,1)S(1)} %get-tuple-element.54), channel_id=1, source_target_pairs={{0,48},{8,56},{16,0},{24,8},{32,16},{40,24},{48,32},{56,40},{1,49}... | collective-permute-start | bytes 221192 | tf_op jit(solution)/shard_map/ppermute | solution.py:624
  111.8 0.7 collective-permute-start.31
  112.5 2.5 %collective-permute-start.32 = (bf16[288,128]{1,0:T(8,128)(2,1)S(1)}, bf16[288,128]{1,0:T(8,128)(2,1)S(1)}, u32[]{:S(2)}, u32[]{:S(2)}) collective-permute-start(bf16[288,128]{1,0:T(8,128)(2,1)S(1)} %get-tuple-element.56), channel_id=1, source_target_pairs={{0,56},{8,0},{16,8},{24,16},{32,24},{40,32},{48,40},{56,48},{1,57}... | collective-permute-start | bytes 221192 | tf_op jit(solution)/shard_map/ppermute | solution.py:624
  115.0 0.7 collective-permute-done.29.refs_4_
  116.1 1.4 %collective-permute-done.31.refs_6_ = bf16[288,128]{1,0:T(8,128)(2,1)S(1)} collective-permute-done((bf16[288,128]{1,0:T(8,128)(2,1)S(1)}, bf16[288,128]{1,0:T(8,128)(2,1)S(1)}, u32[]{:S(2)}, u32[]{:S(2)}) %collective-permute-start.31) | collective-permute-done | bytes 73760 | tf_op jit(solution)/shard_map/ppermute | solution.py:624
  117.8 0.9 shard_map.207
  118.8 1.9 %shard_map.208 = (f32[256,256]{1,0:T(8,128)}, f32[256,256]{1,0:T(8,128)}, f32[8,32]{1,0:T(8,128)}, f32[8,32]{1,0:T(8,128)}) custom-call(s32[27]{0:T(128)S(1)} %copy-done.18, bf16[288,128]{1,0:T(8,128)(2,1)S(1)} %get-tuple-element.49.refs_0_, bf16[288,128]{1,0:T(8,128)(2,1)S(1)} %collective-permute-done.26.refs_1_, ...), custom_call_target="tpu_custom_call" | custom-call | flops 1048576 | bytes 1048576 | tf_op jit(solution)/shard_map/pallas_call | solution.py:501
  (88 shorter events, 2.4 us)
Async XLA Ops:
  3.4 9.5 %collective-permute-start.2 = (bf16[416,128]{1,0:T(8,128)(2,1)}, bf16[416,128]{1,0:T(8,128)(2,1)S(1)}, u32[]{:S(2)}, u32[]{:S(2)}) collective-permute-start(bf16[416,128]{1,0:T(8,128)(2,1)} %get-tuple-element.37.refs_0_), channel_id=1, source_target_pairs={{0,2},{2,4},{4,6},{6,0},{1,3},{3,5},{5,7},{7,1},{8,10},{10,12},{12... | collective-permute-start | bytes 319496 | tf_op jit(solution)/shard_map/ppermute | solution.py:575
  5.0 8.5 %collective-permute-start.1 = (bf16[416,128]{1,0:T(8,128)(2,1)}, bf16[416,128]{1,0:T(8,128)(2,1)S(1)}, u32[]{:S(2)}, u32[]{:S(2)}) collective-permute-start(bf16[416,128]{1,0:T(8,128)(2,1)} %get-tuple-element.37.refs_0_), channel_id=1, source_target_pairs={{0,4},{2,6},{4,0},{6,2},{1,5},{3,7},{5,1},{7,3},{8,12},{10,14},{12... | collective-permute-start | bytes 319496 | tf_op jit(solution)/shard_map/ppermute | solution.py:575
  7.9 5.7 %collective-permute-start = (bf16[416,128]{1,0:T(8,128)(2,1)}, bf16[416,128]{1,0:T(8,128)(2,1)S(1)}, u32[]{:S(2)}, u32[]{:S(2)}) collective-permute-start(bf16[416,128]{1,0:T(8,128)(2,1)} %get-tuple-element.37.refs_0_), channel_id=1, source_target_pairs={{0,6},{2,0},{4,2},{6,4},{1,7},{3,1},{5,3},{7,5},{8,14},{10,8},{12,... | collective-permute-start | bytes 319496 | tf_op jit(solution)/shard_map/ppermute | solution.py:575
  9.2 4.8 %collective-permute-start.3 = (bf16[416,128]{1,0:T(8,128)(2,1)}, bf16[416,128]{1,0:T(8,128)(2,1)S(1)}, u32[]{:S(2)}, u32[]{:S(2)}) collective-permute-start(bf16[416,128]{1,0:T(8,128)(2,1)} %get-tuple-element.37.refs_0_), channel_id=1, source_target_pairs={{0,1},{1,0},{2,3},{3,2},{4,5},{5,4},{6,7},{7,6},{8,9},{9,8},{10,11... | collective-permute-start | bytes 319496 | tf_op jit(solution)/shard_map/ppermute | solution.py:49
  9.3 65.4 %copy-start.17 = (s32[27]{0:T(128)}, s32[27]{0:T(128)S(1)}, u32[]{:S(2)}) copy-start(s32[27]{0:T(128)S(1)} %stack.75.spots_ref) | copy-start | bytes 328
  9.3 0.8 copy-start.4
  10.2 4.7 %copy-start.19 = (bf16[416,128]{1,0:T(8,128)(2,1)S(1)}, bf16[416,128]{1,0:T(8,128)(2,1)}, u32[]{:S(2)}) copy-start(bf16[416,128]{1,0:T(8,128)(2,1)} %get-tuple-element.37.refs_0_) | copy-start | bytes 319492
  12.9 1.5 %collective-permute-start.6 = (bf16[416,128]{1,0:T(8,128)(2,1)S(1)}, bf16[416,128]{1,0:T(8,128)(2,1)S(1)}, u32[]{:S(2)}, u32[]{:S(2)}) collective-permute-start(bf16[416,128]{1,0:T(8,128)(2,1)S(1)} %collective-permute-done.2.refs_3_), channel_id=1, source_target_pairs={{0,1},{1,0},{2,3},{3,2},{4,5},{5,4},{6,7},{7,6},{8,9},{9,8},{10,11... | collective-permute-start | bytes 319496 | tf_op jit(solution)/shard_map/ppermute | solution.py:49
  13.4 1.3 %collective-permute-start.5 = (bf16[416,128]{1,0:T(8,128)(2,1)S(1)}, bf16[416,128]{1,0:T(8,128)(2,1)S(1)}, u32[]{:S(2)}, u32[]{:S(2)}) collective-permute-start(bf16[416,128]{1,0:T(8,128)(2,1)S(1)} %collective-permute-done.1.refs_2_), channel_id=1, source_target_pairs={{0,1},{1,0},{2,3},{3,2},{4,5},{5,4},{6,7},{7,6},{8,9},{9,8},{10,11... | collective-permute-start | bytes 319496 | tf_op jit(solution)/shard_map/ppermute | solution.py:49
  13.6 1.4 %collective-permute-start.4 = (bf16[416,128]{1,0:T(8,128)(2,1)S(1)}, bf16[416,128]{1,0:T(8,128)(2,1)S(1)}, u32[]{:S(2)}, u32[]{:S(2)}) collective-permute-start(bf16[416,128]{1,0:T(8,128)(2,1)S(1)} %shard_map.190.refs_1_), channel_id=1, source_target_pairs={{0,1},{1,0},{2,3},{3,2},{4,5},{5,4},{6,7},{7,6},{8,9},{9,8},{10,11... | collective-permute-start | bytes 319496 | tf_op jit(solution)/shard_map/ppermute | solution.py:49
  15.6 13.8 %collective-permute-start.7 = (bf16[2304,128]{1,0:T(8,128)(2,1)S(1)}, bf16[2304,128]{1,0:T(8,128)(2,1)S(1)}, u32[]{:S(2)}, u32[]{:S(2)}) collective-permute-start(bf16[2304,128]{1,0:T(8,128)(2,1)S(1)} %shard_map.191.refs_0_.refs_4_.refs_2_), channel_id=1, source_target_pairs={{0,8},{1,57},{2,10},{3,59},{4,12},{5,61},{6,14},{7,63},{8,16},{9,1... | collective-permute-start | bytes 1769480 | tf_op jit(solution)/shard_map/ppermute | solution.py:588
  17.6 6.7 %copy-start.5 = (bf16[256,128]{1,0:T(8,128)(2,1)S(1)}, bf16[256,128]{1,0:T(8,128)(2,1)}, u32[]{:S(2)}) copy-start(bf16[256,128]{1,0:T(8,128)(2,1)} %get-tuple-element.38.turned_ref) | copy-start | bytes 196612
  17.6 6.7 %collective-permute-start.9 = (bf16[8,256,128]{2,1,0:T(8,128)(2,1)S(1)}, bf16[8,256,128]{2,1,0:T(8,128)(2,1)S(1)}, u32[]{:S(2)}, u32[]{:S(2)}) collective-permute-start(bf16[8,256,128]{2,1,0:T(8,128)(2,1)S(1)} %get-tuple-element.40), channel_id=1, source_target_pairs={{0,1},{1,0},{2,3},{3,2},{4,5},{5,4},{6,7},{7,6},{8,9},{9,8},{10,11... | collective-permute-start | bytes 1572872 | tf_op jit(solution)/shard_map/ppermute | solution.py:49
  21.6 2.7 %collective-permute-start.8 = (bf16[8,256,128]{2,1,0:T(8,128)(2,1)S(1)}, bf16[8,256,128]{2,1,0:T(8,128)(2,1)S(1)}, u32[]{:S(2)}, u32[]{:S(2)}) collective-permute-start(bf16[8,256,128]{2,1,0:T(8,128)(2,1)S(1)} %get-tuple-element.39.refs_1_), channel_id=1, source_target_pairs={{0,1},{1,0},{2,3},{3,2},{4,5},{5,4},{6,7},{7,6},{8,9},{9,8},{10,11... | collective-permute-start | bytes 1572872 | tf_op jit(solution)/shard_map/ppermute | solution.py:49
  24.3 5.1 %copy-start.27 = (bf16[8,256,128]{2,1,0:T(8,128)(2,1)}, bf16[8,256,128]{2,1,0:T(8,128)(2,1)S(1)}, u32[]{:S(2)}) copy-start(bf16[8,256,128]{2,1,0:T(8,128)(2,1)S(1)} %get-tuple-element.47) | copy-start | bytes 1572868
  29.4 11.1 %collective-permute-start.11 = (bf16[2304,128]{1,0:T(8,128)(2,1)S(1)}, bf16[2304,128]{1,0:T(8,128)(2,1)S(1)}, u32[]{:S(2)}, u32[]{:S(2)}) collective-permute-start(bf16[2304,128]{1,0:T(8,128)(2,1)S(1)} %shard_map.195.refs_1_), channel_id=1, source_target_pairs={{0,8},{1,57},{2,10},{3,59},{4,12},{5,61},{6,14},{7,63},{8,16},{9,1... | collective-permute-start | bytes 1769480 | tf_op jit(solution)/shard_map/ppermute | solution.py:590
  29.4 10.4 %collective-permute-start.12 = (bf16[8,256,128]{2,1,0:T(8,128)(2,1)S(1)}, bf16[8,256,128]{2,1,0:T(8,128)(2,1)S(1)}, u32[]{:S(2)}, u32[]{:S(2)}) collective-permute-start(bf16[8,256,128]{2,1,0:T(8,128)(2,1)S(1)} %get-tuple-element.43), channel_id=1, source_target_pairs={{0,2},{1,7},{2,4},{3,1},{4,6},{5,3},{6,0},{7,5},{8,10},{9,15},{10,... | collective-permute-start | bytes 1572872 | tf_op jit(solution)/shard_map/ppermute | solution.py:584
  30.0 16.2 %collective-permute-start.10 = (bf16[2304,128]{1,0:T(8,128)(2,1)S(1)}, bf16[2304,128]{1,0:T(8,128)(2,1)S(1)}, u32[]{:S(2)}, u32[]{:S(2)}) collective-permute-start(bf16[2304,128]{1,0:T(8,128)(2,1)S(1)} %shard_map.195.refs_1_), channel_id=1, source_target_pairs={{0,1},{1,0},{2,3},{3,2},{4,5},{5,4},{6,7},{7,6},{8,9},{9,8},{10,11... | collective-permute-start | bytes 1769480 | tf_op jit(solution)/shard_map/ppermute | solution.py:49
  40.5 11.1 %collective-permute-start.14 = (bf16[2304,128]{1,0:T(8,128)(2,1)S(1)}, bf16[2304,128]{1,0:T(8,128)(2,1)S(1)}, u32[]{:S(2)}, u32[]{:S(2)}) collective-permute-start(bf16[2304,128]{1,0:T(8,128)(2,1)S(1)} %shard_map.197.refs_1_.refs_3_), channel_id=1, source_target_pairs={{0,8},{1,57},{2,10},{3,59},{4,12},{5,61},{6,14},{7,63},{8,16},{9,1... | collective-permute-start | bytes 1769480 | tf_op jit(solution)/shard_map/ppermute | solution.py:596
  40.5 3.6 %collective-permute-start.15 = (bf16[8,256,128]{2,1,0:T(8,128)(2,1)S(1)}, bf16[8,256,128]{2,1,0:T(8,128)(2,1)S(1)}, u32[]{:S(2)}, u32[]{:S(2)}) collective-permute-start(bf16[8,256,128]{2,1,0:T(8,128)(2,1)S(1)} %get-tuple-element.42.refs_2_), channel_id=1, source_target_pairs={{0,1},{1,0},{2,3},{3,2},{4,5},{5,4},{6,7},{7,6},{8,9},{9,8},{10,11... | collective-permute-start | bytes 1572872 | tf_op jit(solution)/shard_map/ppermute | solution.py:49
  41.8 15.6 %collective-permute-start.13 = (bf16[2304,128]{1,0:T(8,128)(2,1)S(1)}, bf16[2304,128]{1,0:T(8,128)(2,1)}, u32[]{:S(2)}, u32[]{:S(2)}) collective-permute-start(bf16[2304,128]{1,0:T(8,128)(2,1)S(1)} %shard_map.197.refs_1_.refs_3_), channel_id=1, source_target_pairs={{0,1},{1,0},{2,3},{3,2},{4,5},{5,4},{6,7},{7,6},{8,9},{9,8},{10,11... | collective-permute-start | bytes 1769480 | tf_op jit(solution)/shard_map/ppermute | solution.py:49
  41.8 15.6 %collective-permute-start.19 = (bf16[8,256,128]{2,1,0:T(8,128)(2,1)}, bf16[8,256,128]{2,1,0:T(8,128)(2,1)}, u32[]{:S(2)}, u32[]{:S(2)}) collective-permute-start(bf16[8,256,128]{2,1,0:T(8,128)(2,1)} %get-tuple-element.41.refs_1_), channel_id=1, source_target_pairs={{0,2},{1,7},{2,4},{3,1},{4,6},{5,3},{6,0},{7,5},{8,10},{9,15},{10,... | collective-permute-start | bytes 1572872 | tf_op jit(solution)/shard_map/ppermute | solution.py:585
  46.3 5.3 %copy-start.3 = (bf16[8,256,128]{2,1,0:T(8,128)(2,1)}, bf16[8,256,128]{2,1,0:T(8,128)(2,1)S(1)}, u32[]{:S(2)}) copy-start(bf16[8,256,128]{2,1,0:T(8,128)(2,1)S(1)} %shard_map.199.refs_1_) | copy-start | bytes 1572868
  46.3 2.5 %copy-start.1 = (bf16[2304,128]{1,0:T(8,128)(2,1)}, bf16[2304,128]{1,0:T(8,128)(2,1)S(1)}, u32[]{:S(2)}) copy-start(bf16[2304,128]{1,0:T(8,128)(2,1)S(1)} %collective-permute-done.10.refs_2_) | copy-start | bytes 1769476
  48.8 2.8 %copy-start.6 = (f32[128,256]{1,0:T(8,128)}, f32[128,256]{1,0:T(8,128)S(1)}, u32[]{:S(2)}) copy-start(f32[128,256]{1,0:T(8,128)S(1)} %shard_map.196.refs_0_.refs_2_) | copy-start | bytes 393220
  51.6 9.7 %collective-permute-start.16 = (bf16[2304,128]{1,0:T(8,128)(2,1)S(1)}, bf16[2304,128]{1,0:T(8,128)(2,1)}, u32[]{:S(2)}, u32[]{:S(2)}) collective-permute-start(bf16[2304,128]{1,0:T(8,128)(2,1)S(1)} %shard_map.200.refs_1_.refs_5_), channel_id=1, source_target_pairs={{0,1},{1,0},{2,3},{3,2},{4,5},{5,4},{6,7},{7,6},{8,9},{9,8},{10,11... | collective-permute-start | bytes 1769480 | tf_op jit(solution)/shard_map/ppermute | solution.py:49
  51.6 14.2 %collective-permute-start.17 = (bf16[2304,128]{1,0:T(8,128)(2,1)S(1)}, bf16[2304,128]{1,0:T(8,128)(2,1)S(1)}, u32[]{:S(2)}, u32[]{:S(2)}) collective-permute-start(bf16[2304,128]{1,0:T(8,128)(2,1)S(1)} %shard_map.200.refs_1_.refs_5_), channel_id=1, source_target_pairs={{0,8},{1,57},{2,10},{3,59},{4,12},{5,61},{6,14},{7,63},{8,16},{9,1... | collective-permute-start | bytes 1769480 | tf_op jit(solution)/shard_map/ppermute | solution.py:600
  51.7 14.1 %all-to-all-start = ((bf16[4,2,128,256]{3,2,1,0:T(8,128)(2,1)}), bf16[4,2,128,256]{3,2,1,0:T(8,128)(2,1)S(1)}, u32[]{:S(2)}, u32[]{:S(2)}) async-start(bf16[4,2,128,256]{3,2,1,0:T(8,128)(2,1)} %get-tuple-element.44), calls=%async_computation | async-start | bytes 1048576 | tf_op jit(solution)/shard_map/all_to_all | solution.py:578
  56.5 37.3 %collective-permute-start.18 = (bf16[8,256,128]{2,1,0:T(8,128)(2,1)}, bf16[8,256,128]{2,1,0:T(8,128)(2,1)}, u32[]{:S(2)}, u32[]{:S(2)}) collective-permute-start(bf16[8,256,128]{2,1,0:T(8,128)(2,1)} %copy-done.27), channel_id=1, source_target_pairs={{0,1},{1,0},{2,3},{3,2},{4,5},{5,4},{6,7},{7,6},{8,9},{9,8},{10,11... | collective-permute-start | bytes 1572872 | tf_op jit(solution)/shard_map/ppermute | solution.py:49
  57.4 36.4 %collective-permute-start.20 = (bf16[8,256,128]{2,1,0:T(8,128)(2,1)}, bf16[8,256,128]{2,1,0:T(8,128)(2,1)}, u32[]{:S(2)}, u32[]{:S(2)}) collective-permute-start(bf16[8,256,128]{2,1,0:T(8,128)(2,1)} %collective-permute-done.19), channel_id=1, source_target_pairs={{0,1},{1,0},{2,3},{3,2},{4,5},{5,4},{6,7},{7,6},{8,9},{9,8},{10,11... | collective-permute-start | bytes 1572872 | tf_op jit(solution)/shard_map/ppermute | solution.py:49
  57.4 36.4 %collective-permute-start.21 = (bf16[8,256,128]{2,1,0:T(8,128)(2,1)}, bf16[8,256,128]{2,1,0:T(8,128)(2,1)}, u32[]{:S(2)}, u32[]{:S(2)}) collective-permute-start(bf16[8,256,128]{2,1,0:T(8,128)(2,1)} %copy-done.3), channel_id=1, source_target_pairs={{0,2},{1,7},{2,4},{3,1},{4,6},{5,3},{6,0},{7,5},{8,10},{9,15},{10,... | collective-permute-start | bytes 1572872 | tf_op jit(solution)/shard_map/ppermute | solution.py:592
  57.7 0.9 copy-start.7
  61.2 5.6 %copy-start.22 = (s32[128]{0:T(128)S(1)}, s32[128]{0:T(128)}, u32[]{:S(2)}) copy-start(s32[128]{0:T(128)} %param.18) | copy-start | bytes 1540
  63.8 0.7 copy-start.8
  65.7 15.2 %copy-start = (bf16[4,2,128,256]{3,2,1,0:T(8,128)(2,1)}, bf16[4,2,128,256]{3,2,1,0:T(8,128)(2,1)S(1)}, u32[]{:S(2)}) copy-start(bf16[4,2,128,256]{3,2,1,0:T(8,128)(2,1)S(1)} %all-to-all-done.refs_2_.refs_1_) | copy-start | bytes 1572868
  65.7 1.0 copy-start.9
  66.8 1.1 copy-start.2
  68.8 0.6 copy-start.13
  69.4 0.6 copy-start.25
  70.0 10.9 %all-to-all-start.1 = ((bf16[4,80,128]{2,1,0:T(8,128)(2,1)}), bf16[4,80,128]{2,1,0:T(8,128)(2,1)S(1)}, u32[]{:S(2)}, u32[]{:S(2)}) async-start(bf16[4,80,128]{2,1,0:T(8,128)(2,1)} %copy-done.13), calls=%async_computation.1 | async-start | bytes 163840 | tf_op jit(solution)/shard_map/all_to_all | solution.py:607
  74.7 0.9 copy-start.10
  75.6 0.9 copy-start.11
  76.6 0.9 copy-start.14
  77.5 0.7 copy-start.26
  78.2 39.6 %copy-start.12 = (bf16[256,16,32]{0,2,1:T(8,128)(2,1)S(1)}, bf16[256,16,32]{0,2,1:T(8,128)(2,1)}, u32[]{:S(2)}) copy-start(bf16[256,16,32]{0,2,1:T(8,128)(2,1)} %param.16) | copy-start | bytes 786436
  78.2 40.6 %copy-start.23 = (f32[8,32]{1,0:T(8,128)S(1)}, f32[8,32]{1,0:T(8,128)}, u32[]{:S(2)}) copy-start(f32[8,32]{1,0:T(8,128)} %refs_12_.1) | copy-start | bytes 3076
  78.2 40.6 %copy-start.24 = (f32[8,32]{1,0:T(8,128)S(1)}, f32[8,32]{1,0:T(8,128)}, u32[]{:S(2)}) copy-start(f32[8,32]{1,0:T(8,128)} %refs_13_.1) | copy-start | bytes 3076
  80.9 0.6 copy-start.28
  83.9 34.9 %copy-start.15 = (f32[256,256]{1,0:T(8,128)S(1)}, f32[256,256]{1,0:T(8,128)}, u32[]{:S(2)}) copy-start(f32[256,256]{1,0:T(8,128)} %get-tuple-element.58.refs_8_) | copy-start | bytes 786436
  83.9 34.9 %copy-start.16 = (f32[256,256]{1,0:T(8,128)S(1)}, f32[256,256]{1,0:T(8,128)}, u32[]{:S(2)}) copy-start(f32[256,256]{1,0:T(8,128)} %get-tuple-element.59.refs_9_) | copy-start | bytes 786436
  83.9 1.5 %collective-permute-start.22 = (f32[8,256]{1,0:T(8,128)}, f32[8,256]{1,0:T(8,128)S(1)}, u32[]{:S(2)}, u32[]{:S(2)}) collective-permute-start(f32[8,256]{1,0:T(8,128)} %get-tuple-element.48), channel_id=1, source_target_pairs={{0,1},{1,0},{2,3},{3,2},{4,5},{5,4},{6,7},{7,6},{8,9},{9,8},{10,11... | collective-permute-start | bytes 24584 | tf_op jit(solution)/shard_map/ppermute | solution.py:49
  86.0 0.9 collective-permute-start.24
  86.7 3.7 %collective-permute-start.23 = (f32[8,256]{1,0:T(8,128)S(1)}, f32[8,256]{1,0:T(8,128)S(1)}, u32[]{:S(2)}, u32[]{:S(2)}) collective-permute-start(f32[8,256]{1,0:T(8,128)S(1)} %add.83), channel_id=1, source_target_pairs={{0,2},{1,5},{2,0},{3,7},{4,6},{5,1},{6,4},{7,3},{8,10},{9,13},{10,... | collective-permute-start | bytes 24584 | tf_op jit(solution)/shard_map/ppermute | solution.py:530
  90.4 4.2 %collective-permute-start.25 = (f32[8,256]{1,0:T(8,128)S(1)}, f32[8,256]{1,0:T(8,128)S(1)}, u32[]{:S(2)}, u32[]{:S(2)}) collective-permute-start(f32[8,256]{1,0:T(8,128)S(1)} %add_select_fusion.p_ref), channel_id=1, source_target_pairs={{0,1},{1,0},{2,3},{3,2},{4,5},{5,4},{6,7},{7,6},{8,9},{9,8},{10,11... | collective-permute-start | bytes 24584 | tf_op jit(solution)/shard_map/ppermute | solution.py:49
  94.6 0.7 copy-start.18
  95.3 23.4 %copy-start.20 = (f32[8,256]{1,0:T(8,128)S(1)}, f32[8,256]{1,0:T(8,128)}, u32[]{:S(2)}) copy-start(f32[8,256]{1,0:T(8,128)} %get-tuple-element.33.refs_10_) | copy-start | bytes 24580
  95.3 23.4 %copy-start.21 = (f32[8,256]{1,0:T(8,128)S(1)}, f32[8,256]{1,0:T(8,128)}, u32[]{:S(2)}) copy-start(f32[8,256]{1,0:T(8,128)} %get-tuple-element.36.refs_11_) | copy-start | bytes 24580
  97.9 13.8 %collective-permute-start.26 = (bf16[288,128]{1,0:T(8,128)(2,1)S(1)}, bf16[288,128]{1,0:T(8,128)(2,1)S(1)}, u32[]{:S(2)}, u32[]{:S(2)}) collective-permute-start(bf16[288,128]{1,0:T(8,128)(2,1)S(1)} %get-tuple-element.50), channel_id=1, source_target_pairs={{0,32},{8,40},{16,48},{24,56},{32,0},{40,8},{48,16},{56,24},{1,33}... | collective-permute-start | bytes 221192 | tf_op jit(solution)/shard_map/ppermute | solution.py:624
  102.6 9.9 %collective-permute-start.27 = (bf16[288,128]{1,0:T(8,128)(2,1)S(1)}, bf16[288,128]{1,0:T(8,128)(2,1)S(1)}, u32[]{:S(2)}, u32[]{:S(2)}) collective-permute-start(bf16[288,128]{1,0:T(8,128)(2,1)S(1)} %get-tuple-element.51), channel_id=1, source_target_pairs={{0,24},{8,32},{16,40},{24,48},{32,56},{40,0},{48,8},{56,16},{1,25}... | collective-permute-start | bytes 221192 | tf_op jit(solution)/shard_map/ppermute | solution.py:624
  104.1 11.0 %collective-permute-start.28 = (bf16[288,128]{1,0:T(8,128)(2,1)S(1)}, bf16[288,128]{1,0:T(8,128)(2,1)S(1)}, u32[]{:S(2)}, u32[]{:S(2)}) collective-permute-start(bf16[288,128]{1,0:T(8,128)(2,1)S(1)} %get-tuple-element.52), channel_id=1, source_target_pairs={{0,40},{8,48},{16,56},{24,0},{32,8},{40,16},{48,24},{56,32},{1,41}... | collective-permute-start | bytes 221192 | tf_op jit(solution)/shard_map/ppermute | solution.py:624
  107.6 8.1 %collective-permute-start.29 = (bf16[288,128]{1,0:T(8,128)(2,1)S(1)}, bf16[288,128]{1,0:T(8,128)(2,1)S(1)}, u32[]{:S(2)}, u32[]{:S(2)}) collective-permute-start(bf16[288,128]{1,0:T(8,128)(2,1)S(1)} %get-tuple-element.53), channel_id=1, source_target_pairs={{0,16},{8,24},{16,32},{24,40},{32,48},{40,56},{48,0},{56,8},{1,17}... | collective-permute-start | bytes 221192 | tf_op jit(solution)/shard_map/ppermute | solution.py:624
  107.7 8.4 %collective-permute-start.30 = (bf16[288,128]{1,0:T(8,128)(2,1)S(1)}, bf16[288,128]{1,0:T(8,128)(2,1)S(1)}, u32[]{:S(2)}, u32[]{:S(2)}) collective-permute-start(bf16[288,128]{1,0:T(8,128)(2,1)S(1)} %get-tuple-element.54), channel_id=1, source_target_pairs={{0,48},{8,56},{16,0},{24,8},{32,16},{40,24},{48,32},{56,40},{1,49}... | collective-permute-start | bytes 221192 | tf_op jit(solution)/shard_map/ppermute | solution.py:624
  111.8 5.7 %collective-permute-start.31 = (bf16[288,128]{1,0:T(8,128)(2,1)S(1)}, bf16[288,128]{1,0:T(8,128)(2,1)S(1)}, u32[]{:S(2)}, u32[]{:S(2)}) collective-permute-start(bf16[288,128]{1,0:T(8,128)(2,1)S(1)} %get-tuple-element.55), channel_id=1, source_target_pairs={{0,8},{8,16},{16,24},{24,32},{32,40},{40,48},{48,56},{56,0},{1,9},... | collective-permute-start | bytes 221192 | tf_op jit(solution)/shard_map/ppermute | solution.py:624
  112.5 5.3 %collective-permute-start.32 = (bf16[288,128]{1,0:T(8,128)(2,1)S(1)}, bf16[288,128]{1,0:T(8,128)(2,1)S(1)}, u32[]{:S(2)}, u32[]{:S(2)}) collective-permute-start(bf16[288,128]{1,0:T(8,128)(2,1)S(1)} %get-tuple-element.56), channel_id=1, source_target_pairs={{0,56},{8,0},{16,8},{24,16},{32,24},{40,32},{48,40},{56,48},{1,57}... | collective-permute-start | bytes 221192 | tf_op jit(solution)/shard_map/ppermute | solution.py:624

commit v3 on v2

--- a/solution.py
+++ b/solution.py
@@ -590,16 +590,16 @@
     two = lax.ppermute(one, F, Z_BY_CORE)
     (t_near,) = part_kernel(w5, turned, spots, 6, [[r_near, g_two]], [])
     g_near = lax.ppermute(t_near, F, Y_BY_CORE)
-    two = tied(two, g_two, frozen_zero)
+    two = tied(two, t_near, frozen_zero)
     two_o = swap(two)
     frozen_one = frozen_kernel(w4, spots, frozen_zero, [one, one_o], [20, 21])
     three = lax.ppermute(two, F, Z_BY_CORE)
-    three = tied(three, t_near, frozen_one)
+    three = tied(three, frozen_one, boths)
     three_o = swap(three)
     frozen_two = frozen_kernel(w4, spots, frozen_one, [two, two_o], [22, 23])
     four = lax.ppermute(three, F, Z_BY_CORE)
     frozen_three = frozen_kernel(w4, spots, frozen_two, [three, three_o], [24, 25])
-    four = tied(four, frozen_three, boths)
+    four = tied(four, frozen_three)
 
     small, back, scale = small_kernel(
         spots, [block, one, one_o, two, two_o, three, three_o, four], tenant

time: 122 us -> 122 us (level)
  waiting for transfers between devices: 22.6 us -> 30.2 us
  local copies, waits for them, and re-layouts: 10.6 us -> 6.56 us
  starting transfers between devices: 50.3 us -> 46.5 us
    ppermute x7, waiting for transfers between devices: 2.78 us -> 7.61 us  [on_device(): pieces.append(lax.ppermute(piece, 'z', turn(NZ, k)))]
    ppermute x7, starting transfers between devices: 17.1 us -> 12.7 us  [on_device(): pieces.append(lax.ppermute(piece, 'z', turn(NZ, k)))]
    unnamed x58 -> x52, local copies, waits for them, and re-layouts: 10.5 us -> 6.46 us
    ppermute x1, waiting for transfers between devices: 2.79 us -> 0.01 us  [on_device(): three = lax.ppermute(two, F, Z_BY_CORE)]
    ppermute x1, waiting for transfers between devices: 0.01 us -> 2.28 us  [on_device(): four = lax.ppermute(three, F, Z_BY_CORE)]
    all_to_all x1, waiting for transfers between devices: 1.23 us -> 3.36 us  [on_device(): boths = lax.all_to_all(both, 'dp', 0, 0, tiled=True)]
    ppermute x1, waiting for transfers between devices: 4.88 us -> 7.01 us  [on_device(): g_two = lax.ppermute(t_two, F, Y_BY_CORE)]
    ppermute x14, waiting for transfers between devices: 5.03 us -> 3.16 us  [swap(): return lax.ppermute(v, 'core', turn(NC, 1))]
  transfers between devices with their start and end apart: 35 -> 35, of which waited for: 16 -> 15; matrix products, arithmetic and copies ran while one was open for 1% -> 1% of each run, Pallas kernels for 22% -> 22%
where the time goes in v3:
time: 122 us; the launch traced here: 120 us
  starting transfers between devices  46.5 us (38%)
  Pallas kernels  34.7 us (28%)
  waiting for transfers between devices  30.2 us (25%)
  local copies, waits for them, and re-layouts  6.56 us (5%)
  between operations  1.68 us (1%)
    ppermute x14, starting transfers between devices, swap(): return lax.ppermute(v, 'core', turn(NC, 1))  13.8 us
    ppermute x7, starting transfers between devices, on_device(): pieces.append(lax.ppermute(piece, 'z', turn(NZ, k)))  12.7 us
    pallas_call x4, Pallas kernels, part_kernel(): pl.pallas_call(functools.partial(part_body, [len(a) for a in adds]), grid...  10.2 us
    pallas_call x4, Pallas kernels, frozen_kernel(): pl.pallas_call(functools.partial(frozen_body, n, has_acc), grid_spec=pltp...  9.6 us
    ppermute x7, waiting for transfers between devices, on_device(): pieces.append(lax.ppermute(piece, 'z', turn(NZ, k)))  7.61 us
    ppermute x1, waiting for transfers between devices, on_device(): g_two = lax.ppermute(t_two, F, Y_BY_CORE)  7.01 us
    unnamed x52, local copies, waits for them, and re-layouts  6.46 us
    ppermute x3, starting transfers between devices, on_device(): lax.ppermute(message, 'y', turn(NY, k))  5.82 us
  transfers between devices with their start and end apart: 35, of which 15 were waited for; matrix products, arithmetic and copies ran while one was open for 1% of the time, Pallas kernels for 22%

profile of v3, /device:TPU:2, one launch (start us, length us, event | category | flops | bytes accessed | tf_op | source)
XLA Modules:
  0.0 120.4 jit_solution(12601833911595236200)
XLA Ops:
  1.3 2.1 %shard_map.188 = (bf16[416,128]{1,0:T(8,128)(2,1)}, bf16[4,2,128,256]{3,2,1,0:T(8,128)(2,1)}, bf16[256,128]{1,0:T(8,128)(2,1)}) custom-call(s32[1]{0:T(128)S(6)} %copy.31.live_ref, bf16[128,256]{1,0:T(8,128)(2,1)} %x_ref.1, bf16[256]{0:T(256)(128)(2,1)} %gain_ref.1, bf16[128,256]{1,0:T(8,128)(2,1)} %cot_ref.1, bf16[512,256]{1,0:T(8,128)(2,1)} %bitcast.28, ...), custom_call_target="tpu_custom_call" | custom-call | flops 67108864 | bytes 1048576 | tf_op jit(solution)/shard_map/pallas_call | solution.py:124
  3.4 1.6 %collective-permute-start.2 = (bf16[416,128]{1,0:T(8,128)(2,1)}, bf16[416,128]{1,0:T(8,128)(2,1)S(1)}, u32[]{:S(2)}, u32[]{:S(2)}) collective-permute-start(bf16[416,128]{1,0:T(8,128)(2,1)} %get-tuple-element.37.refs_0_), channel_id=1, source_target_pairs={{0,2},{2,4},{4,6},{6,0},{1,3},{3,5},{5,7},{7,1},{8,10},{10,12},{12... | collective-permute-start | bytes 319496 | tf_op jit(solution)/shard_map/ppermute | solution.py:575
  5.0 2.9 %collective-permute-start.1 = (bf16[416,128]{1,0:T(8,128)(2,1)}, bf16[416,128]{1,0:T(8,128)(2,1)S(1)}, u32[]{:S(2)}, u32[]{:S(2)}) collective-permute-start(bf16[416,128]{1,0:T(8,128)(2,1)} %get-tuple-element.37.refs_0_), channel_id=1, source_target_pairs={{0,4},{2,6},{4,0},{6,2},{1,5},{3,7},{5,1},{7,3},{8,12},{10,14},{12... | collective-permute-start | bytes 319496 | tf_op jit(solution)/shard_map/ppermute | solution.py:575
  7.9 1.3 %collective-permute-start = (bf16[416,128]{1,0:T(8,128)(2,1)}, bf16[416,128]{1,0:T(8,128)(2,1)S(1)}, u32[]{:S(2)}, u32[]{:S(2)}) collective-permute-start(bf16[416,128]{1,0:T(8,128)(2,1)} %get-tuple-element.37.refs_0_), channel_id=1, source_target_pairs={{0,6},{2,0},{4,2},{6,4},{1,7},{3,1},{5,3},{7,5},{8,14},{10,8},{12,... | collective-permute-start | bytes 319496 | tf_op jit(solution)/shard_map/ppermute | solution.py:575
  9.2 0.1 stack.75.spots_ref
  9.3 0.8 copy-done.4
  10.2 2.7 %shard_map.189 = (bf16[8,256,128]{2,1,0:T(8,128)(2,1)S(1)}, bf16[8,256,128]{2,1,0:T(8,128)(2,1)S(1)}) custom-call(s32[27]{0:T(128)S(1)} %stack.75.spots_ref, bf16[256,128]{1,0:T(8,128)(2,1)S(1)} %copy-done.4, bf16[8,4,2,256,256]{4,3,2,1,0:T(8,128)(2,1)} %bitcast.34, bf16[8,4,2,256,256]{4,3,2,1,0:T(8,128)(2,1)} %bitcast.35), custom_call_target="tpu_custom_call" | custom-call | flops 268435456 | bytes 4194304 | tf_op jit(solution)/shard_map/pallas_call | solution.py:166
  12.9 0.6 collective-permute-start.6
  13.4 0.1 collective-permute-start.5
  13.6 0.4 collective-permute-start.4
  14.0 0.4 collective-permute-done.6.refs_7_
  14.4 0.4 collective-permute-done.5.refs_6_
  14.8 0.2 collective-permute-done.4.refs_5_
  14.9 0.6 shard_map.191.refs_0_.refs_4_.refs_2_
  15.6 2.0 %collective-permute-start.7 = (bf16[2304,128]{1,0:T(8,128)(2,1)S(1)}, bf16[2304,128]{1,0:T(8,128)(2,1)S(1)}, u32[]{:S(2)}, u32[]{:S(2)}) collective-permute-start(bf16[2304,128]{1,0:T(8,128)(2,1)S(1)} %shard_map.191.refs_0_.refs_4_.refs_2_), channel_id=1, source_target_pairs={{0,8},{1,57},{2,10},{3,59},{4,12},{5,61},{6,14},{7,63},{8,16},{9,1... | collective-permute-start | bytes 1769480 | tf_op jit(solution)/shard_map/ppermute | solution.py:588
  17.6 4.0 %collective-permute-start.9 = (bf16[8,256,128]{2,1,0:T(8,128)(2,1)S(1)}, bf16[8,256,128]{2,1,0:T(8,128)(2,1)S(1)}, u32[]{:S(2)}, u32[]{:S(2)}) collective-permute-start(bf16[8,256,128]{2,1,0:T(8,128)(2,1)S(1)} %get-tuple-element.40), channel_id=1, source_target_pairs={{0,1},{1,0},{2,3},{3,2},{4,5},{5,4},{6,7},{7,6},{8,9},{9,8},{10,11... | collective-permute-start | bytes 1572872 | tf_op jit(solution)/shard_map/ppermute | solution.py:49
  21.6 2.7 %shard_map.194 = (bf16[8,256,128]{2,1,0:T(8,128)(2,1)S(1)}, bf16[8,256,128]{2,1,0:T(8,128)(2,1)S(1)}) custom-call(s32[27]{0:T(128)S(1)} %stack.75.spots_ref, bf16[256,128]{1,0:T(8,128)(2,1)S(1)} %copy-done.4, bf16[8,4,2,256,256]{4,3,2,1,0:T(8,128)(2,1)} %bitcast.36, bf16[8,4,2,256,256]{4,3,2,1,0:T(8,128)(2,1)} %bitcast.37, ...), custom_call_target="tpu_custom_call" | custom-call | flops 268435456 | bytes 4194304 | tf_op jit(solution)/shard_map/pallas_call | solution.py:166
  24.3 2.7 %shard_map.193 = (bf16[8,256,128]{2,1,0:T(8,128)(2,1)S(1)}, bf16[8,256,128]{2,1,0:T(8,128)(2,1)S(1)}) custom-call(s32[27]{0:T(128)S(1)} %stack.75.spots_ref, bf16[256,128]{1,0:T(8,128)(2,1)S(1)} %copy-done.5, bf16[8,4,2,256,256]{4,3,2,1,0:T(8,128)(2,1)} %bitcast.38, bf16[8,4,2,256,256]{4,3,2,1,0:T(8,128)(2,1)} %bitcast.39, ...), custom_call_target="tpu_custom_call" | custom-call | flops 268435456 | bytes 4194304 | tf_op jit(solution)/shard_map/pallas_call | solution.py:166
  27.0 2.4 %collective-permute-done.7.refs_0_ = bf16[2304,128]{1,0:T(8,128)(2,1)S(1)} collective-permute-done((bf16[2304,128]{1,0:T(8,128)(2,1)S(1)}, bf16[2304,128]{1,0:T(8,128)(2,1)S(1)}, u32[]{:S(2)}, u32[]{:S(2)}) %collective-permute-start.7) | collective-permute-done | bytes 589856 | tf_op jit(solution)/shard_map/ppermute | solution.py:588
  29.4 2.2 %collective-permute-start.12 = (bf16[8,256,128]{2,1,0:T(8,128)(2,1)S(1)}, bf16[8,256,128]{2,1,0:T(8,128)(2,1)S(1)}, u32[]{:S(2)}, u32[]{:S(2)}) collective-permute-start(bf16[8,256,128]{2,1,0:T(8,128)(2,1)S(1)} %get-tuple-element.42.refs_2_), channel_id=1, source_target_pairs={{0,1},{1,0},{2,3},{3,2},{4,5},{5,4},{6,7},{7,6},{8,9},{9,8},{10,11... | collective-permute-start | bytes 1572872 | tf_op jit(solution)/shard_map/ppermute | solution.py:49
  31.5 0.7 collective-permute-start.13
  32.2 0.6 collective-permute-start.10
  32.8 2.1 %shard_map.192.refs_0_.refs_2_ = f32[128,256]{1,0:T(8,128)S(1)} custom-call(s32[27]{0:T(128)S(1)} %stack.75.spots_ref, bf16[2304,128]{1,0:T(8,128)(2,1)S(1)} %shard_map.191.refs_0_.refs_4_.refs_2_, bf16[8,8,256,256]{3,2,1,0:T(8,128)(2,1)} %bitcast.40), custom_call_target="tpu_custom_call" | custom-call | flops 134217728 | bytes 9437184 | tf_op jit(solution)/shard_map/pallas_call | solution.py:290
  34.9 7.0 %collective-permute-done.13.refs_2_ = bf16[8,256,128]{2,1,0:T(8,128)(2,1)S(1)} collective-permute-done((bf16[8,256,128]{2,1,0:T(8,128)(2,1)S(1)}, bf16[8,256,128]{2,1,0:T(8,128)(2,1)S(1)}, u32[]{:S(2)}, u32[]{:S(2)}) %collective-permute-start.13) | collective-permute-done | bytes 524320 | tf_op jit(solution)/shard_map/ppermute | solution.py:584
  41.9 2.2 %shard_map.197.refs_1_ = bf16[8,256,128]{2,1,0:T(8,128)(2,1)S(1)} custom-call(s32[27]{0:T(128)S(1)} %stack.75.spots_ref, bf16[256,128]{1,0:T(8,128)(2,1)S(1)} %copy-done.5, bf16[8,4,2,256,256]{4,3,2,1,0:T(8,128)(2,1)} %bitcast.41, bf16[8,256,128]{2,1,0:T(8,128)(2,1)S(1)} %collective-permute-done.12.refs_1_, ...), custom_call_target="tpu_custom_call" | custom-call | flops 134217728 | bytes 2097152 | tf_op jit(solution)/shard_map/pallas_call | solution.py:166
  44.2 0.8 copy-done.3
  45.0 4.8 %all-to-all-start = ((bf16[4,2,128,256]{3,2,1,0:T(8,128)(2,1)}), bf16[4,2,128,256]{3,2,1,0:T(8,128)(2,1)S(1)}, u32[]{:S(2)}, u32[]{:S(2)}) async-start(bf16[4,2,128,256]{3,2,1,0:T(8,128)(2,1)} %get-tuple-element.44), calls=%async_computation | async-start | bytes 1048576 | tf_op jit(solution)/shard_map/all_to_all | solution.py:578
  49.8 0.9 copy-done.10
  50.7 2.4 %shard_map.196.refs_0_.refs_1_ = f32[128,256]{1,0:T(8,128)S(1)} custom-call(s32[27]{0:T(128)S(1)} %stack.75.spots_ref, f32[128,256]{1,0:T(8,128)S(1)} %copy-done.10, bf16[2304,128]{1,0:T(8,128)(2,1)S(1)} %shard_map.195.refs_1_, bf16[2304,128]{1,0:T(8,128)(2,1)S(1)} %collective-permute-done.10.refs_2_, bf16[8,8,256,256]{3,2,1,0:T(8,128)(2,1)} %bitcast.42, ...), custom_call_target="tpu_custom_call" | custom-call | flops 268435456 | bytes 9437184 | tf_op jit(solution)/shard_map/pallas_call | solution.py:290
  53.2 0.6 copy-done.6
  53.8 3.4 %all-to-all-done.refs_2_.refs_1_ = bf16[4,2,128,256]{3,2,1,0:T(8,128)(2,1)S(1)} async-done(((bf16[4,2,128,256]{3,2,1,0:T(8,128)(2,1)}), bf16[4,2,128,256]{3,2,1,0:T(8,128)(2,1)S(1)}, u32[]{:S(2)}, u32[]{:S(2)}) %all-to-all-start) | async-done | bytes 524320 | tf_op jit(solution)/shard_map/all_to_all | solution.py:578
  57.2 1.0 copy-done.7
  58.2 0.4 collective-permute-start.17
  58.7 2.2 %collective-permute-start.18 = (bf16[8,256,128]{2,1,0:T(8,128)(2,1)}, bf16[8,256,128]{2,1,0:T(8,128)(2,1)}, u32[]{:S(2)}, u32[]{:S(2)}) collective-permute-start(bf16[8,256,128]{2,1,0:T(8,128)(2,1)} %copy-done.24), channel_id=1, source_target_pairs={{0,1},{1,0},{2,3},{3,2},{4,5},{5,4},{6,7},{7,6},{8,9},{9,8},{10,11... | collective-permute-start | bytes 1572872 | tf_op jit(solution)/shard_map/ppermute | solution.py:49
  61.0 0.9 copy-done.8
  61.9 2.6 %shard_map.199.refs_0_ = f32[128,256]{1,0:T(8,128)S(1)} custom-call(s32[27]{0:T(128)S(1)} %stack.75.spots_ref, f32[128,256]{1,0:T(8,128)S(1)} %copy-done.8, bf16[2304,128]{1,0:T(8,128)(2,1)S(1)} %shard_map.198.refs_1_.refs_3_, bf16[2304,128]{1,0:T(8,128)(2,1)} %collective-permute-done.14.refs_2_.refs_4_, bf16[8,8,256,256]{3,2,1,0:T(8,128)(2,1)} %bitcast.44, ...), custom_call_target="tpu_custom_call" | custom-call | flops 268435456 | bytes 9437184 | tf_op jit(solution)/shard_map/pallas_call | solution.py:290
  64.6 2.5 %shard_map.201.refs_1_.acc_ref = f32[128,256]{1,0:T(8,128)S(1)} custom-call(s32[27]{0:T(128)S(1)} %stack.75.spots_ref, f32[128,256]{1,0:T(8,128)S(1)} %shard_map.199.refs_0_, bf16[2304,128]{1,0:T(8,128)(2,1)S(1)} %shard_map.200.refs_1_.refs_5_, bf16[2304,128]{1,0:T(8,128)(2,1)S(1)} %collective-permute-done.16.refs_2_.refs_6_, ...), custom_call_target="tpu_custom_call" | custom-call | flops 268435456 | bytes 9437184 | tf_op jit(solution)/shard_map/pallas_call | solution.py:290
  67.0 2.3 %collective-permute-done.17.refs_0_ = bf16[2304,128]{1,0:T(8,128)(2,1)S(1)} collective-permute-done((bf16[2304,128]{1,0:T(8,128)(2,1)S(1)}, bf16[2304,128]{1,0:T(8,128)(2,1)S(1)}, u32[]{:S(2)}, u32[]{:S(2)}) %collective-permute-start.17) | collective-permute-done | bytes 589856 | tf_op jit(solution)/shard_map/ppermute | solution.py:600
  69.3 1.5 %shard_map.203 = (bf16[4,80,128]{2,1,0:T(8,128)(2,1)}, bf16[32,128]{1,0:T(8,128)(2,1)S(1)}, f32[8,128]{1,0:T(8,128)S(1)}) custom-call(s32[27]{0:T(128)S(1)} %stack.75.spots_ref, bf16[2304,128]{1,0:T(8,128)(2,1)S(1)} %shard_map.191.refs_0_.refs_4_.refs_2_, bf16[2304,128]{1,0:T(8,128)(2,1)S(1)} %shard_map.195.refs_1_, bf16[2304,128]{1,0:T(8,128)(2,1)S(1)} %copy-done.2, ...), custom_call_target="tpu_custom_call" | custom-call | tf_op jit(solution)/shard_map/pallas_call | solution.py:388
  70.9 4.7 %all-to-all-start.1 = ((bf16[4,80,128]{2,1,0:T(8,128)(2,1)}), bf16[4,80,128]{2,1,0:T(8,128)(2,1)S(1)}, u32[]{:S(2)}, u32[]{:S(2)}) async-start(bf16[4,80,128]{2,1,0:T(8,128)(2,1)} %get-tuple-element.46.small_ref), calls=%async_computation.1 | async-start | bytes 163840 | tf_op jit(solution)/shard_map/all_to_all | solution.py:607
  75.6 2.8 %shard_map.204.refs_4_ = bf16[128,256]{1,0:T(8,128)(2,1)} custom-call(s32[27]{0:T(128)S(1)} %stack.75.spots_ref, f32[128,256]{1,0:T(8,128)S(1)} %shard_map.201.refs_1_.acc_ref, bf16[2304,128]{1,0:T(8,128)(2,1)S(1)} %shard_map.202.refs_7_.x_ref, bf16[8,8,256,256]{3,2,1,0:T(8,128)(2,1)} %bitcast.48, f32[8,128]{1,0:T(8,128)S(1)} %get-tuple-element.45.scale_ref, ...), custom_call_target="tpu_custom_call" | custom-call | flops 268435456 | bytes 9437184 | tf_op jit(solution)/shard_map/pallas_call | solution.py:324
  78.4 1.4 %all-to-all-done.1.refs_0_ = bf16[4,80,128]{2,1,0:T(8,128)(2,1)S(1)} async-done(((bf16[4,80,128]{2,1,0:T(8,128)(2,1)}), bf16[4,80,128]{2,1,0:T(8,128)(2,1)S(1)}, u32[]{:S(2)}, u32[]{:S(2)}) %all-to-all-start.1) | async-done | bytes 81952 | tf_op jit(solution)/shard_map/all_to_all | solution.py:607
  79.9 0.6 copy-done.25
  80.5 2.3 %shard_map.205 = (f32[256,256]{1,0:T(8,128)}, f32[256,256]{1,0:T(8,128)}, f32[8,256]{1,0:T(8,128)}, f32[8,256]{1,0:T(8,128)}, f32[8,256]{1,0:T(8,128)}) custom-call(s32[16]{0:T(128)} %slot_ref.1, s32[27]{0:T(128)} %copy-done.16, bf16[4,80,128]{2,1,0:T(8,128)(2,1)} %copy-done.25, bf16[4,2,128,256]{3,2,1,0:T(8,128)(2,1)} %copy-done, f32[8,256]{1,0:T(8,128)} %refs_2_.1, ...), custom_call_target="tpu_custom_call" | custom-call | flops 134217728 | bytes 2097152 | tf_op jit(solution)/shard_map/pallas_call | solution.py:451
  82.8 0.1 collective-permute-start.22
  82.9 1.4 %collective-permute-done.22 = f32[8,256]{1,0:T(8,128)S(1)} collective-permute-done((f32[8,256]{1,0:T(8,128)}, f32[8,256]{1,0:T(8,128)S(1)}, u32[]{:S(2)}, u32[]{:S(2)}) %collective-permute-start.22) | collective-permute-done | bytes 8224 | tf_op jit(solution)/shard_map/ppermute | solution.py:49
  84.3 0.7 add.83
  85.0 0.6 collective-permute-start.24
  85.6 0.8 collective-permute-start.23
  86.4 3.0 %collective-permute-done.23 = f32[8,256]{1,0:T(8,128)S(1)} collective-permute-done((f32[8,256]{1,0:T(8,128)S(1)}, f32[8,256]{1,0:T(8,128)S(1)}, u32[]{:S(2)}, u32[]{:S(2)}) %collective-permute-start.23) | collective-permute-done | bytes 8224 | tf_op jit(solution)/shard_map/ppermute | solution.py:530
  89.4 3.6 %collective-permute-start.25 = (f32[8,256]{1,0:T(8,128)S(1)}, f32[8,256]{1,0:T(8,128)S(1)}, u32[]{:S(2)}, u32[]{:S(2)}) collective-permute-start(f32[8,256]{1,0:T(8,128)S(1)} %add_select_fusion.p_ref), channel_id=1, source_target_pairs={{0,1},{1,0},{2,3},{3,2},{4,5},{5,4},{6,7},{7,6},{8,9},{9,8},{10,11... | collective-permute-start | bytes 24584 | tf_op jit(solution)/shard_map/ppermute | solution.py:49
  93.0 0.8 collective-permute-done.25.q_ref
  93.9 0.7 copy-done.17
  94.5 2.6 %shard_map.206 = (bf16[288,128]{1,0:T(8,128)(2,1)S(1)}, bf16[288,128]{1,0:T(8,128)(2,1)S(1)}, bf16[288,128]{1,0:T(8,128)(2,1)S(1)}, bf16[288,128]{1,0:T(8,128)(2...) custom-call(s32[27]{0:T(128)S(1)} %copy-done.17, ...), custom_call_target="tpu_custom_call" | custom-call | flops 134217728 | bytes 2097152 | tf_op jit(solution)/shard_map/pallas_call | solution.py:206
  97.2 3.5 %collective-permute-start.26 = (bf16[288,128]{1,0:T(8,128)(2,1)S(1)}, bf16[288,128]{1,0:T(8,128)(2,1)S(1)}, u32[]{:S(2)}, u32[]{:S(2)}) collective-permute-start(bf16[288,128]{1,0:T(8,128)(2,1)S(1)} %get-tuple-element.50), channel_id=1, source_target_pairs={{0,32},{8,40},{16,48},{24,56},{32,0},{40,8},{48,16},{56,24},{1,33}... | collective-permute-start | bytes 221192 | tf_op jit(solution)/shard_map/ppermute | solution.py:624
  100.7 1.4 %collective-permute-start.27 = (bf16[288,128]{1,0:T(8,128)(2,1)S(1)}, bf16[288,128]{1,0:T(8,128)(2,1)S(1)}, u32[]{:S(2)}, u32[]{:S(2)}) collective-permute-start(bf16[288,128]{1,0:T(8,128)(2,1)S(1)} %get-tuple-element.51), channel_id=1, source_target_pairs={{0,24},{8,32},{16,40},{24,48},{32,56},{40,0},{48,8},{56,16},{1,25}... | collective-permute-start | bytes 221192 | tf_op jit(solution)/shard_map/ppermute | solution.py:624
  102.1 3.6 %collective-permute-start.28 = (bf16[288,128]{1,0:T(8,128)(2,1)S(1)}, bf16[288,128]{1,0:T(8,128)(2,1)S(1)}, u32[]{:S(2)}, u32[]{:S(2)}) collective-permute-start(bf16[288,128]{1,0:T(8,128)(2,1)S(1)} %get-tuple-element.52), channel_id=1, source_target_pairs={{0,40},{8,48},{16,56},{24,0},{32,8},{40,16},{48,24},{56,32},{1,41}... | collective-permute-start | bytes 221192 | tf_op jit(solution)/shard_map/ppermute | solution.py:624
  105.7 4.1 %collective-permute-start.30 = (bf16[288,128]{1,0:T(8,128)(2,1)S(1)}, bf16[288,128]{1,0:T(8,128)(2,1)S(1)}, u32[]{:S(2)}, u32[]{:S(2)}) collective-permute-start(bf16[288,128]{1,0:T(8,128)(2,1)S(1)} %get-tuple-element.54), channel_id=1, source_target_pairs={{0,48},{8,56},{16,0},{24,8},{32,16},{40,24},{48,32},{56,40},{1,49}... | collective-permute-start | bytes 221192 | tf_op jit(solution)/shard_map/ppermute | solution.py:624
  109.9 3.3 %collective-permute-done.27.refs_2_ = bf16[288,128]{1,0:T(8,128)(2,1)S(1)} collective-permute-done((bf16[288,128]{1,0:T(8,128)(2,1)S(1)}, bf16[288,128]{1,0:T(8,128)(2,1)S(1)}, u32[]{:S(2)}, u32[]{:S(2)}) %collective-permute-start.27) | collective-permute-done | bytes 73760 | tf_op jit(solution)/shard_map/ppermute | solution.py:624
  113.2 1.9 %collective-permute-done.29.refs_4_ = bf16[288,128]{1,0:T(8,128)(2,1)S(1)} collective-permute-done((bf16[288,128]{1,0:T(8,128)(2,1)S(1)}, bf16[288,128]{1,0:T(8,128)(2,1)S(1)}, u32[]{:S(2)}, u32[]{:S(2)}) %collective-permute-start.29) | collective-permute-done | bytes 73760 | tf_op jit(solution)/shard_map/ppermute | solution.py:624
  115.0 1.3 %collective-permute-done.31.refs_6_ = bf16[288,128]{1,0:T(8,128)(2,1)S(1)} collective-permute-done((bf16[288,128]{1,0:T(8,128)(2,1)S(1)}, bf16[288,128]{1,0:T(8,128)(2,1)S(1)}, u32[]{:S(2)}, u32[]{:S(2)}) %collective-permute-start.31) | collective-permute-done | bytes 73760 | tf_op jit(solution)/shard_map/ppermute | solution.py:624
  116.3 1.2 %collective-permute-done.32.refs_7_ = bf16[288,128]{1,0:T(8,128)(2,1)S(1)} collective-permute-done((bf16[288,128]{1,0:T(8,128)(2,1)S(1)}, bf16[288,128]{1,0:T(8,128)(2,1)S(1)}, u32[]{:S(2)}, u32[]{:S(2)}) %collective-permute-start.32) | collective-permute-done | bytes 73760 | tf_op jit(solution)/shard_map/ppermute | solution.py:624
  117.5 0.9 shard_map.207
  118.5 1.9 %shard_map.208 = (f32[256,256]{1,0:T(8,128)}, f32[256,256]{1,0:T(8,128)}, f32[8,32]{1,0:T(8,128)}, f32[8,32]{1,0:T(8,128)}) custom-call(s32[27]{0:T(128)S(1)} %copy-done.17, bf16[288,128]{1,0:T(8,128)(2,1)S(1)} %get-tuple-element.49.refs_0_, bf16[288,128]{1,0:T(8,128)(2,1)S(1)} %collective-permute-done.26.refs_1_, ...), custom_call_target="tpu_custom_call" | custom-call | flops 1048576 | bytes 1048576 | tf_op jit(solution)/shard_map/pallas_call | solution.py:501
  (82 shorter events, 0.3 us)
Async XLA Ops:
  3.4 9.5 %collective-permute-start.2 = (bf16[416,128]{1,0:T(8,128)(2,1)}, bf16[416,128]{1,0:T(8,128)(2,1)S(1)}, u32[]{:S(2)}, u32[]{:S(2)}) collective-permute-start(bf16[416,128]{1,0:T(8,128)(2,1)} %get-tuple-element.37.refs_0_), channel_id=1, source_target_pairs={{0,2},{2,4},{4,6},{6,0},{1,3},{3,5},{5,7},{7,1},{8,10},{10,12},{12... | collective-permute-start | bytes 319496 | tf_op jit(solution)/shard_map/ppermute | solution.py:575
  5.0 8.5 %collective-permute-start.1 = (bf16[416,128]{1,0:T(8,128)(2,1)}, bf16[416,128]{1,0:T(8,128)(2,1)S(1)}, u32[]{:S(2)}, u32[]{:S(2)}) collective-permute-start(bf16[416,128]{1,0:T(8,128)(2,1)} %get-tuple-element.37.refs_0_), channel_id=1, source_target_pairs={{0,4},{2,6},{4,0},{6,2},{1,5},{3,7},{5,1},{7,3},{8,12},{10,14},{12... | collective-permute-start | bytes 319496 | tf_op jit(solution)/shard_map/ppermute | solution.py:575
  7.9 5.7 %collective-permute-start = (bf16[416,128]{1,0:T(8,128)(2,1)}, bf16[416,128]{1,0:T(8,128)(2,1)S(1)}, u32[]{:S(2)}, u32[]{:S(2)}) collective-permute-start(bf16[416,128]{1,0:T(8,128)(2,1)} %get-tuple-element.37.refs_0_), channel_id=1, source_target_pairs={{0,6},{2,0},{4,2},{6,4},{1,7},{3,1},{5,3},{7,5},{8,14},{10,8},{12,... | collective-permute-start | bytes 319496 | tf_op jit(solution)/shard_map/ppermute | solution.py:575
  9.2 4.8 %collective-permute-start.3 = (bf16[416,128]{1,0:T(8,128)(2,1)}, bf16[416,128]{1,0:T(8,128)(2,1)S(1)}, u32[]{:S(2)}, u32[]{:S(2)}) collective-permute-start(bf16[416,128]{1,0:T(8,128)(2,1)} %get-tuple-element.37.refs_0_), channel_id=1, source_target_pairs={{0,1},{1,0},{2,3},{3,2},{4,5},{5,4},{6,7},{7,6},{8,9},{9,8},{10,11... | collective-permute-start | bytes 319496 | tf_op jit(solution)/shard_map/ppermute | solution.py:49
  9.3 66.3 %copy-start.16 = (s32[27]{0:T(128)}, s32[27]{0:T(128)S(1)}, u32[]{:S(2)}) copy-start(s32[27]{0:T(128)S(1)} %stack.75.spots_ref) | copy-start | bytes 328
  9.3 0.8 copy-start.4
  10.2 4.7 %copy-start.18 = (bf16[416,128]{1,0:T(8,128)(2,1)S(1)}, bf16[416,128]{1,0:T(8,128)(2,1)}, u32[]{:S(2)}) copy-start(bf16[416,128]{1,0:T(8,128)(2,1)} %get-tuple-element.37.refs_0_) | copy-start | bytes 319492
  12.9 1.5 %collective-permute-start.6 = (bf16[416,128]{1,0:T(8,128)(2,1)S(1)}, bf16[416,128]{1,0:T(8,128)(2,1)S(1)}, u32[]{:S(2)}, u32[]{:S(2)}) collective-permute-start(bf16[416,128]{1,0:T(8,128)(2,1)S(1)} %collective-permute-done.2.refs_3_), channel_id=1, source_target_pairs={{0,1},{1,0},{2,3},{3,2},{4,5},{5,4},{6,7},{7,6},{8,9},{9,8},{10,11... | collective-permute-start | bytes 319496 | tf_op jit(solution)/shard_map/ppermute | solution.py:49
  13.4 1.3 %collective-permute-start.5 = (bf16[416,128]{1,0:T(8,128)(2,1)S(1)}, bf16[416,128]{1,0:T(8,128)(2,1)S(1)}, u32[]{:S(2)}, u32[]{:S(2)}) collective-permute-start(bf16[416,128]{1,0:T(8,128)(2,1)S(1)} %collective-permute-done.1.refs_2_), channel_id=1, source_target_pairs={{0,1},{1,0},{2,3},{3,2},{4,5},{5,4},{6,7},{7,6},{8,9},{9,8},{10,11... | collective-permute-start | bytes 319496 | tf_op jit(solution)/shard_map/ppermute | solution.py:49
  13.6 1.4 %collective-permute-start.4 = (bf16[416,128]{1,0:T(8,128)(2,1)S(1)}, bf16[416,128]{1,0:T(8,128)(2,1)S(1)}, u32[]{:S(2)}, u32[]{:S(2)}) collective-permute-start(bf16[416,128]{1,0:T(8,128)(2,1)S(1)} %shard_map.190.refs_1_), channel_id=1, source_target_pairs={{0,1},{1,0},{2,3},{3,2},{4,5},{5,4},{6,7},{7,6},{8,9},{9,8},{10,11... | collective-permute-start | bytes 319496 | tf_op jit(solution)/shard_map/ppermute | solution.py:49
  15.6 13.8 %collective-permute-start.7 = (bf16[2304,128]{1,0:T(8,128)(2,1)S(1)}, bf16[2304,128]{1,0:T(8,128)(2,1)S(1)}, u32[]{:S(2)}, u32[]{:S(2)}) collective-permute-start(bf16[2304,128]{1,0:T(8,128)(2,1)S(1)} %shard_map.191.refs_0_.refs_4_.refs_2_), channel_id=1, source_target_pairs={{0,8},{1,57},{2,10},{3,59},{4,12},{5,61},{6,14},{7,63},{8,16},{9,1... | collective-permute-start | bytes 1769480 | tf_op jit(solution)/shard_map/ppermute | solution.py:588
  17.6 6.7 %copy-start.5 = (bf16[256,128]{1,0:T(8,128)(2,1)S(1)}, bf16[256,128]{1,0:T(8,128)(2,1)}, u32[]{:S(2)}) copy-start(bf16[256,128]{1,0:T(8,128)(2,1)} %get-tuple-element.38.turned_ref) | copy-start | bytes 196612
  17.6 6.7 %collective-permute-start.9 = (bf16[8,256,128]{2,1,0:T(8,128)(2,1)S(1)}, bf16[8,256,128]{2,1,0:T(8,128)(2,1)S(1)}, u32[]{:S(2)}, u32[]{:S(2)}) collective-permute-start(bf16[8,256,128]{2,1,0:T(8,128)(2,1)S(1)} %get-tuple-element.40), channel_id=1, source_target_pairs={{0,1},{1,0},{2,3},{3,2},{4,5},{5,4},{6,7},{7,6},{8,9},{9,8},{10,11... | collective-permute-start | bytes 1572872 | tf_op jit(solution)/shard_map/ppermute | solution.py:49
  21.6 2.7 %collective-permute-start.8 = (bf16[8,256,128]{2,1,0:T(8,128)(2,1)S(1)}, bf16[8,256,128]{2,1,0:T(8,128)(2,1)S(1)}, u32[]{:S(2)}, u32[]{:S(2)}) collective-permute-start(bf16[8,256,128]{2,1,0:T(8,128)(2,1)S(1)} %get-tuple-element.39.refs_1_), channel_id=1, source_target_pairs={{0,1},{1,0},{2,3},{3,2},{4,5},{5,4},{6,7},{7,6},{8,9},{9,8},{10,11... | collective-permute-start | bytes 1572872 | tf_op jit(solution)/shard_map/ppermute | solution.py:49
  24.3 10.7 %copy-start.24 = (bf16[8,256,128]{2,1,0:T(8,128)(2,1)}, bf16[8,256,128]{2,1,0:T(8,128)(2,1)S(1)}, u32[]{:S(2)}) copy-start(bf16[8,256,128]{2,1,0:T(8,128)(2,1)S(1)} %get-tuple-element.47) | copy-start | bytes 1572868
  27.0 17.2 %copy-start.13 = (bf16[8,256,128]{2,1,0:T(8,128)(2,1)}, bf16[8,256,128]{2,1,0:T(8,128)(2,1)S(1)}, u32[]{:S(2)}) copy-start(bf16[8,256,128]{2,1,0:T(8,128)(2,1)S(1)} %get-tuple-element.41.refs_1_) | copy-start | bytes 1572868
  29.4 14.8 %collective-permute-start.11 = (bf16[2304,128]{1,0:T(8,128)(2,1)S(1)}, bf16[2304,128]{1,0:T(8,128)(2,1)S(1)}, u32[]{:S(2)}, u32[]{:S(2)}) collective-permute-start(bf16[2304,128]{1,0:T(8,128)(2,1)S(1)} %shard_map.195.refs_1_), channel_id=1, source_target_pairs={{0,8},{1,57},{2,10},{3,59},{4,12},{5,61},{6,14},{7,63},{8,16},{9,1... | collective-permute-start | bytes 1769480 | tf_op jit(solution)/shard_map/ppermute | solution.py:590
  29.4 5.5 %collective-permute-start.12 = (bf16[8,256,128]{2,1,0:T(8,128)(2,1)S(1)}, bf16[8,256,128]{2,1,0:T(8,128)(2,1)S(1)}, u32[]{:S(2)}, u32[]{:S(2)}) collective-permute-start(bf16[8,256,128]{2,1,0:T(8,128)(2,1)S(1)} %get-tuple-element.42.refs_2_), channel_id=1, source_target_pairs={{0,1},{1,0},{2,3},{3,2},{4,5},{5,4},{6,7},{7,6},{8,9},{9,8},{10,11... | collective-permute-start | bytes 1572872 | tf_op jit(solution)/shard_map/ppermute | solution.py:49
  31.5 10.4 %collective-permute-start.13 = (bf16[8,256,128]{2,1,0:T(8,128)(2,1)S(1)}, bf16[8,256,128]{2,1,0:T(8,128)(2,1)S(1)}, u32[]{:S(2)}, u32[]{:S(2)}) collective-permute-start(bf16[8,256,128]{2,1,0:T(8,128)(2,1)S(1)} %get-tuple-element.43), channel_id=1, source_target_pairs={{0,2},{1,7},{2,4},{3,1},{4,6},{5,3},{6,0},{7,5},{8,10},{9,15},{10,... | collective-permute-start | bytes 1572872 | tf_op jit(solution)/shard_map/ppermute | solution.py:584
  32.2 17.6 %collective-permute-start.10 = (bf16[2304,128]{1,0:T(8,128)(2,1)S(1)}, bf16[2304,128]{1,0:T(8,128)(2,1)S(1)}, u32[]{:S(2)}, u32[]{:S(2)}) collective-permute-start(bf16[2304,128]{1,0:T(8,128)(2,1)S(1)} %shard_map.195.refs_1_), channel_id=1, source_target_pairs={{0,1},{1,0},{2,3},{3,2},{4,5},{5,4},{6,7},{7,6},{8,9},{9,8},{10,11... | collective-permute-start | bytes 1769480 | tf_op jit(solution)/shard_map/ppermute | solution.py:49
  34.9 10.1 %copy-start.9 = (f32[128,256]{1,0:T(8,128)}, f32[128,256]{1,0:T(8,128)S(1)}, u32[]{:S(2)}) copy-start(f32[128,256]{1,0:T(8,128)S(1)} %shard_map.192.refs_0_.refs_2_) | copy-start | bytes 393220
  44.2 0.8 copy-start.3
  45.0 12.2 %collective-permute-start.15 = (bf16[2304,128]{1,0:T(8,128)(2,1)S(1)}, bf16[2304,128]{1,0:T(8,128)(2,1)S(1)}, u32[]{:S(2)}, u32[]{:S(2)}) collective-permute-start(bf16[2304,128]{1,0:T(8,128)(2,1)S(1)} %shard_map.198.refs_1_.refs_3_), channel_id=1, source_target_pairs={{0,8},{1,57},{2,10},{3,59},{4,12},{5,61},{6,14},{7,63},{8,16},{9,1... | collective-permute-start | bytes 1769480 | tf_op jit(solution)/shard_map/ppermute | solution.py:596
  45.0 12.2 %all-to-all-start = ((bf16[4,2,128,256]{3,2,1,0:T(8,128)(2,1)}), bf16[4,2,128,256]{3,2,1,0:T(8,128)(2,1)S(1)}, u32[]{:S(2)}, u32[]{:S(2)}) async-start(bf16[4,2,128,256]{3,2,1,0:T(8,128)(2,1)} %get-tuple-element.44), calls=%async_computation | async-start | bytes 1048576 | tf_op jit(solution)/shard_map/all_to_all | solution.py:578
  49.8 11.1 %collective-permute-start.14 = (bf16[2304,128]{1,0:T(8,128)(2,1)S(1)}, bf16[2304,128]{1,0:T(8,128)(2,1)}, u32[]{:S(2)}, u32[]{:S(2)}) collective-permute-start(bf16[2304,128]{1,0:T(8,128)(2,1)S(1)} %shard_map.198.refs_1_.refs_3_), channel_id=1, source_target_pairs={{0,1},{1,0},{2,3},{3,2},{4,5},{5,4},{6,7},{7,6},{8,9},{9,8},{10,11... | collective-permute-start | bytes 1769480 | tf_op jit(solution)/shard_map/ppermute | solution.py:49
  49.8 11.1 %collective-permute-start.19 = (bf16[8,256,128]{2,1,0:T(8,128)(2,1)}, bf16[8,256,128]{2,1,0:T(8,128)(2,1)}, u32[]{:S(2)}, u32[]{:S(2)}) collective-permute-start(bf16[8,256,128]{2,1,0:T(8,128)(2,1)} %copy-done.13), channel_id=1, source_target_pairs={{0,2},{1,7},{2,4},{3,1},{4,6},{5,3},{6,0},{7,5},{8,10},{9,15},{10,... | collective-permute-start | bytes 1572872 | tf_op jit(solution)/shard_map/ppermute | solution.py:585
  49.8 0.9 copy-start.10
  50.7 2.5 %copy-start.1 = (bf16[2304,128]{1,0:T(8,128)(2,1)}, bf16[2304,128]{1,0:T(8,128)(2,1)S(1)}, u32[]{:S(2)}) copy-start(bf16[2304,128]{1,0:T(8,128)(2,1)S(1)} %collective-permute-done.10.refs_2_) | copy-start | bytes 1769476
  53.2 0.7 copy-start.6
  57.2 7.3 %copy-start = (bf16[4,2,128,256]{3,2,1,0:T(8,128)(2,1)}, bf16[4,2,128,256]{3,2,1,0:T(8,128)(2,1)S(1)}, u32[]{:S(2)}) copy-start(bf16[4,2,128,256]{3,2,1,0:T(8,128)(2,1)S(1)} %all-to-all-done.refs_2_.refs_1_) | copy-start | bytes 1572868
  57.2 1.0 copy-start.7
  58.2 6.3 %collective-permute-start.16 = (bf16[2304,128]{1,0:T(8,128)(2,1)S(1)}, bf16[2304,128]{1,0:T(8,128)(2,1)S(1)}, u32[]{:S(2)}, u32[]{:S(2)}) collective-permute-start(bf16[2304,128]{1,0:T(8,128)(2,1)S(1)} %shard_map.200.refs_1_.refs_5_), channel_id=1, source_target_pairs={{0,1},{1,0},{2,3},{3,2},{4,5},{5,4},{6,7},{7,6},{8,9},{9,8},{10,11... | collective-permute-start | bytes 1769480 | tf_op jit(solution)/shard_map/ppermute | solution.py:49
  58.2 11.1 %collective-permute-start.17 = (bf16[2304,128]{1,0:T(8,128)(2,1)S(1)}, bf16[2304,128]{1,0:T(8,128)(2,1)S(1)}, u32[]{:S(2)}, u32[]{:S(2)}) collective-permute-start(bf16[2304,128]{1,0:T(8,128)(2,1)S(1)} %shard_map.200.refs_1_.refs_5_), channel_id=1, source_target_pairs={{0,8},{1,57},{2,10},{3,59},{4,12},{5,61},{6,14},{7,63},{8,16},{9,1... | collective-permute-start | bytes 1769480 | tf_op jit(solution)/shard_map/ppermute | solution.py:600
  58.7 34.3 %collective-permute-start.18 = (bf16[8,256,128]{2,1,0:T(8,128)(2,1)}, bf16[8,256,128]{2,1,0:T(8,128)(2,1)}, u32[]{:S(2)}, u32[]{:S(2)}) collective-permute-start(bf16[8,256,128]{2,1,0:T(8,128)(2,1)} %copy-done.24), channel_id=1, source_target_pairs={{0,1},{1,0},{2,3},{3,2},{4,5},{5,4},{6,7},{7,6},{8,9},{9,8},{10,11... | collective-permute-start | bytes 1572872 | tf_op jit(solution)/shard_map/ppermute | solution.py:49
  60.9 32.1 %collective-permute-start.20 = (bf16[8,256,128]{2,1,0:T(8,128)(2,1)}, bf16[8,256,128]{2,1,0:T(8,128)(2,1)}, u32[]{:S(2)}, u32[]{:S(2)}) collective-permute-start(bf16[8,256,128]{2,1,0:T(8,128)(2,1)} %collective-permute-done.19), channel_id=1, source_target_pairs={{0,1},{1,0},{2,3},{3,2},{4,5},{5,4},{6,7},{7,6},{8,9},{9,8},{10,11... | collective-permute-start | bytes 1572872 | tf_op jit(solution)/shard_map/ppermute | solution.py:49
  60.9 32.1 %collective-permute-start.21 = (bf16[8,256,128]{2,1,0:T(8,128)(2,1)}, bf16[8,256,128]{2,1,0:T(8,128)(2,1)}, u32[]{:S(2)}, u32[]{:S(2)}) collective-permute-start(bf16[8,256,128]{2,1,0:T(8,128)(2,1)} %copy-done.3), channel_id=1, source_target_pairs={{0,2},{1,7},{2,4},{3,1},{4,6},{5,3},{6,0},{7,5},{8,10},{9,15},{10,... | collective-permute-start | bytes 1572872 | tf_op jit(solution)/shard_map/ppermute | solution.py:592
  61.0 0.9 copy-start.8
  64.5 4.8 %copy-start.2 = (bf16[2304,128]{1,0:T(8,128)(2,1)S(1)}, bf16[2304,128]{1,0:T(8,128)(2,1)}, u32[]{:S(2)}) copy-start(bf16[2304,128]{1,0:T(8,128)(2,1)} %copy-done.1) | copy-start | bytes 1769476
  64.6 4.8 %copy-start.21 = (s32[128]{0:T(128)S(1)}, s32[128]{0:T(128)}, u32[]{:S(2)}) copy-start(s32[128]{0:T(128)} %param.18) | copy-start | bytes 1540
  64.6 11.0 %copy-start.11 = (bf16[16,32,256]{2,1,0:T(8,128)(2,1)S(1)}, bf16[16,32,256]{2,1,0:T(8,128)(2,1)}, u32[]{:S(2)}) copy-start(bf16[16,32,256]{2,1,0:T(8,128)(2,1)} %param.17) | copy-start | bytes 786436
  70.9 9.0 %all-to-all-start.1 = ((bf16[4,80,128]{2,1,0:T(8,128)(2,1)}), bf16[4,80,128]{2,1,0:T(8,128)(2,1)S(1)}, u32[]{:S(2)}, u32[]{:S(2)}) async-start(bf16[4,80,128]{2,1,0:T(8,128)(2,1)} %get-tuple-element.46.small_ref), calls=%async_computation.1 | async-start | bytes 163840 | tf_op jit(solution)/shard_map/all_to_all | solution.py:607
  75.6 41.9 %copy-start.12 = (bf16[256,16,32]{0,2,1:T(8,128)(2,1)S(1)}, bf16[256,16,32]{0,2,1:T(8,128)(2,1)}, u32[]{:S(2)}) copy-start(bf16[256,16,32]{0,2,1:T(8,128)(2,1)} %param.16) | copy-start | bytes 786436
  75.6 42.8 %copy-start.22 = (f32[8,32]{1,0:T(8,128)S(1)}, f32[8,32]{1,0:T(8,128)}, u32[]{:S(2)}) copy-start(f32[8,32]{1,0:T(8,128)} %refs_12_.1) | copy-start | bytes 3076
  75.6 42.8 %copy-start.23 = (f32[8,32]{1,0:T(8,128)S(1)}, f32[8,32]{1,0:T(8,128)}, u32[]{:S(2)}) copy-start(f32[8,32]{1,0:T(8,128)} %refs_13_.1) | copy-start | bytes 3076
  79.9 0.6 copy-start.25
  82.8 35.6 %copy-start.14 = (f32[256,256]{1,0:T(8,128)S(1)}, f32[256,256]{1,0:T(8,128)}, u32[]{:S(2)}) copy-start(f32[256,256]{1,0:T(8,128)} %get-tuple-element.58.refs_8_) | copy-start | bytes 786436
  82.8 35.6 %copy-start.15 = (f32[256,256]{1,0:T(8,128)S(1)}, f32[256,256]{1,0:T(8,128)}, u32[]{:S(2)}) copy-start(f32[256,256]{1,0:T(8,128)} %get-tuple-element.59.refs_9_) | copy-start | bytes 786436
  82.8 1.5 %collective-permute-start.22 = (f32[8,256]{1,0:T(8,128)}, f32[8,256]{1,0:T(8,128)S(1)}, u32[]{:S(2)}, u32[]{:S(2)}) collective-permute-start(f32[8,256]{1,0:T(8,128)} %get-tuple-element.48), channel_id=1, source_target_pairs={{0,1},{1,0},{2,3},{3,2},{4,5},{5,4},{6,7},{7,6},{8,9},{9,8},{10,11... | collective-permute-start | bytes 24584 | tf_op jit(solution)/shard_map/ppermute | solution.py:49
  85.0 1.4 %collective-permute-start.24 = (f32[8,256]{1,0:T(8,128)S(1)}, f32[8,256]{1,0:T(8,128)S(1)}, u32[]{:S(2)}, u32[]{:S(2)}) collective-permute-start(f32[8,256]{1,0:T(8,128)S(1)} %add.83), channel_id=1, source_target_pairs={{1,7},{3,5},{5,3},{7,1},{9,15},{11,13},{13,11},{15,9},{17,23},{19,... | collective-permute-start | bytes 24584 | tf_op jit(solution)/shard_map/ppermute | solution.py:531
  85.6 3.7 %collective-permute-start.23 = (f32[8,256]{1,0:T(8,128)S(1)}, f32[8,256]{1,0:T(8,128)S(1)}, u32[]{:S(2)}, u32[]{:S(2)}) collective-permute-start(f32[8,256]{1,0:T(8,128)S(1)} %add.83), channel_id=1, source_target_pairs={{0,2},{1,5},{2,0},{3,7},{4,6},{5,1},{6,4},{7,3},{8,10},{9,13},{10,... | collective-permute-start | bytes 24584 | tf_op jit(solution)/shard_map/ppermute | solution.py:530
  89.4 4.5 %collective-permute-start.25 = (f32[8,256]{1,0:T(8,128)S(1)}, f32[8,256]{1,0:T(8,128)S(1)}, u32[]{:S(2)}, u32[]{:S(2)}) collective-permute-start(f32[8,256]{1,0:T(8,128)S(1)} %add_select_fusion.p_ref), channel_id=1, source_target_pairs={{0,1},{1,0},{2,3},{3,2},{4,5},{5,4},{6,7},{7,6},{8,9},{9,8},{10,11... | collective-permute-start | bytes 24584 | tf_op jit(solution)/shard_map/ppermute | solution.py:49
  93.8 0.7 copy-start.17
  94.5 23.9 %copy-start.19 = (f32[8,256]{1,0:T(8,128)S(1)}, f32[8,256]{1,0:T(8,128)}, u32[]{:S(2)}) copy-start(f32[8,256]{1,0:T(8,128)} %get-tuple-element.33.refs_10_) | copy-start | bytes 24580
  94.5 23.9 %copy-start.20 = (f32[8,256]{1,0:T(8,128)S(1)}, f32[8,256]{1,0:T(8,128)}, u32[]{:S(2)}) copy-start(f32[8,256]{1,0:T(8,128)} %get-tuple-element.36.refs_11_) | copy-start | bytes 24580
  97.2 12.7 %collective-permute-start.26 = (bf16[288,128]{1,0:T(8,128)(2,1)S(1)}, bf16[288,128]{1,0:T(8,128)(2,1)S(1)}, u32[]{:S(2)}, u32[]{:S(2)}) collective-permute-start(bf16[288,128]{1,0:T(8,128)(2,1)S(1)} %get-tuple-element.50), channel_id=1, source_target_pairs={{0,32},{8,40},{16,48},{24,56},{32,0},{40,8},{48,16},{56,24},{1,33}... | collective-permute-start | bytes 221192 | tf_op jit(solution)/shard_map/ppermute | solution.py:624
  100.7 12.4 %collective-permute-start.27 = (bf16[288,128]{1,0:T(8,128)(2,1)S(1)}, bf16[288,128]{1,0:T(8,128)(2,1)S(1)}, u32[]{:S(2)}, u32[]{:S(2)}) collective-permute-start(bf16[288,128]{1,0:T(8,128)(2,1)S(1)} %get-tuple-element.51), channel_id=1, source_target_pairs={{0,24},{8,32},{16,40},{24,48},{32,56},{40,0},{48,8},{56,16},{1,25}... | collective-permute-start | bytes 221192 | tf_op jit(solution)/shard_map/ppermute | solution.py:624
  102.1 11.0 %collective-permute-start.28 = (bf16[288,128]{1,0:T(8,128)(2,1)S(1)}, bf16[288,128]{1,0:T(8,128)(2,1)S(1)}, u32[]{:S(2)}, u32[]{:S(2)}) collective-permute-start(bf16[288,128]{1,0:T(8,128)(2,1)S(1)} %get-tuple-element.52), channel_id=1, source_target_pairs={{0,40},{8,48},{16,56},{24,0},{32,8},{40,16},{48,24},{56,32},{1,41}... | collective-permute-start | bytes 221192 | tf_op jit(solution)/shard_map/ppermute | solution.py:624
  105.7 9.3 %collective-permute-start.29 = (bf16[288,128]{1,0:T(8,128)(2,1)S(1)}, bf16[288,128]{1,0:T(8,128)(2,1)S(1)}, u32[]{:S(2)}, u32[]{:S(2)}) collective-permute-start(bf16[288,128]{1,0:T(8,128)(2,1)S(1)} %get-tuple-element.53), channel_id=1, source_target_pairs={{0,16},{8,24},{16,32},{24,40},{32,48},{40,56},{48,0},{56,8},{1,17}... | collective-permute-start | bytes 221192 | tf_op jit(solution)/shard_map/ppermute | solution.py:624
  105.7 9.3 %collective-permute-start.30 = (bf16[288,128]{1,0:T(8,128)(2,1)S(1)}, bf16[288,128]{1,0:T(8,128)(2,1)S(1)}, u32[]{:S(2)}, u32[]{:S(2)}) collective-permute-start(bf16[288,128]{1,0:T(8,128)(2,1)S(1)} %get-tuple-element.54), channel_id=1, source_target_pairs={{0,48},{8,56},{16,0},{24,8},{32,16},{40,24},{48,32},{56,40},{1,49}... | collective-permute-start | bytes 221192 | tf_op jit(solution)/shard_map/ppermute | solution.py:624
  109.9 6.4 %collective-permute-start.31 = (bf16[288,128]{1,0:T(8,128)(2,1)S(1)}, bf16[288,128]{1,0:T(8,128)(2,1)S(1)}, u32[]{:S(2)}, u32[]{:S(2)}) collective-permute-start(bf16[288,128]{1,0:T(8,128)(2,1)S(1)} %get-tuple-element.55), channel_id=1, source_target_pairs={{0,8},{8,16},{16,24},{24,32},{32,40},{40,48},{48,56},{56,0},{1,9},... | collective-permute-start | bytes 221192 | tf_op jit(solution)/shard_map/ppermute | solution.py:624
  113.1 4.4 %collective-permute-start.32 = (bf16[288,128]{1,0:T(8,128)(2,1)S(1)}, bf16[288,128]{1,0:T(8,128)(2,1)S(1)}, u32[]{:S(2)}, u32[]{:S(2)}) collective-permute-start(bf16[288,128]{1,0:T(8,128)(2,1)S(1)} %get-tuple-element.56), channel_id=1, source_target_pairs={{0,56},{8,0},{16,8},{24,16},{32,24},{40,32},{48,40},{56,48},{1,57}... | collective-permute-start | bytes 221192 | tf_op jit(solution)/shard_map/ppermute | solution.py:624
